TPU v7x, 32 devices: a whole 2x2x4 slice. The times are simulated.
32 devices in a mesh: group: 2 (over x), rows: 16 (over z, y, core).
Axes of the slice: x: 2, y: 2, z: 4, core: 2. Of those that a mesh axis runs over, the one named last changes fastest.
Arguments:
- queries: bfloat16 [256, 3072], P(('group', 'rows')), parts along dimension 0, may hold values from -200 to 200
- prefix_keys: bfloat16 [2048, 1024], P(('group', 'rows')), parts along dimension 0, may hold values from -6 to 6
- prefix_values: bfloat16 [2048, 1024], P(('group', 'rows')), parts along dimension 0, may hold values from -6 to 6
- tree_keys: bfloat16 [256, 1024], P(('group', 'rows')), parts along dimension 0, may hold values from -12 to 12
- tree_values: bfloat16 [256, 1024], P(('group', 'rows')), parts along dimension 0, may hold values from -6 to 6
- parents: int32 [256], P('group'), parts along dimension 0, may hold values from 0 to 95, as said below
Outputs:
- attended: bfloat16 [256, 3072], P(('group', 'rows')), parts along dimension 0
There are 2 independent parts, one for each index of `group`. A program takes and returns all parts, laid end to end along the dimension named above; each array names one. Nothing has to cross between parts.
Inputs may be any that keep to these rules, and one draw needn't show every extreme that they name: `parents`: the rows hold the candidate trees of many requests, in 4 levels of 32 rows in order; a row of the first level is a tree's root and its own parent; every other row's parent is a row of the level before its own, and the first and the last row of each later level have the last row of the level before as parent.
All inputs are finite; a program needn't handle non-finite values.
Results may differ from a plain program's by a relative error of at most 0.005.
Values may be sent and summed in bfloat16 or wider, within the bound.
No kernel may reach another device: no remote copies, remote signals or barrier semaphores. Data moves between devices by JAX's collectives and lax.ppermute only.
A program may use at most 192 MiB of HBM per device.

v0:
```python
import jax
import jax.numpy as jnp
from jax import lax
from jax.sharding import PartitionSpec as P

QUERY_HEADS = 24
KV_HEADS = 8
HEAD_DIM = 128
TREE_DEPTH = 4


def as_sent(x):

    def short(part):
        return part.astype(jnp.bfloat16) if part.dtype == jnp.float32 else part

    return jax.tree.map(short, x)


def partner(x, axis, bit):
    return lax.ppermute(x, axis, [(i, i ^ 1 << bit) for i in range(lax.axis_size(axis))])


def lineage_mask(parents, row_ids):
    walker = row_ids
    columns = jnp.arange(parents.shape[0], dtype=jnp.int32)
    allowed = walker[:, None] == columns[None, :]
    for level_step in range(TREE_DEPTH - 1):
        walker = parents[walker]
        allowed = allowed | (walker[:, None] == columns[None, :])
    return allowed


def empty_stats(count):
    groups = QUERY_HEADS // KV_HEADS
    maxima = jnp.full((count, KV_HEADS, groups), -jnp.inf, jnp.float32)
    masses = jnp.zeros((count, KV_HEADS, groups), jnp.float32)
    weighted = jnp.zeros((count, KV_HEADS, groups, HEAD_DIM), jnp.float32)
    return (maxima, masses, weighted)


def score_tile(query_rows, key_tile):
    key_heads = key_tile.reshape(-1, KV_HEADS, HEAD_DIM)
    scores = jnp.einsum("rkgd,nkd->rkgn", query_rows, key_heads, preferred_element_type=jnp.float32)
    return scores * HEAD_DIM ** (-0.5)


def absorb(running, query_rows, key_tile, value_tile, allowed):
    maxima, masses, weighted = running
    scores = score_tile(query_rows, key_tile)
    scores = jnp.where(allowed[:, None, None, :], scores, -jnp.inf)
    raised = jnp.max(scores, axis=-1)
    shrink = jnp.exp(maxima - raised)
    weights = jnp.exp(scores - raised[..., None])
    masses = masses * shrink + jnp.sum(weights, axis=-1)
    value_heads = value_tile.reshape(-1, KV_HEADS, HEAD_DIM)
    update = jnp.einsum(
        "rkgn,nkd->rkgd",
        weights.astype(jnp.bfloat16),
        value_heads,
        preferred_element_type=jnp.float32,
    )
    weighted = weighted * shrink[..., None] + update
    return (raised, masses, weighted)


def empty_head(count):
    groups = QUERY_HEADS // KV_HEADS
    maxima = jnp.full((count, groups), -jnp.inf, jnp.float32)
    masses = jnp.zeros((count, groups), jnp.float32)
    weighted = jnp.zeros((count, groups, HEAD_DIM), jnp.float32)
    return (maxima, masses, weighted)


def absorb_head(running, query_rows, key_tile, value_tile):
    maxima, masses, weighted = running
    scores = jnp.einsum(
        "rgd,nd->rgn", query_rows, key_tile, preferred_element_type=jnp.float32
    ) * HEAD_DIM ** (-0.5)
    raised = jnp.maximum(maxima, jnp.max(scores, axis=-1))
    shrink = jnp.exp(maxima - raised)
    weights = jnp.exp(scores - raised[..., None])
    masses = masses * shrink + jnp.sum(weights, axis=-1)
    update = jnp.einsum(
        "rgn,nd->rgd", weights.astype(jnp.bfloat16), value_tile, preferred_element_type=jnp.float32
    )
    weighted = weighted * shrink[..., None] + update
    return (raised, masses, weighted)


def combine_stats(left, right):
    maxima = jnp.maximum(left[0], right[0])
    left_factor = jnp.exp(left[0] - maxima)
    right_factor = jnp.exp(right[0] - maxima)
    masses = left[1] * left_factor + right[1] * right_factor
    weighted = left[2] * left_factor[..., None] + right[2] * right_factor[..., None]
    return (maxima, masses, weighted)


def head_transpose(members, position, mover):
    slot_count = members[0].shape[0]
    bit_count = slot_count.bit_length() - 1
    for level_bit in range(bit_count):
        own_bit = position // 2**level_bit % 2
        kept_list = []
        sent_list = []
        for member in members:
            shaped = member.reshape(
                (slot_count // 2 ** (level_bit + 1), 2, 2**level_bit) + member.shape[1:]
            )
            lower_half = shaped[:, 0]
            upper_half = shaped[:, 1]
            kept_list.append(jnp.where(own_bit == 0, lower_half, upper_half))
            sent_list.append(jnp.where(own_bit == 0, upper_half, lower_half))
        received = mover(tuple(sent_list), level_bit)
        fresh = []
        for kept, arrived, member in zip(kept_list, received, members):
            first_half = jnp.where(own_bit == 0, kept, arrived)
            second_half = jnp.where(own_bit == 0, arrived, kept)
            fresh.append(jnp.stack([first_half, second_half], axis=1).reshape(member.shape))
        members = tuple(fresh)
    return members


def shards(queries, prefix_keys, prefix_values, tree_keys, tree_values, parents):
    groups = QUERY_HEADS // KV_HEADS
    local_rows = queries.shape[0]
    query_rows = queries.reshape(local_rows, KV_HEADS, groups, HEAD_DIM)
    every_tree_key, every_tree_value = (
        lax.all_gather(tree_keys, "rows", axis=0, tiled=True),
        lax.all_gather(tree_values, "rows", axis=0, tiled=True),
    )
    first_row = lax.axis_index("rows") * local_rows
    row_ids = first_row + jnp.arange(local_rows, dtype=jnp.int32)
    allowed = lineage_mask(parents, row_ids)
    tree_stats = absorb(
        empty_stats(local_rows), query_rows, every_tree_key, every_tree_value, allowed
    )
    position = lax.axis_index("rows")
    head_queries = jnp.transpose(
        queries.reshape(local_rows, KV_HEADS, groups * HEAD_DIM), (1, 0, 2)
    )
    head_keys = jnp.transpose(prefix_keys.reshape(-1, KV_HEADS, HEAD_DIM), (1, 0, 2))
    head_values = jnp.transpose(prefix_values.reshape(-1, KV_HEADS, HEAD_DIM), (1, 0, 2))

    def inward(sent, level_bit):
        return jax.tree.map(
            lambda part, own: part.astype(own.dtype),
            partner(as_sent(sent), "rows", level_bit),
            sent,
        )

    head_queries, head_keys, head_values = head_transpose(
        (head_queries, head_keys, head_values), position, inward
    )
    block_rows = KV_HEADS * local_rows
    my_queries = head_queries.reshape(block_rows, groups, HEAD_DIM)
    slab_keys = head_keys.reshape(-1, HEAD_DIM)
    slab_values = head_values.reshape(-1, HEAD_DIM)
    running = absorb_head(empty_head(block_rows), my_queries, slab_keys, slab_values)
    low_bits = KV_HEADS.bit_length() - 1
    all_bits = lax.axis_size("rows").bit_length() - 1
    for level_bit in range(low_bits, all_bits):
        far_keys, far_values = partner((slab_keys, slab_values), "rows", level_bit)
        running = absorb_head(running, my_queries, far_keys, far_values)
        if level_bit + 1 < all_bits:
            slab_keys = jnp.concatenate([slab_keys, far_keys], axis=0)
            slab_values = jnp.concatenate([slab_values, far_values], axis=0)
    shaped = (
        running[0].reshape(KV_HEADS, local_rows, groups),
        running[1].reshape(KV_HEADS, local_rows, groups),
        running[2].reshape(KV_HEADS, local_rows, groups, HEAD_DIM),
    )

    def outward(sent, level_bit):
        return partner(sent, "rows", level_bit)

    returned = head_transpose(shaped, position, outward)
    owned = (
        jnp.transpose(returned[0], (1, 0, 2)),
        jnp.transpose(returned[1], (1, 0, 2)),
        jnp.transpose(returned[2], (1, 0, 2, 3)),
    )
    final = combine_stats(tree_stats, owned)
    result = final[2] / final[1][..., None]
    return result.reshape(local_rows, QUERY_HEADS * HEAD_DIM).astype(jnp.bfloat16)


def solution(mesh):
    placed = (
        P(("group", "rows"), None),
        P(("group", "rows"), None),
        P(("group", "rows"), None),
        P(("group", "rows"), None),
        P(("group", "rows"), None),
        P("group"),
    )
    return jax.shard_map(
        shards, mesh=mesh, in_specs=placed, out_specs=P(("group", "rows"), None), check_vma=False
    )
```

profile of v0, /device:TPU:0, one launch (start us, length us, event | category | flops | bytes accessed | tf_op | source)
XLA Modules:
  0.0 93.2 jit_solution(2986927178429913200)
XLA Ops:
  0.0 0.9 %copy.258 = bf16[8,8,8,128]{3,2,1,0:T(8,128)(2,1)S(1)} copy(bf16[8,8,8,128]{3,1,2,0:T(8,128)(2,1)} %bitcast.540) | data formatting | bytes 262144
  1.0 0.5 collective-permute-start.10
  2.0 0.5 collective-permute-start.3
  2.7 0.5 collective-permute-start
  3.5 23.8 %all_gather.6 = bf16[128,1024]{1,0:T(8,128)(2,1)S(1)} all-gather(bf16[8,1024]{1,0:T(8,128)(2,1)S(1)} %copy-done.3), channel_id=1, replica_groups=mesh['group'=2,'rows'=16] {'rows'}, dimensions={0}, use_global_device_ids=true | all-gather | bytes 278528 | tf_op jit(solution)/shard_map/all_gather | solution.py:130
  27.4 0.6 gather_fusion
  28.1 0.6 gather_fusion.1
  28.8 0.6 gather_fusion.2
  30.1 0.6 copy-done.4
  30.8 19.3 %all_gather.7 = bf16[128,1024]{1,0:T(8,128)(2,1)S(1)} all-gather(bf16[8,1024]{1,0:T(8,128)(2,1)S(1)} %copy-done.4), channel_id=1, replica_groups=mesh['group'=2,'rows'=16] {'rows'}, dimensions={0}, use_global_device_ids=true | all-gather | bytes 278528 | tf_op jit(solution)/shard_map/all_gather | solution.py:131
  50.4 0.6 collective-permute-start.11
  51.1 1.6 %collective-permute-start.4 = (bf16[2,2,64,128]{3,2,0,1:T(8,128)(2,1)S(1)}, bf16[2,2,64,128]{3,2,0,1:T(8,128)(2,1)S(1)}, u32[]{:S(2)}, u32[]{:S(2)}) collective-permute-start(bf16[2,2,64,128]{3,2,0,1:T(8,128)(2,1)S(1)} %fusion.21), channel_id=1, source_target_pairs={{0,2},{1,3},{2,0},{3,1},{4,6},{5,7},{6,4},{7,5},{8,10},{9,11},{10,... | collective-permute-start | bytes 196616 | tf_op jit(solution)/shard_map/ppermute | solution.py:21
  52.6 1.6 %collective-permute-done.2 = bf16[1,4,8,384]{3,2,1,0:T(8,128)(2,1)S(1)} collective-permute-done((bf16[1,4,8,384]{3,2,1,0:T(8,128)(2,1)S(1)}, bf16[1,4,8,384]{3,2,1,0:T(8,128)(2,1)S(1)}, u32[]{:S(2)}, u32[]{:S(2)}) %collective-permute-start.2) | collective-permute-done | bytes 24608 | tf_op jit(solution)/shard_map/ppermute | solution.py:21
  54.2 2.0 %collective-permute-done.4 = bf16[2,2,64,128]{3,2,0,1:T(8,128)(2,1)S(1)} collective-permute-done((bf16[2,2,64,128]{3,2,0,1:T(8,128)(2,1)S(1)}, bf16[2,2,64,128]{3,2,0,1:T(8,128)(2,1)S(1)}, u32[]{:S(2)}, u32[]{:S(2)}) %collective-permute-start.4) | collective-permute-done | bytes 65568 | tf_op jit(solution)/shard_map/ppermute | solution.py:21
  56.3 1.8 %collective-permute-start.5 = (bf16[1,4,64,128]{3,2,1,0:T(8,128)(2,1)S(1)}, bf16[1,4,64,128]{3,2,1,0:T(8,128)(2,1)S(1)}, u32[]{:S(2)}, u32[]{:S(2)}) collective-permute-start(bf16[1,4,64,128]{3,2,1,0:T(8,128)(2,1)S(1)} %select_bitcast_fusion.3), channel_id=1, source_target_pairs={{0,4},{1,5},{2,6},{3,7},{4,0},{5,1},{6,2},{7,3},{8,12},{9,13},{10,... | collective-permute-start | bytes 196616 | tf_op jit(solution)/shard_map/ppermute | solution.py:21
  58.5 2.6 %collective-permute-done.5 = bf16[1,4,64,128]{3,2,1,0:T(8,128)(2,1)S(1)} collective-permute-done((bf16[1,4,64,128]{3,2,1,0:T(8,128)(2,1)S(1)}, bf16[1,4,64,128]{3,2,1,0:T(8,128)(2,1)S(1)}, u32[]{:S(2)}, u32[]{:S(2)}) %collective-permute-start.5) | collective-permute-done | bytes 65568 | tf_op jit(solution)/shard_map/ppermute | solution.py:21
  61.3 1.2 %collective-permute-done.12 = bf16[1,4,64,128]{3,2,1,0:T(8,128)(2,1)S(1)} collective-permute-done((bf16[1,4,64,128]{3,2,1,0:T(8,128)(2,1)S(1)}, bf16[1,4,64,128]{3,2,1,0:T(8,128)(2,1)S(1)}, u32[]{:S(2)}, u32[]{:S(2)}) %collective-permute-start.12) | collective-permute-done | bytes 65568 | tf_op jit(solution)/shard_map/ppermute | solution.py:21
  62.5 1.8 %collective-permute-start.13 = (bf16[512,128]{1,0:T(8,128)(2,1)S(1)}, bf16[512,128]{1,0:T(8,128)(2,1)S(1)}, u32[]{:S(2)}, u32[]{:S(2)}) collective-permute-start(bf16[512,128]{1,0:T(8,128)(2,1)S(1)} %bitcast.522), channel_id=1, source_target_pairs={{0,8},{1,9},{2,10},{3,11},{4,12},{5,13},{6,14},{7,15},{8,0},{9,1},... | collective-permute-start | bytes 393224 | tf_op jit(solution)/shard_map/ppermute | solution.py:21
  65.0 7.0 %collective-permute-done.6 = bf16[512,128]{1,0:T(8,128)(2,1)S(1)} collective-permute-done((bf16[512,128]{1,0:T(8,128)(2,1)S(1)}, bf16[512,128]{1,0:T(8,128)(2,1)S(1)}, u32[]{:S(2)}, u32[]{:S(2)}) %collective-permute-start.6) | collective-permute-done | bytes 131104 | tf_op jit(solution)/shard_map/ppermute | solution.py:21
  72.9 0.9 collective-permute-done.13
  74.4 0.6 collective-permute-start.17
  75.0 0.7 collective-permute-done.17
  76.3 1.8 %collective-permute-start.8 = (f32[2,2,8,3]{2,1,3,0:T(2,128)S(1)}, f32[2,2,8,3]{2,1,3,0:T(2,128)S(1)}, u32[]{:S(2)}, u32[]{:S(2)}) collective-permute-start(f32[2,2,8,3]{2,1,3,0:T(2,128)S(1)} %bitcast.559), channel_id=1, source_target_pairs={{0,2},{1,3},{2,0},{3,1},{4,6},{5,7},{6,4},{7,5},{8,10},{9,11},{10,... | collective-permute-start | bytes 1160 | tf_op jit(solution)/shard_map/ppermute | solution.py:21
  78.1 1.5 %collective-permute-done.18 = f32[2,2,8,3]{2,1,3,0:T(2,128)S(1)} collective-permute-done((f32[2,2,8,3]{2,1,3,0:T(2,128)S(1)}, f32[2,2,8,3]{2,1,3,0:T(2,128)S(1)}, u32[]{:S(2)}, u32[]{:S(2)}) %collective-permute-start.18) | collective-permute-done | bytes 416 | tf_op jit(solution)/shard_map/ppermute | solution.py:21
  80.0 1.8 %collective-permute-start.9 = (f32[1,4,8,3]{2,1,3,0:T(4,128)S(1)}, f32[1,4,8,3]{2,1,3,0:T(4,128)S(1)}, u32[]{:S(2)}, u32[]{:S(2)}) collective-permute-start(f32[1,4,8,3]{2,1,3,0:T(4,128)S(1)} %select_bitcast_fusion.13), channel_id=1, source_target_pairs={{0,4},{1,5},{2,6},{3,7},{4,0},{5,1},{6,2},{7,3},{8,12},{9,13},{10,... | collective-permute-start | bytes 1160 | tf_op jit(solution)/shard_map/ppermute | solution.py:21
  81.8 1.5 %collective-permute-done.19 = f32[1,4,8,3]{2,1,3,0:T(4,128)S(1)} collective-permute-done((f32[1,4,8,3]{2,1,3,0:T(4,128)S(1)}, f32[1,4,8,3]{2,1,3,0:T(4,128)S(1)}, u32[]{:S(2)}, u32[]{:S(2)}) %collective-permute-start.19) | collective-permute-done | bytes 416 | tf_op jit(solution)/shard_map/ppermute | solution.py:21
  83.3 0.4 collective-permute-done.9
  83.8 1.8 %collective-permute-start.15 = (f32[2,2,8,3,128]{4,2,3,1,0:T(8,128)S(1)}, f32[2,2,8,3,128]{4,2,3,1,0:T(8,128)S(1)}, u32[]{:S(2)}, u32[]{:S(2)}) collective-permute-start(f32[2,2,8,3,128]{4,2,3,1,0:T(8,128)S(1)} %select_bitcast_fusion.7), channel_id=1, source_target_pairs={{0,2},{1,3},{2,0},{3,1},{4,6},{5,7},{6,4},{7,5},{8,10},{9,11},{10,... | collective-permute-start | bytes 147464 | tf_op jit(solution)/shard_map/ppermute | solution.py:21
  85.6 2.4 %collective-permute-done.15 = f32[2,2,8,3,128]{4,2,3,1,0:T(8,128)S(1)} collective-permute-done((f32[2,2,8,3,128]{4,2,3,1,0:T(8,128)S(1)}, f32[2,2,8,3,128]{4,2,3,1,0:T(8,128)S(1)}, u32[]{:S(2)}, u32[]{:S(2)}) %collective-permute-start.15) | collective-permute-done | bytes 49184 | tf_op jit(solution)/shard_map/ppermute | solution.py:21
  88.0 1.8 %collective-permute-start.16 = (f32[1,4,8,3,128]{4,2,3,1,0:T(8,128)S(1)}, f32[1,4,8,3,128]{4,2,3,1,0:T(8,128)S(1)}, u32[]{:S(2)}, u32[]{:S(2)}) collective-permute-start(f32[1,4,8,3,128]{4,2,3,1,0:T(8,128)S(1)} %select_bitcast_fusion.6), channel_id=1, source_target_pairs={{0,4},{1,5},{2,6},{3,7},{4,0},{5,1},{6,2},{7,3},{8,12},{9,13},{10,... | collective-permute-start | bytes 147464 | tf_op jit(solution)/shard_map/ppermute | solution.py:21
  89.8 2.4 %collective-permute-done.16 = f32[1,4,8,3,128]{4,2,3,1,0:T(8,128)S(1)} collective-permute-done((f32[1,4,8,3,128]{4,2,3,1,0:T(8,128)S(1)}, f32[1,4,8,3,128]{4,2,3,1,0:T(8,128)S(1)}, u32[]{:S(2)}, u32[]{:S(2)}) %collective-permute-start.16) | collective-permute-done | bytes 49184 | tf_op jit(solution)/shard_map/ppermute | solution.py:21
  92.3 0.9 fusion.7
  (112 shorter events, 6.0 us)
Async XLA Ops:
  0.0 27.4 %copy-start = (s32[128]{0:T(128)S(1)}, s32[128]{0:T(128)}, u32[]{:S(2)}) copy-start(s32[128]{0:T(128)} %param.11) | copy-start | bytes 1540
  1.0 0.9 copy-start.2
  1.0 49.4 %collective-permute-start.10 = (bf16[4,1,64,128]{3,2,0,1:T(8,128)(2,1)S(1)}, bf16[4,1,64,128]{3,2,0,1:T(8,128)(2,1)S(1)}, u32[]{:S(2)}, u32[]{:S(2)}) collective-permute-start(bf16[4,1,64,128]{3,2,0,1:T(8,128)(2,1)S(1)} %select_bitcast_fusion.2), channel_id=1, source_target_pairs={{0,1},{1,0},{2,3},{3,2},{4,5},{5,4},{6,7},{7,6},{8,9},{9,8},{10,11... | collective-permute-start | bytes 196616 | tf_op jit(solution)/shard_map/ppermute | solution.py:21
  1.9 0.8 copy-start.1
  2.0 49.1 %collective-permute-start.3 = (bf16[4,1,64,128]{3,2,0,1:T(8,128)(2,1)S(1)}, bf16[4,1,64,128]{3,2,0,1:T(8,128)(2,1)S(1)}, u32[]{:S(2)}, u32[]{:S(2)}) collective-permute-start(bf16[4,1,64,128]{3,2,0,1:T(8,128)(2,1)S(1)} %fusion.20), channel_id=1, source_target_pairs={{0,1},{1,0},{2,3},{3,2},{4,5},{5,4},{6,7},{7,6},{8,9},{9,8},{10,11... | collective-permute-start | bytes 196616 | tf_op jit(solution)/shard_map/ppermute | solution.py:21
  2.7 0.7 copy-start.3
  2.7 27.3 %collective-permute-start = (bf16[4,1,8,384]{3,2,0,1:T(8,128)(2,1)S(1)}, bf16[4,1,8,384]{3,2,0,1:T(8,128)(2,1)S(1)}, u32[]{:S(2)}, u32[]{:S(2)}) collective-permute-start(bf16[4,1,8,384]{3,2,0,1:T(8,128)(2,1)S(1)} %fusion.44), channel_id=1, source_target_pairs={{0,1},{1,0},{2,3},{3,2},{4,5},{5,4},{6,7},{7,6},{8,9},{9,8},{10,11... | collective-permute-start | bytes 73736 | tf_op jit(solution)/shard_map/ppermute | solution.py:21
  30.0 0.7 copy-start.4
  30.1 20.2 %collective-permute-start.1 = (bf16[2,2,8,384]{3,2,0,1:T(8,128)(2,1)S(1)}, bf16[2,2,8,384]{3,2,0,1:T(8,128)(2,1)S(1)}, u32[]{:S(2)}, u32[]{:S(2)}) collective-permute-start(bf16[2,2,8,384]{3,2,0,1:T(8,128)(2,1)S(1)} %fusion.45), channel_id=1, source_target_pairs={{0,2},{1,3},{2,0},{3,1},{4,6},{5,7},{6,4},{7,5},{8,10},{9,11},{10,... | collective-permute-start | bytes 73736 | tf_op jit(solution)/shard_map/ppermute | solution.py:21
  50.3 3.9 %collective-permute-start.2 = (bf16[1,4,8,384]{3,2,1,0:T(8,128)(2,1)S(1)}, bf16[1,4,8,384]{3,2,1,0:T(8,128)(2,1)S(1)}, u32[]{:S(2)}, u32[]{:S(2)}) collective-permute-start(bf16[1,4,8,384]{3,2,1,0:T(8,128)(2,1)S(1)} %select_bitcast_fusion.9), channel_id=1, source_target_pairs={{0,4},{1,5},{2,6},{3,7},{4,0},{5,1},{6,2},{7,3},{8,12},{9,13},{10,... | collective-permute-start | bytes 73736 | tf_op jit(solution)/shard_map/ppermute | solution.py:21
  50.4 7.7 %collective-permute-start.11 = (bf16[2,2,64,128]{3,2,0,1:T(8,128)(2,1)S(1)}, bf16[2,2,64,128]{3,2,0,1:T(8,128)(2,1)S(1)}, u32[]{:S(2)}, u32[]{:S(2)}) collective-permute-start(bf16[2,2,64,128]{3,2,0,1:T(8,128)(2,1)S(1)} %select_bitcast_fusion.1), channel_id=1, source_target_pairs={{0,2},{1,3},{2,0},{3,1},{4,6},{5,7},{6,4},{7,5},{8,10},{9,11},{10,... | collective-permute-start | bytes 196616 | tf_op jit(solution)/shard_map/ppermute | solution.py:21
  51.1 5.2 %collective-permute-start.4 = (bf16[2,2,64,128]{3,2,0,1:T(8,128)(2,1)S(1)}, bf16[2,2,64,128]{3,2,0,1:T(8,128)(2,1)S(1)}, u32[]{:S(2)}, u32[]{:S(2)}) collective-permute-start(bf16[2,2,64,128]{3,2,0,1:T(8,128)(2,1)S(1)} %fusion.21), channel_id=1, source_target_pairs={{0,2},{1,3},{2,0},{3,1},{4,6},{5,7},{6,4},{7,5},{8,10},{9,11},{10,... | collective-permute-start | bytes 196616 | tf_op jit(solution)/shard_map/ppermute | solution.py:21
  56.3 4.9 %collective-permute-start.5 = (bf16[1,4,64,128]{3,2,1,0:T(8,128)(2,1)S(1)}, bf16[1,4,64,128]{3,2,1,0:T(8,128)(2,1)S(1)}, u32[]{:S(2)}, u32[]{:S(2)}) collective-permute-start(bf16[1,4,64,128]{3,2,1,0:T(8,128)(2,1)S(1)} %select_bitcast_fusion.3), channel_id=1, source_target_pairs={{0,4},{1,5},{2,6},{3,7},{4,0},{5,1},{6,2},{7,3},{8,12},{9,13},{10,... | collective-permute-start | bytes 196616 | tf_op jit(solution)/shard_map/ppermute | solution.py:21
  58.2 4.3 %collective-permute-start.12 = (bf16[1,4,64,128]{3,2,1,0:T(8,128)(2,1)S(1)}, bf16[1,4,64,128]{3,2,1,0:T(8,128)(2,1)S(1)}, u32[]{:S(2)}, u32[]{:S(2)}) collective-permute-start(bf16[1,4,64,128]{3,2,1,0:T(8,128)(2,1)S(1)} %select_bitcast_fusion), channel_id=1, source_target_pairs={{0,4},{1,5},{2,6},{3,7},{4,0},{5,1},{6,2},{7,3},{8,12},{9,13},{10,... | collective-permute-start | bytes 196616 | tf_op jit(solution)/shard_map/ppermute | solution.py:21
  61.2 10.8 %collective-permute-start.6 = (bf16[512,128]{1,0:T(8,128)(2,1)S(1)}, bf16[512,128]{1,0:T(8,128)(2,1)S(1)}, u32[]{:S(2)}, u32[]{:S(2)}) collective-permute-start(bf16[512,128]{1,0:T(8,128)(2,1)S(1)} %bitcast.526), channel_id=1, source_target_pairs={{0,8},{1,9},{2,10},{3,11},{4,12},{5,13},{6,14},{7,15},{8,0},{9,1},... | collective-permute-start | bytes 393224 | tf_op jit(solution)/shard_map/ppermute | solution.py:21
  62.5 11.3 %collective-permute-start.13 = (bf16[512,128]{1,0:T(8,128)(2,1)S(1)}, bf16[512,128]{1,0:T(8,128)(2,1)S(1)}, u32[]{:S(2)}, u32[]{:S(2)}) collective-permute-start(bf16[512,128]{1,0:T(8,128)(2,1)S(1)} %bitcast.522), channel_id=1, source_target_pairs={{0,8},{1,9},{2,10},{3,11},{4,12},{5,13},{6,14},{7,15},{8,0},{9,1},... | collective-permute-start | bytes 393224 | tf_op jit(solution)/shard_map/ppermute | solution.py:21
  74.2 9.6 %collective-permute-start.14 = (f32[4,1,8,3,128]{4,2,0,3,1:T(8,128)S(1)}, f32[4,1,8,3,128]{4,2,0,3,1:T(8,128)S(1)}, u32[]{:S(2)}, u32[]{:S(2)}) collective-permute-start(f32[4,1,8,3,128]{4,2,0,3,1:T(8,128)S(1)} %select_bitcast_fusion.8), channel_id=1, source_target_pairs={{0,1},{1,0},{2,3},{3,2},{4,5},{5,4},{6,7},{7,6},{8,9},{9,8},{10,11... | collective-permute-start | bytes 147464 | tf_op jit(solution)/shard_map/ppermute | solution.py:21
  74.4 1.4 %collective-permute-start.17 = (f32[4,1,8,3]{2,0,3,1:T(4,128)S(1)}, f32[4,1,8,3]{2,0,3,1:T(4,128)S(1)}, u32[]{:S(2)}, u32[]{:S(2)}) collective-permute-start(f32[4,1,8,3]{2,0,3,1:T(4,128)S(1)} %bitcast.561), channel_id=1, source_target_pairs={{0,1},{1,0},{2,3},{3,2},{4,5},{5,4},{6,7},{7,6},{8,9},{9,8},{10,11... | collective-permute-start | bytes 1160 | tf_op jit(solution)/shard_map/ppermute | solution.py:21
  75.0 1.3 %collective-permute-start.7 = (f32[4,1,8,3]{2,0,3,1:T(4,128)S(1)}, f32[4,1,8,3]{2,0,3,1:T(4,128)S(1)}, u32[]{:S(2)}, u32[]{:S(2)}) collective-permute-start(f32[4,1,8,3]{2,0,3,1:T(4,128)S(1)} %bitcast.560), channel_id=1, source_target_pairs={{0,1},{1,0},{2,3},{3,2},{4,5},{5,4},{6,7},{7,6},{8,9},{9,8},{10,11... | collective-permute-start | bytes 1160 | tf_op jit(solution)/shard_map/ppermute | solution.py:21
  75.8 3.7 %collective-permute-start.18 = (f32[2,2,8,3]{2,1,3,0:T(2,128)S(1)}, f32[2,2,8,3]{2,1,3,0:T(2,128)S(1)}, u32[]{:S(2)}, u32[]{:S(2)}) collective-permute-start(f32[2,2,8,3]{2,1,3,0:T(2,128)S(1)} %bitcast.558), channel_id=1, source_target_pairs={{0,2},{1,3},{2,0},{3,1},{4,6},{5,7},{6,4},{7,5},{8,10},{9,11},{10,... | collective-permute-start | bytes 1160 | tf_op jit(solution)/shard_map/ppermute | solution.py:21
  76.3 3.7 %collective-permute-start.8 = (f32[2,2,8,3]{2,1,3,0:T(2,128)S(1)}, f32[2,2,8,3]{2,1,3,0:T(2,128)S(1)}, u32[]{:S(2)}, u32[]{:S(2)}) collective-permute-start(f32[2,2,8,3]{2,1,3,0:T(2,128)S(1)} %bitcast.559), channel_id=1, source_target_pairs={{0,2},{1,3},{2,0},{3,1},{4,6},{5,7},{6,4},{7,5},{8,10},{9,11},{10,... | collective-permute-start | bytes 1160 | tf_op jit(solution)/shard_map/ppermute | solution.py:21
  79.6 3.7 %collective-permute-start.19 = (f32[1,4,8,3]{2,1,3,0:T(4,128)S(1)}, f32[1,4,8,3]{2,1,3,0:T(4,128)S(1)}, u32[]{:S(2)}, u32[]{:S(2)}) collective-permute-start(f32[1,4,8,3]{2,1,3,0:T(4,128)S(1)} %select_bitcast_fusion.12), channel_id=1, source_target_pairs={{0,4},{1,5},{2,6},{3,7},{4,0},{5,1},{6,2},{7,3},{8,12},{9,13},{10,... | collective-permute-start | bytes 1160 | tf_op jit(solution)/shard_map/ppermute | solution.py:21
  80.0 3.7 %collective-permute-start.9 = (f32[1,4,8,3]{2,1,3,0:T(4,128)S(1)}, f32[1,4,8,3]{2,1,3,0:T(4,128)S(1)}, u32[]{:S(2)}, u32[]{:S(2)}) collective-permute-start(f32[1,4,8,3]{2,1,3,0:T(4,128)S(1)} %select_bitcast_fusion.13), channel_id=1, source_target_pairs={{0,4},{1,5},{2,6},{3,7},{4,0},{5,1},{6,2},{7,3},{8,12},{9,13},{10,... | collective-permute-start | bytes 1160 | tf_op jit(solution)/shard_map/ppermute | solution.py:21
  83.8 4.2 %collective-permute-start.15 = (f32[2,2,8,3,128]{4,2,3,1,0:T(8,128)S(1)}, f32[2,2,8,3,128]{4,2,3,1,0:T(8,128)S(1)}, u32[]{:S(2)}, u32[]{:S(2)}) collective-permute-start(f32[2,2,8,3,128]{4,2,3,1,0:T(8,128)S(1)} %select_bitcast_fusion.7), channel_id=1, source_target_pairs={{0,2},{1,3},{2,0},{3,1},{4,6},{5,7},{6,4},{7,5},{8,10},{9,11},{10,... | collective-permute-start | bytes 147464 | tf_op jit(solution)/shard_map/ppermute | solution.py:21
  88.0 4.2 %collective-permute-start.16 = (f32[1,4,8,3,128]{4,2,3,1,0:T(8,128)S(1)}, f32[1,4,8,3,128]{4,2,3,1,0:T(8,128)S(1)}, u32[]{:S(2)}, u32[]{:S(2)}) collective-permute-start(f32[1,4,8,3,128]{4,2,3,1,0:T(8,128)S(1)} %select_bitcast_fusion.6), channel_id=1, source_target_pairs={{0,4},{1,5},{2,6},{3,7},{4,0},{5,1},{6,2},{7,3},{8,12},{9,13},{10,... | collective-permute-start | bytes 147464 | tf_op jit(solution)/shard_map/ppermute | solution.py:21
where the time goes:
time: 93.5 us; the launch traced here: 93.2 us
  blocking collectives  43.1 us (46%)
  waiting for transfers between devices  24.6 us (26%)
  starting transfers between devices  16.1 us (17%)
  local copies, waits for them, and re-layouts  5.11 us (5%)
  matrix products  2.31 us (2%)
  other arithmetic  1.46 us (2%)
    ppermute x20, waiting for transfers between devices, partner(): lax.ppermute(x, axis, [(i, i ^ 1 << bit) for i in range(lax.axis_size(axi...  24.6 us
    all_gather x1, blocking collectives, shards(): lax.all_gather(tree_keys, 'rows', axis=0, tiled=True)  23.8 us
    all_gather x1, blocking collectives, shards(): lax.all_gather(tree_values, 'rows', axis=0, tiled=True)  19.3 us
    ppermute x20, starting transfers between devices, partner(): lax.ppermute(x, axis, [(i, i ^ 1 << bit) for i in range(lax.axis_size(axi...  16.1 us
    unnamed x12, local copies, waits for them, and re-layouts  2.37 us
    gather x3, local copies, waits for them, and re-layouts, lineage_mask(): walker = parents[walker]  1.93 us
  transfers between devices with their start and end apart: 20, of which 13 were waited for; matrix products, arithmetic and copies ran while one was open for 6% of the time, Pallas kernels for 0%

commit v1 on v0

v1 whole, which is shorter than its diff:
```python
import functools

import jax
import jax.numpy as jnp
from jax import lax
from jax.experimental import pallas as pl
from jax.experimental.pallas import tpu as pltpu
from jax.sharding import PartitionSpec as P

QUERY_HEADS = 24
KV_HEADS = 8
HEAD_DIM = 128
TREE_DEPTH = 4
GROUPS = QUERY_HEADS // KV_HEADS
WIDTH = QUERY_HEADS * HEAD_DIM
LANES = 128
STRIDE = 32


def stacked(refs, columns):
    blocks = [ref[:, columns] for ref in refs]
    if blocks[0].shape[0] % 16 == 0:
        return jnp.concatenate(blocks, axis=0)
    wide = jnp.concatenate([block.astype(jnp.float32) for block in blocks], axis=0)
    return wide.astype(jnp.bfloat16)


def attend_kernel(owners, pieces, *refs):
    queries = refs[:owners]
    at = owners
    slab_keys, slab_values, tree_keys, tree_values = (
        refs[at + i * pieces : at + (i + 1) * pieces] for i in range(4)
    )
    at += 4 * pieces
    bias_ref = refs[at]
    outs = refs[at + 1 :]
    local_rows = queries[0].shape[0]
    rows = owners * local_rows
    bias = jnp.concatenate([bias_ref[...]] * GROUPS, axis=0)
    lane = lax.broadcasted_iota(jnp.int32, (rows, LANES), 1)
    stats = jnp.zeros((rows, LANES), jnp.float32)
    nt = (((1,), (1,)), ((), ()))
    for head in range(KV_HEADS):
        columns = slice(head * HEAD_DIM, (head + 1) * HEAD_DIM)
        query = jnp.concatenate(
            [
                ref[:, (head * GROUPS + g) * HEAD_DIM : (head * GROUPS + g + 1) * HEAD_DIM].astype(jnp.float32)
                for g in range(GROUPS)
                for ref in queries
            ],
            axis=0,
        ).astype(jnp.bfloat16)
        slab = lax.dot_general(query, stacked(slab_keys, columns), nt, preferred_element_type=jnp.float32)
        tree = lax.dot_general(query, stacked(tree_keys, columns), nt, preferred_element_type=jnp.float32)
        slab = slab * HEAD_DIM ** (-0.5)
        tree = tree * HEAD_DIM ** (-0.5) + bias
        maxima = jnp.maximum(
            jnp.max(slab, axis=1, keepdims=True), jnp.max(tree, axis=1, keepdims=True)
        )
        slab = jnp.exp(slab - maxima)
        tree = jnp.exp(tree - maxima)
        masses = jnp.sum(slab, axis=1, keepdims=True) + jnp.sum(tree, axis=1, keepdims=True)
        weighted = jnp.dot(
            slab.astype(jnp.bfloat16), stacked(slab_values, columns), preferred_element_type=jnp.float32
        ) + jnp.dot(
            tree.astype(jnp.bfloat16), stacked(tree_values, columns), preferred_element_type=jnp.float32
        )
        weighted = weighted / masses
        level = maxima + jnp.log(masses)
        for g in range(GROUPS):
            query_head = head * GROUPS + g
            wide = slice(query_head * HEAD_DIM, (query_head + 1) * HEAD_DIM)
            here = (lane % STRIDE == query_head) & (lane < 3 * STRIDE)
            stats = jnp.where(here, level[g * rows : (g + 1) * rows], stats)
            for owner in range(owners):
                first = g * rows + owner * local_rows
                outs[owner][:, wide] = weighted[first : first + local_rows].astype(jnp.bfloat16)
    high = stats.astype(jnp.bfloat16).astype(jnp.float32)
    rest = stats - high
    middle = rest.astype(jnp.bfloat16).astype(jnp.float32)
    low = rest - middle
    sent = jnp.where(lane < STRIDE, high, jnp.where(lane < 2 * STRIDE, middle, low))
    for owner in range(owners):
        outs[owner][:, WIDTH:] = sent[owner * local_rows : (owner + 1) * local_rows].astype(jnp.bfloat16)


def merge_kernel(*refs):
    parts, out = refs[:-1], refs[-1]
    levels = []
    for part in parts:
        terms = part[:, WIDTH:].astype(jnp.float32)
        levels.append(
            terms[:, :STRIDE] + terms[:, STRIDE : 2 * STRIDE] + terms[:, 2 * STRIDE : 3 * STRIDE]
        )
    top = functools.reduce(jnp.maximum, levels)
    shares = [jnp.exp(level - top) for level in levels]
    whole = 1.0 / functools.reduce(jnp.add, shares)
    shares = [share * whole for share in shares]
    for head in range(QUERY_HEADS):
        wide = slice(head * HEAD_DIM, (head + 1) * HEAD_DIM)
        total = functools.reduce(
            jnp.add,
            [
                share[:, head : head + 1] * part[:, wide].astype(jnp.float32)
                for share, part in zip(shares, parts)
            ],
        )
        out[:, wide] = total.astype(out.dtype)


def swap(x, offset):
    return lax.ppermute(x, "rows", [(i, i ^ offset) for i in range(lax.axis_size("rows"))])


def tree_bias(parents, row_ids, token_ids):
    columns = jnp.arange(parents.shape[0], dtype=jnp.int32)
    walker = row_ids
    allowed = walker[:, None] == token_ids[None, :]
    for _ in range(TREE_DEPTH - 1):
        walker = jnp.sum(jnp.where(walker[:, None] == columns[None, :], parents[None, :], 0), axis=1)
        allowed = allowed | (walker[:, None] == token_ids[None, :])
    return jnp.where(allowed, 0.0, -jnp.inf).astype(jnp.float32)


def shards(queries, prefix_keys, prefix_values, tree_keys, tree_values, parents):
    size = lax.axis_size("rows")
    bits = size.bit_length() - 1
    near_bits = (bits + 1) // 2
    near = 2**near_bits
    far = size // near
    local_rows = queries.shape[0]
    position = lax.axis_index("rows")

    pieces = {0: (prefix_keys, prefix_values, tree_keys, tree_values)}
    for bit in reversed(range(near_bits)):
        for offset in list(pieces):
            pieces[offset ^ (1 << bit)] = tuple(swap(x, 1 << bit) for x in pieces[offset])
    far_offsets = [near * i for i in range(far)]
    all_queries = [queries] + [swap(queries, offset) for offset in far_offsets[1:]]

    slots = jnp.arange(local_rows, dtype=jnp.int32)[None, :]
    row_ids = ((position ^ jnp.array(far_offsets, jnp.int32))[:, None] * local_rows + slots).reshape(-1)
    offsets = sorted(pieces)
    token_ids = ((position ^ jnp.array(offsets, jnp.int32))[:, None] * local_rows + slots).reshape(-1)
    bias = tree_bias(parents, row_ids, token_ids)

    operands = all_queries + [pieces[offset][i] for i in range(4) for offset in offsets] + [bias]
    vmem = pl.BlockSpec(memory_space=pltpu.VMEM)
    partials = pl.pallas_call(
        functools.partial(attend_kernel, far, near),
        out_shape=[jax.ShapeDtypeStruct((local_rows, WIDTH + LANES), jnp.bfloat16)] * far,
        in_specs=[vmem] * len(operands),
        out_specs=[vmem] * far,
        compiler_params=pltpu.CompilerParams(vmem_limit_bytes=32 * 2**20),
    )(*operands)
    parts = [partials[0]] + [swap(partials[i], far_offsets[i]) for i in range(1, far)]
    return pl.pallas_call(
        merge_kernel,
        out_shape=jax.ShapeDtypeStruct((local_rows, WIDTH), jnp.bfloat16),
        in_specs=[vmem] * far,
        out_specs=vmem,
    )(*parts)


def solution(mesh):
    placed = (
        P(("group", "rows"), None),
        P(("group", "rows"), None),
        P(("group", "rows"), None),
        P(("group", "rows"), None),
        P(("group", "rows"), None),
        P("group"),
    )
    return jax.shard_map(
        shards, mesh=mesh, in_specs=placed, out_specs=P(("group", "rows"), None), check_vma=False
    )
```

time: 93.5 us -> 33.6 us (0.36)
  blocking collectives: 43.1 us -> 0 us
  waiting for transfers between devices: 24.6 us -> 8.7 us
  Pallas kernels: 0 us -> 3.96 us
  matrix products: 2.31 us -> 0 us
    all_gather x2 -> x0, blocking collectives: 43.1 us -> none  [the longest x1 23.8 us: shards(): lax.all_gather(tree_keys, 'rows', axis=0, tiled=True)]
    ppermute x20 -> x18, waiting for transfers between devices: 24.6 us -> 8.7 us  [swap(): lax.ppermute(x, 'rows', [(i, i ^ offset) for i in range(lax.axis_size('ro...]
    pallas_call x0 -> x2, Pallas kernels: none -> 3.96 us  [the longest x1 2.16 us: shards(): pl.pallas_call(functools.partial(attend_kernel, far, near), out_shape=[ja...]
    dot_general x6 -> x0, matrix products: 2.31 us -> none  [the longest x1 0.92 us: absorb(): jnp.einsum('rkgn,nkd->rkgd', weights.astype(jnp.bfloat16), value_heads, p...]
    gather x3 -> x0, local copies, waits for them, and re-layouts: 1.93 us -> none  [lineage_mask(): walker = parents[walker]]
    unnamed x12 -> x20, local copies, waits for them, and re-layouts: 2.37 us -> 4.25 us
    ppermute x20 -> x18, starting transfers between devices: 16.1 us -> 15.4 us  [swap(): lax.ppermute(x, 'rows', [(i, i ^ offset) for i in range(lax.axis_size('ro...]
  transfers between devices with their start and end apart: 20 -> 18, of which waited for: 13 -> 5; matrix products, arithmetic and copies ran while one was open for 6% -> 3% of each run, Pallas kernels for 0% -> 0%
where the time goes in v1:
time: 33.6 us; the launch traced here: 33.3 us
  starting transfers between devices  15.4 us (46%)
  waiting for transfers between devices  8.7 us (26%)
  local copies, waits for them, and re-layouts  4.42 us (13%)
  Pallas kernels  3.96 us (12%)
  other arithmetic  0.75 us (2%)
    ppermute x18, starting transfers between devices, swap(): lax.ppermute(x, 'rows', [(i, i ^ offset) for i in range(lax.axis_size('ro...  15.4 us
    ppermute x18, waiting for transfers between devices, swap(): lax.ppermute(x, 'rows', [(i, i ^ offset) for i in range(lax.axis_size('ro...  8.7 us
    unnamed x20, local copies, waits for them, and re-layouts  4.25 us
    pallas_call x1, Pallas kernels, shards(): pl.pallas_call(functools.partial(attend_kernel, far, near), out_shape=[ja...  2.16 us
    pallas_call x1, Pallas kernels, shards(): pl.pallas_call(merge_kernel, out_shape=jax.ShapeDtypeStruct((local_rows,...  1.8 us
  transfers between devices with their start and end apart: 18, of which 5 were waited for; matrix products, arithmetic and copies ran while one was open for 3% of the time, Pallas kernels for 0%

profile of v1, /device:TPU:0, one launch (start us, length us, event | category | flops | bytes accessed | tf_op | source)
XLA Modules:
  0.0 33.3 jit_solution(9588011496886775796)
XLA Ops:
  0.0 0.5 %collective-permute-start.9 = (bf16[8,1024]{1,0:T(8,128)(2,1)}, bf16[8,1024]{1,0:T(8,128)(2,1)S(1)}, u32[]{:S(2)}, u32[]{:S(2)}) collective-permute-start(bf16[8,1024]{1,0:T(8,128)(2,1)} %refs_12_.1), channel_id=1, source_target_pairs={{0,1},{1,0},{2,3},{3,2},{4,5},{5,4},{6,7},{7,6},{8,9},{9,8},{10,11... | collective-permute-start | bytes 49160 | tf_op jit(solution)/shard_map/ppermute | solution.py:112
  0.5 2.5 %collective-permute-start.10 = (bf16[8,1024]{1,0:T(8,128)(2,1)}, bf16[8,1024]{1,0:T(8,128)(2,1)S(1)}, u32[]{:S(2)}, u32[]{:S(2)}) collective-permute-start(bf16[8,1024]{1,0:T(8,128)(2,1)} %refs_12_.1), channel_id=1, source_target_pairs={{0,2},{1,3},{2,0},{3,1},{4,6},{5,7},{6,4},{7,5},{8,10},{9,11},{10,... | collective-permute-start | bytes 49160 | tf_op jit(solution)/shard_map/ppermute | solution.py:112
  3.0 0.2 collective-permute-start.12
  3.2 0.3 collective-permute-start.13
  3.5 1.7 %collective-permute-start.4 = (bf16[64,1024]{1,0:T(8,128)(2,1)}, bf16[64,1024]{1,0:T(8,128)(2,1)S(1)}, u32[]{:S(2)}, u32[]{:S(2)}) collective-permute-start(bf16[64,1024]{1,0:T(8,128)(2,1)} %refs_4_.1), channel_id=1, source_target_pairs={{0,2},{1,3},{2,0},{3,1},{4,6},{5,7},{6,4},{7,5},{8,10},{9,11},{10,... | collective-permute-start | bytes 393224 | tf_op jit(solution)/shard_map/ppermute | solution.py:112
  5.2 0.1 iota_add_fusion
  5.4 0.1 add.43
  5.5 0.4 %copy-done.9 = s32[128]{0:T(128)S(1)} copy-done((s32[128]{0:T(128)S(1)}, s32[128]{0:T(128)}, u32[]{:S(2)}) %copy-start.9) | copy-done | bytes 536
  5.9 0.2 select_reduce_fusion.2
  6.1 0.3 %collective-permute-start.7 = (bf16[64,1024]{1,0:T(8,128)(2,1)}, bf16[64,1024]{1,0:T(8,128)(2,1)S(1)}, u32[]{:S(2)}, u32[]{:S(2)}) collective-permute-start(bf16[64,1024]{1,0:T(8,128)(2,1)} %refs_8_.1), channel_id=1, source_target_pairs={{0,2},{1,3},{2,0},{3,1},{4,6},{5,7},{6,4},{7,5},{8,10},{9,11},{10,... | collective-permute-start | bytes 393224 | tf_op jit(solution)/shard_map/ppermute | solution.py:112
  6.4 0.2 select_reduce_fusion.1
  6.6 2.9 %collective-permute-start.1 = (bf16[8,3072]{1,0:T(8,128)(2,1)}, bf16[8,3072]{1,0:T(8,128)(2,1)S(1)}, u32[]{:S(2)}, u32[]{:S(2)}) collective-permute-start(bf16[8,3072]{1,0:T(8,128)(2,1)} %refs_0_.1), channel_id=1, source_target_pairs={{0,8},{1,9},{2,10},{3,11},{4,12},{5,13},{6,14},{7,15},{8,0},{9,1},... | collective-permute-start | bytes 147464 | tf_op jit(solution)/shard_map/ppermute | solution.py:112
  9.5 1.6 %collective-permute-start = (bf16[8,3072]{1,0:T(8,128)(2,1)}, bf16[8,3072]{1,0:T(8,128)(2,1)S(1)}, u32[]{:S(2)}, u32[]{:S(2)}) collective-permute-start(bf16[8,3072]{1,0:T(8,128)(2,1)} %refs_0_.1), channel_id=1, source_target_pairs={{0,4},{1,5},{2,6},{3,7},{4,0},{5,1},{6,2},{7,3},{8,12},{9,13},{10,... | collective-permute-start | bytes 147464 | tf_op jit(solution)/shard_map/ppermute | solution.py:112
  11.1 0.2 select_reduce_fusion
  11.3 0.1 add.47
  11.3 0.9 %collective-permute-done.14.refs_19_ = bf16[8,1024]{1,0:T(8,128)(2,1)S(1)} collective-permute-done((bf16[8,1024]{1,0:T(8,128)(2,1)S(1)}, bf16[8,1024]{1,0:T(8,128)(2,1)S(1)}, u32[]{:S(2)}, u32[]{:S(2)}) %collective-permute-start.14) | collective-permute-done | bytes 16416 | tf_op jit(solution)/shard_map/ppermute | solution.py:112
  12.3 0.4 %collective-permute-start.2 = (bf16[8,3072]{1,0:T(8,128)(2,1)}, bf16[8,3072]{1,0:T(8,128)(2,1)S(1)}, u32[]{:S(2)}, u32[]{:S(2)}) collective-permute-start(bf16[8,3072]{1,0:T(8,128)(2,1)} %refs_0_.1), channel_id=1, source_target_pairs={{0,12},{1,13},{2,14},{3,15},{4,8},{5,9},{6,10},{7,11},{8,4},{9,5},... | collective-permute-start | bytes 147464 | tf_op jit(solution)/shard_map/ppermute | solution.py:112
  12.6 1.2 %collective-permute-done.refs_1_ = bf16[8,3072]{1,0:T(8,128)(2,1)S(1)} collective-permute-done((bf16[8,3072]{1,0:T(8,128)(2,1)}, bf16[8,3072]{1,0:T(8,128)(2,1)S(1)}, u32[]{:S(2)}, u32[]{:S(2)}) %collective-permute-start) | collective-permute-done | bytes 49184 | tf_op jit(solution)/shard_map/ppermute | solution.py:112
  13.8 0.5 %collective-permute-start.5 = (bf16[64,1024]{1,0:T(8,128)(2,1)S(1)}, bf16[64,1024]{1,0:T(8,128)(2,1)S(1)}, u32[]{:S(2)}, u32[]{:S(2)}) collective-permute-start(bf16[64,1024]{1,0:T(8,128)(2,1)S(1)} %collective-permute-done.4.refs_6_), channel_id=1, source_target_pairs={{0,1},{1,0},{2,3},{3,2},{4,5},{5,4},{6,7},{7,6},{8,9},{9,8},{10,11... | collective-permute-start | bytes 393224 | tf_op jit(solution)/shard_map/ppermute | solution.py:112
  14.4 0.1 or_select_fusion.refs_20_
  14.5 3.9 %collective-permute-done.2.refs_3_ = bf16[8,3072]{1,0:T(8,128)(2,1)S(1)} collective-permute-done((bf16[8,3072]{1,0:T(8,128)(2,1)}, bf16[8,3072]{1,0:T(8,128)(2,1)S(1)}, u32[]{:S(2)}, u32[]{:S(2)}) %collective-permute-start.2) | collective-permute-done | bytes 49184 | tf_op jit(solution)/shard_map/ppermute | solution.py:112
  18.4 0.9 %copy-done = bf16[64,1024]{1,0:T(8,128)(2,1)S(1)} copy-done((bf16[64,1024]{1,0:T(8,128)(2,1)S(1)}, bf16[64,1024]{1,0:T(8,128)(2,1)}, u32[]{:S(2)}) %copy-start) | copy-done | bytes 131096
  19.3 0.9 %copy-done.1 = bf16[64,1024]{1,0:T(8,128)(2,1)S(1)} copy-done((bf16[64,1024]{1,0:T(8,128)(2,1)S(1)}, bf16[64,1024]{1,0:T(8,128)(2,1)}, u32[]{:S(2)}) %copy-start.1) | copy-done | bytes 131096
  20.2 0.8 %copy-done.3 = bf16[8,3072]{1,0:T(8,128)(2,1)S(1)} copy-done((bf16[8,3072]{1,0:T(8,128)(2,1)S(1)}, bf16[8,3072]{1,0:T(8,128)(2,1)}, u32[]{:S(2)}) %copy-start.3) | copy-done | bytes 49176
  21.0 2.2 %shard_map.82 = (bf16[8,3200]{1,0:T(8,128)(2,1)S(1)}, bf16[8,3200]{1,0:T(8,128)(2,1)S(1)}, bf16[8,3200]{1,0:T(8,128)(2,1)S(1)}, bf16[8,3200]{1,0:T(8,128)(2,1)S(1)}) custom-call(bf16[8,3072]{1,0:T(8,128)(2,1)S(1)} %copy-done.3, bf16[8,3072]{1,0:T(8,128)(2,1)S(1)} %collective-permute-done.refs_1_, bf16[8,3072]{1,0:T(8,128)(2,1)S(1)} %collective-permute-done.1.refs_2_, ...), custom_call_target="tpu_custom_call" | custom-call | tf_op jit(solution)/shard_map/pallas_call | solution.py:149
  23.2 0.6 %copy-done.2 = bf16[8,3200]{1,0:T(8,128)(2,1)} copy-done((bf16[8,3200]{1,0:T(8,128)(2,1)}, bf16[8,3200]{1,0:T(8,128)(2,1)S(1)}, u32[]{:S(2)}) %copy-start.2) | copy-done | bytes 51224
  23.8 1.0 %collective-permute-start.16 = (bf16[8,3200]{1,0:T(8,128)(2,1)S(1)}, bf16[8,3200]{1,0:T(8,128)(2,1)S(1)}, u32[]{:S(2)}, u32[]{:S(2)}) collective-permute-start(bf16[8,3200]{1,0:T(8,128)(2,1)S(1)} %get-tuple-element.11), channel_id=1, source_target_pairs={{0,8},{1,9},{2,10},{3,11},{4,12},{5,13},{6,14},{7,15},{8,0},{9,1},... | collective-permute-start | bytes 153608 | tf_op jit(solution)/shard_map/ppermute | solution.py:112
  24.8 3.4 %collective-permute-start.17 = (bf16[8,3200]{1,0:T(8,128)(2,1)S(1)}, bf16[8,3200]{1,0:T(8,128)(2,1)S(1)}, u32[]{:S(2)}, u32[]{:S(2)}) collective-permute-start(bf16[8,3200]{1,0:T(8,128)(2,1)S(1)} %get-tuple-element.12), channel_id=1, source_target_pairs={{0,12},{1,13},{2,14},{3,15},{4,8},{5,9},{6,10},{7,11},{8,4},{9,5},... | collective-permute-start | bytes 153608 | tf_op jit(solution)/shard_map/ppermute | solution.py:112
  28.2 0.6 %collective-permute-done.16.refs_2_ = bf16[8,3200]{1,0:T(8,128)(2,1)S(1)} collective-permute-done((bf16[8,3200]{1,0:T(8,128)(2,1)S(1)}, bf16[8,3200]{1,0:T(8,128)(2,1)S(1)}, u32[]{:S(2)}, u32[]{:S(2)}) %collective-permute-start.16) | collective-permute-done | bytes 51232 | tf_op jit(solution)/shard_map/ppermute | solution.py:112
  28.8 2.1 %collective-permute-done.17.refs_3_ = bf16[8,3200]{1,0:T(8,128)(2,1)S(1)} collective-permute-done((bf16[8,3200]{1,0:T(8,128)(2,1)S(1)}, bf16[8,3200]{1,0:T(8,128)(2,1)S(1)}, u32[]{:S(2)}, u32[]{:S(2)}) %collective-permute-start.17) | collective-permute-done | bytes 51232 | tf_op jit(solution)/shard_map/ppermute | solution.py:112
  30.9 0.6 %copy-done.8 = bf16[8,3200]{1,0:T(8,128)(2,1)} copy-done((bf16[8,3200]{1,0:T(8,128)(2,1)}, bf16[8,3200]{1,0:T(8,128)(2,1)S(1)}, u32[]{:S(2)}) %copy-start.8) | copy-done | bytes 51224
  31.5 1.8 %shard_map.83 = bf16[8,3072]{1,0:T(8,128)(2,1)} custom-call(bf16[8,3200]{1,0:T(8,128)(2,1)} %copy-done.2, bf16[8,3200]{1,0:T(8,128)(2,1)} %copy-done.6, bf16[8,3200]{1,0:T(8,128)(2,1)} %copy-done.7, bf16[8,3200]{1,0:T(8,128)(2,1)} %copy-done.8), custom_call_target="tpu_custom_call" | custom-call | tf_op jit(solution)/shard_map/pallas_call | solution.py:157
  (35 shorter events, 0.2 us)
Async XLA Ops:
  0.0 6.1 %collective-permute-start.9 = (bf16[8,1024]{1,0:T(8,128)(2,1)}, bf16[8,1024]{1,0:T(8,128)(2,1)S(1)}, u32[]{:S(2)}, u32[]{:S(2)}) collective-permute-start(bf16[8,1024]{1,0:T(8,128)(2,1)} %refs_12_.1), channel_id=1, source_target_pairs={{0,1},{1,0},{2,3},{3,2},{4,5},{5,4},{6,7},{7,6},{8,9},{9,8},{10,11... | collective-permute-start | bytes 49160 | tf_op jit(solution)/shard_map/ppermute | solution.py:112
  0.5 6.0 %collective-permute-start.10 = (bf16[8,1024]{1,0:T(8,128)(2,1)}, bf16[8,1024]{1,0:T(8,128)(2,1)S(1)}, u32[]{:S(2)}, u32[]{:S(2)}) collective-permute-start(bf16[8,1024]{1,0:T(8,128)(2,1)} %refs_12_.1), channel_id=1, source_target_pairs={{0,2},{1,3},{2,0},{3,1},{4,6},{5,7},{6,4},{7,5},{8,10},{9,11},{10,... | collective-permute-start | bytes 49160 | tf_op jit(solution)/shard_map/ppermute | solution.py:112
  3.0 3.6 %collective-permute-start.12 = (bf16[8,1024]{1,0:T(8,128)(2,1)}, bf16[8,1024]{1,0:T(8,128)(2,1)S(1)}, u32[]{:S(2)}, u32[]{:S(2)}) collective-permute-start(bf16[8,1024]{1,0:T(8,128)(2,1)} %refs_16_.1), channel_id=1, source_target_pairs={{0,1},{1,0},{2,3},{3,2},{4,5},{5,4},{6,7},{7,6},{8,9},{9,8},{10,11... | collective-permute-start | bytes 49160 | tf_op jit(solution)/shard_map/ppermute | solution.py:112
  3.2 6.3 %collective-permute-start.13 = (bf16[8,1024]{1,0:T(8,128)(2,1)}, bf16[8,1024]{1,0:T(8,128)(2,1)S(1)}, u32[]{:S(2)}, u32[]{:S(2)}) collective-permute-start(bf16[8,1024]{1,0:T(8,128)(2,1)} %refs_16_.1), channel_id=1, source_target_pairs={{0,2},{1,3},{2,0},{3,1},{4,6},{5,7},{6,4},{7,5},{8,10},{9,11},{10,... | collective-permute-start | bytes 49160 | tf_op jit(solution)/shard_map/ppermute | solution.py:112
  3.5 10.3 %collective-permute-start.4 = (bf16[64,1024]{1,0:T(8,128)(2,1)}, bf16[64,1024]{1,0:T(8,128)(2,1)S(1)}, u32[]{:S(2)}, u32[]{:S(2)}) collective-permute-start(bf16[64,1024]{1,0:T(8,128)(2,1)} %refs_4_.1), channel_id=1, source_target_pairs={{0,2},{1,3},{2,0},{3,1},{4,6},{5,7},{6,4},{7,5},{8,10},{9,11},{10,... | collective-permute-start | bytes 393224 | tf_op jit(solution)/shard_map/ppermute | solution.py:112
  5.2 0.7 %copy-start.9 = (s32[128]{0:T(128)S(1)}, s32[128]{0:T(128)}, u32[]{:S(2)}) copy-start(s32[128]{0:T(128)} %param.13) | copy-start | bytes 1540
  5.3 13.1 %copy-start.5 = (bf16[8,1024]{1,0:T(8,128)(2,1)S(1)}, bf16[8,1024]{1,0:T(8,128)(2,1)}, u32[]{:S(2)}) copy-start(bf16[8,1024]{1,0:T(8,128)(2,1)} %refs_16_.1) | copy-start | bytes 49156
  5.3 13.1 %copy-start.4 = (bf16[8,1024]{1,0:T(8,128)(2,1)S(1)}, bf16[8,1024]{1,0:T(8,128)(2,1)}, u32[]{:S(2)}) copy-start(bf16[8,1024]{1,0:T(8,128)(2,1)} %refs_12_.1) | copy-start | bytes 49156
  6.1 8.2 %collective-permute-start.7 = (bf16[64,1024]{1,0:T(8,128)(2,1)}, bf16[64,1024]{1,0:T(8,128)(2,1)S(1)}, u32[]{:S(2)}, u32[]{:S(2)}) collective-permute-start(bf16[64,1024]{1,0:T(8,128)(2,1)} %refs_8_.1), channel_id=1, source_target_pairs={{0,2},{1,3},{2,0},{3,1},{4,6},{5,7},{6,4},{7,5},{8,10},{9,11},{10,... | collective-permute-start | bytes 393224 | tf_op jit(solution)/shard_map/ppermute | solution.py:112
  6.4 4.7 %collective-permute-start.11 = (bf16[8,1024]{1,0:T(8,128)(2,1)S(1)}, bf16[8,1024]{1,0:T(8,128)(2,1)S(1)}, u32[]{:S(2)}, u32[]{:S(2)}) collective-permute-start(bf16[8,1024]{1,0:T(8,128)(2,1)S(1)} %collective-permute-done.10.refs_14_), channel_id=1, source_target_pairs={{0,1},{1,0},{2,3},{3,2},{4,5},{5,4},{6,7},{7,6},{8,9},{9,8},{10,11... | collective-permute-start | bytes 49160 | tf_op jit(solution)/shard_map/ppermute | solution.py:112
  6.6 6.0 %collective-permute-start.1 = (bf16[8,3072]{1,0:T(8,128)(2,1)}, bf16[8,3072]{1,0:T(8,128)(2,1)S(1)}, u32[]{:S(2)}, u32[]{:S(2)}) collective-permute-start(bf16[8,3072]{1,0:T(8,128)(2,1)} %refs_0_.1), channel_id=1, source_target_pairs={{0,8},{1,9},{2,10},{3,11},{4,12},{5,13},{6,14},{7,15},{8,0},{9,1},... | collective-permute-start | bytes 147464 | tf_op jit(solution)/shard_map/ppermute | solution.py:112
  9.5 4.3 %collective-permute-start = (bf16[8,3072]{1,0:T(8,128)(2,1)}, bf16[8,3072]{1,0:T(8,128)(2,1)S(1)}, u32[]{:S(2)}, u32[]{:S(2)}) collective-permute-start(bf16[8,3072]{1,0:T(8,128)(2,1)} %refs_0_.1), channel_id=1, source_target_pairs={{0,4},{1,5},{2,6},{3,7},{4,0},{5,1},{6,2},{7,3},{8,12},{9,13},{10,... | collective-permute-start | bytes 147464 | tf_op jit(solution)/shard_map/ppermute | solution.py:112
  11.1 1.2 %collective-permute-start.14 = (bf16[8,1024]{1,0:T(8,128)(2,1)S(1)}, bf16[8,1024]{1,0:T(8,128)(2,1)S(1)}, u32[]{:S(2)}, u32[]{:S(2)}) collective-permute-start(bf16[8,1024]{1,0:T(8,128)(2,1)S(1)} %collective-permute-done.13.refs_18_), channel_id=1, source_target_pairs={{0,1},{1,0},{2,3},{3,2},{4,5},{5,4},{6,7},{7,6},{8,9},{9,8},{10,11... | collective-permute-start | bytes 49160 | tf_op jit(solution)/shard_map/ppermute | solution.py:112
  12.3 6.1 %collective-permute-start.2 = (bf16[8,3072]{1,0:T(8,128)(2,1)}, bf16[8,3072]{1,0:T(8,128)(2,1)S(1)}, u32[]{:S(2)}, u32[]{:S(2)}) collective-permute-start(bf16[8,3072]{1,0:T(8,128)(2,1)} %refs_0_.1), channel_id=1, source_target_pairs={{0,12},{1,13},{2,14},{3,15},{4,8},{5,9},{6,10},{7,11},{8,4},{9,5},... | collective-permute-start | bytes 147464 | tf_op jit(solution)/shard_map/ppermute | solution.py:112
  12.6 5.7 %collective-permute-start.3 = (bf16[64,1024]{1,0:T(8,128)(2,1)}, bf16[64,1024]{1,0:T(8,128)(2,1)S(1)}, u32[]{:S(2)}, u32[]{:S(2)}) collective-permute-start(bf16[64,1024]{1,0:T(8,128)(2,1)} %refs_4_.1), channel_id=1, source_target_pairs={{0,1},{1,0},{2,3},{3,2},{4,5},{5,4},{6,7},{7,6},{8,9},{9,8},{10,11... | collective-permute-start | bytes 393224 | tf_op jit(solution)/shard_map/ppermute | solution.py:112
  13.8 4.6 %collective-permute-start.6 = (bf16[64,1024]{1,0:T(8,128)(2,1)}, bf16[64,1024]{1,0:T(8,128)(2,1)S(1)}, u32[]{:S(2)}, u32[]{:S(2)}) collective-permute-start(bf16[64,1024]{1,0:T(8,128)(2,1)} %refs_8_.1), channel_id=1, source_target_pairs={{0,1},{1,0},{2,3},{3,2},{4,5},{5,4},{6,7},{7,6},{8,9},{9,8},{10,11... | collective-permute-start | bytes 393224 | tf_op jit(solution)/shard_map/ppermute | solution.py:112
  13.8 4.6 %collective-permute-start.5 = (bf16[64,1024]{1,0:T(8,128)(2,1)S(1)}, bf16[64,1024]{1,0:T(8,128)(2,1)S(1)}, u32[]{:S(2)}, u32[]{:S(2)}) collective-permute-start(bf16[64,1024]{1,0:T(8,128)(2,1)S(1)} %collective-permute-done.4.refs_6_), channel_id=1, source_target_pairs={{0,1},{1,0},{2,3},{3,2},{4,5},{5,4},{6,7},{7,6},{8,9},{9,8},{10,11... | collective-permute-start | bytes 393224 | tf_op jit(solution)/shard_map/ppermute | solution.py:112
  14.3 4.1 %collective-permute-start.8 = (bf16[64,1024]{1,0:T(8,128)(2,1)S(1)}, bf16[64,1024]{1,0:T(8,128)(2,1)S(1)}, u32[]{:S(2)}, u32[]{:S(2)}) collective-permute-start(bf16[64,1024]{1,0:T(8,128)(2,1)S(1)} %collective-permute-done.7.refs_10_), channel_id=1, source_target_pairs={{0,1},{1,0},{2,3},{3,2},{4,5},{5,4},{6,7},{7,6},{8,9},{9,8},{10,11... | collective-permute-start | bytes 393224 | tf_op jit(solution)/shard_map/ppermute | solution.py:112
  18.4 0.9 %copy-start = (bf16[64,1024]{1,0:T(8,128)(2,1)S(1)}, bf16[64,1024]{1,0:T(8,128)(2,1)}, u32[]{:S(2)}) copy-start(bf16[64,1024]{1,0:T(8,128)(2,1)} %refs_4_.1) | copy-start | bytes 393220
  19.3 0.9 %copy-start.1 = (bf16[64,1024]{1,0:T(8,128)(2,1)S(1)}, bf16[64,1024]{1,0:T(8,128)(2,1)}, u32[]{:S(2)}) copy-start(bf16[64,1024]{1,0:T(8,128)(2,1)} %refs_8_.1) | copy-start | bytes 393220
  20.2 0.8 %copy-start.3 = (bf16[8,3072]{1,0:T(8,128)(2,1)S(1)}, bf16[8,3072]{1,0:T(8,128)(2,1)}, u32[]{:S(2)}) copy-start(bf16[8,3072]{1,0:T(8,128)(2,1)} %refs_0_.1) | copy-start | bytes 147460
  23.2 0.6 %copy-start.2 = (bf16[8,3200]{1,0:T(8,128)(2,1)}, bf16[8,3200]{1,0:T(8,128)(2,1)S(1)}, u32[]{:S(2)}) copy-start(bf16[8,3200]{1,0:T(8,128)(2,1)S(1)} %get-tuple-element.9.refs_0_) | copy-start | bytes 153604
  23.8 4.4 %collective-permute-start.15 = (bf16[8,3200]{1,0:T(8,128)(2,1)S(1)}, bf16[8,3200]{1,0:T(8,128)(2,1)S(1)}, u32[]{:S(2)}, u32[]{:S(2)}) collective-permute-start(bf16[8,3200]{1,0:T(8,128)(2,1)S(1)} %get-tuple-element.10), channel_id=1, source_target_pairs={{0,4},{1,5},{2,6},{3,7},{4,0},{5,1},{6,2},{7,3},{8,12},{9,13},{10,... | collective-permute-start | bytes 153608 | tf_op jit(solution)/shard_map/ppermute | solution.py:112
  23.8 5.0 %collective-permute-start.16 = (bf16[8,3200]{1,0:T(8,128)(2,1)S(1)}, bf16[8,3200]{1,0:T(8,128)(2,1)S(1)}, u32[]{:S(2)}, u32[]{:S(2)}) collective-permute-start(bf16[8,3200]{1,0:T(8,128)(2,1)S(1)} %get-tuple-element.11), channel_id=1, source_target_pairs={{0,8},{1,9},{2,10},{3,11},{4,12},{5,13},{6,14},{7,15},{8,0},{9,1},... | collective-permute-start | bytes 153608 | tf_op jit(solution)/shard_map/ppermute | solution.py:112
  24.8 6.1 %collective-permute-start.17 = (bf16[8,3200]{1,0:T(8,128)(2,1)S(1)}, bf16[8,3200]{1,0:T(8,128)(2,1)S(1)}, u32[]{:S(2)}, u32[]{:S(2)}) collective-permute-start(bf16[8,3200]{1,0:T(8,128)(2,1)S(1)} %get-tuple-element.12), channel_id=1, source_target_pairs={{0,12},{1,13},{2,14},{3,15},{4,8},{5,9},{6,10},{7,11},{8,4},{9,5},... | collective-permute-start | bytes 153608 | tf_op jit(solution)/shard_map/ppermute | solution.py:112
  28.2 2.7 %copy-start.6 = (bf16[8,3200]{1,0:T(8,128)(2,1)}, bf16[8,3200]{1,0:T(8,128)(2,1)S(1)}, u32[]{:S(2)}) copy-start(bf16[8,3200]{1,0:T(8,128)(2,1)S(1)} %collective-permute-done.15.refs_1_) | copy-start | bytes 153604
  28.8 2.1 %copy-start.7 = (bf16[8,3200]{1,0:T(8,128)(2,1)}, bf16[8,3200]{1,0:T(8,128)(2,1)S(1)}, u32[]{:S(2)}) copy-start(bf16[8,3200]{1,0:T(8,128)(2,1)S(1)} %collective-permute-done.16.refs_2_) | copy-start | bytes 153604
  30.9 0.6 %copy-start.8 = (bf16[8,3200]{1,0:T(8,128)(2,1)}, bf16[8,3200]{1,0:T(8,128)(2,1)S(1)}, u32[]{:S(2)}) copy-start(bf16[8,3200]{1,0:T(8,128)(2,1)S(1)} %collective-permute-done.17.refs_3_) | copy-start | bytes 153604

commit v2 on v1

--- a/solution.py
+++ b/solution.py
@@ -17,25 +17,51 @@
 STRIDE = 32
 
 
-def stacked(refs, columns):
-    blocks = [ref[:, columns] for ref in refs]
-    if blocks[0].shape[0] % 16 == 0:
-        return jnp.concatenate(blocks, axis=0)
-    wide = jnp.concatenate([block.astype(jnp.float32) for block in blocks], axis=0)
-    return wide.astype(jnp.bfloat16)
+def prepare_kernel(
+    near, queries, prefix_keys, prefix_values, tree_keys, tree_values, parents,
+    own_queries, own, bias, tree_scratch, parent_scratch, sems,
+):
+    slab = prefix_keys.shape[0]
+    copies = [
+        pltpu.make_async_copy(prefix_keys, own.at[:slab], sems.at[0]),
+        pltpu.make_async_copy(prefix_values, own.at[slab : 2 * slab], sems.at[1]),
+        pltpu.make_async_copy(tree_keys, tree_scratch.at[0], sems.at[2]),
+        pltpu.make_async_copy(tree_values, tree_scratch.at[1], sems.at[3]),
+        pltpu.make_async_copy(queries, own_queries, sems.at[4]),
+    ]
+    parent_copy = pltpu.make_async_copy(parents, parent_scratch, sems.at[5])
+    parent_copy.start()
+    for copy in copies:
+        copy.start()
+    position = lax.axis_index("rows")
+    local_rows = queries.shape[0]
+    rows, tokens = bias.shape
+    slot = lax.broadcasted_iota(jnp.int32, (rows, 1), 0)
+    walker = (position ^ (slot // local_rows * near)) * local_rows + slot % local_rows
+    slot = lax.broadcasted_iota(jnp.int32, (1, tokens), 1)
+    token = (position ^ (slot // local_rows)) * local_rows + slot % local_rows
+    columns = lax.broadcasted_iota(jnp.int32, (rows, parents.shape[1]), 1)
+    allowed = walker == token
+    parent_copy.wait()
+    parent = parent_scratch[...]
+    for _ in range(TREE_DEPTH - 1):
+        walker = jnp.sum(jnp.where(walker == columns, parent, 0), axis=1, keepdims=True)
+        allowed = allowed | (walker == token)
+    bias[...] = jnp.where(allowed, 0.0, -jnp.inf)
+    for copy in copies:
+        copy.wait()
+    both = jnp.concatenate([tree_scratch[0].astype(jnp.float32), tree_scratch[1].astype(jnp.float32)], axis=0)
+    own[2 * slab :] = both.astype(own.dtype)
 
 
 def attend_kernel(owners, pieces, *refs):
     queries = refs[:owners]
-    at = owners
-    slab_keys, slab_values, tree_keys, tree_values = (
-        refs[at + i * pieces : at + (i + 1) * pieces] for i in range(4)
-    )
-    at += 4 * pieces
-    bias_ref = refs[at]
-    outs = refs[at + 1 :]
+    blocks = refs[owners : owners + pieces]
+    bias_ref = refs[owners + pieces]
+    outs = refs[owners + pieces + 1 :]
     local_rows = queries[0].shape[0]
     rows = owners * local_rows
+    slab_rows = (blocks[0].shape[0] - 2 * local_rows) // 2
     bias = jnp.concatenate([bias_ref[...]] * GROUPS, axis=0)
     lane = lax.broadcasted_iota(jnp.int32, (rows, LANES), 1)
     stats = jnp.zeros((rows, LANES), jnp.float32)
@@ -50,8 +76,13 @@
             ],
             axis=0,
         ).astype(jnp.bfloat16)
-        slab = lax.dot_general(query, stacked(slab_keys, columns), nt, preferred_element_type=jnp.float32)
-        tree = lax.dot_general(query, stacked(tree_keys, columns), nt, preferred_element_type=jnp.float32)
+        slab_keys = jnp.concatenate([ref[:slab_rows, columns] for ref in blocks], axis=0)
+        slab_values = jnp.concatenate([ref[slab_rows : 2 * slab_rows, columns] for ref in blocks], axis=0)
+        trees = [ref[2 * slab_rows :, columns].astype(jnp.float32) for ref in blocks]
+        tree_keys = jnp.concatenate([tree[:local_rows] for tree in trees], axis=0).astype(jnp.bfloat16)
+        tree_values = jnp.concatenate([tree[local_rows:] for tree in trees], axis=0).astype(jnp.bfloat16)
+        slab = lax.dot_general(query, slab_keys, nt, preferred_element_type=jnp.float32)
+        tree = lax.dot_general(query, tree_keys, nt, preferred_element_type=jnp.float32)
         slab = slab * HEAD_DIM ** (-0.5)
         tree = tree * HEAD_DIM ** (-0.5) + bias
         maxima = jnp.maximum(
@@ -61,10 +92,8 @@
         tree = jnp.exp(tree - maxima)
         masses = jnp.sum(slab, axis=1, keepdims=True) + jnp.sum(tree, axis=1, keepdims=True)
         weighted = jnp.dot(
-            slab.astype(jnp.bfloat16), stacked(slab_values, columns), preferred_element_type=jnp.float32
-        ) + jnp.dot(
-            tree.astype(jnp.bfloat16), stacked(tree_values, columns), preferred_element_type=jnp.float32
-        )
+            slab.astype(jnp.bfloat16), slab_values, preferred_element_type=jnp.float32
+        ) + jnp.dot(tree.astype(jnp.bfloat16), tree_values, preferred_element_type=jnp.float32)
         weighted = weighted / masses
         level = maxima + jnp.log(masses)
         for g in range(GROUPS):
@@ -108,18 +137,12 @@
         out[:, wide] = total.astype(out.dtype)
 
 
+def held(memory, arrays):
+    return [pltpu.with_memory_space_constraint(x, memory) for x in arrays]
+
+
 def swap(x, offset):
     return lax.ppermute(x, "rows", [(i, i ^ offset) for i in range(lax.axis_size("rows"))])
-
-
-def tree_bias(parents, row_ids, token_ids):
-    columns = jnp.arange(parents.shape[0], dtype=jnp.int32)
-    walker = row_ids
-    allowed = walker[:, None] == token_ids[None, :]
-    for _ in range(TREE_DEPTH - 1):
-        walker = jnp.sum(jnp.where(walker[:, None] == columns[None, :], parents[None, :], 0), axis=1)
-        allowed = allowed | (walker[:, None] == token_ids[None, :])
-    return jnp.where(allowed, 0.0, -jnp.inf).astype(jnp.float32)
 
 
 def shards(queries, prefix_keys, prefix_values, tree_keys, tree_values, parents):
@@ -129,37 +152,53 @@
     near = 2**near_bits
     far = size // near
     local_rows = queries.shape[0]
-    position = lax.axis_index("rows")
-
-    pieces = {0: (prefix_keys, prefix_values, tree_keys, tree_values)}
+    slab = prefix_keys.shape[0]
+    far_offsets = [near * i for i in range(far)]
+    offsets = list(range(near))
+    vmem = pl.BlockSpec(memory_space=pltpu.VMEM)
+    hbm = pl.BlockSpec(memory_space=pltpu.HBM)
+    own_queries, own, bias = pl.pallas_call(
+        functools.partial(prepare_kernel, near),
+        out_shape=[
+            pltpu.VMEM(queries.shape, queries.dtype),
+            pltpu.VMEM((2 * (slab + local_rows), prefix_keys.shape[1]), prefix_keys.dtype),
+            pltpu.VMEM((far * local_rows, near * local_rows), jnp.float32),
+        ],
+        in_specs=[hbm] * 6,
+        out_specs=[vmem] * 3,
+        scratch_shapes=[
+            pltpu.VMEM((2,) + tree_keys.shape, tree_keys.dtype),
+            pltpu.VMEM((1,) + parents.shape, parents.dtype),
+            pltpu.SemaphoreType.DMA((6,)),
+        ],
+        compiler_params=pltpu.CompilerParams(vmem_limit_bytes=16 * 2**20),
+    )(*held(pltpu.HBM, [queries, prefix_keys, prefix_values, tree_keys, tree_values, parents[None, :]]))
+
+    all_queries = [own_queries] + [swap(queries, offset) for offset in far_offsets[1:]]
+    pieces = {0: own}
     for bit in reversed(range(near_bits)):
         for offset in list(pieces):
-            pieces[offset ^ (1 << bit)] = tuple(swap(x, 1 << bit) for x in pieces[offset])
-    far_offsets = [near * i for i in range(far)]
-    all_queries = [queries] + [swap(queries, offset) for offset in far_offsets[1:]]
-
-    slots = jnp.arange(local_rows, dtype=jnp.int32)[None, :]
-    row_ids = ((position ^ jnp.array(far_offsets, jnp.int32))[:, None] * local_rows + slots).reshape(-1)
-    offsets = sorted(pieces)
-    token_ids = ((position ^ jnp.array(offsets, jnp.int32))[:, None] * local_rows + slots).reshape(-1)
-    bias = tree_bias(parents, row_ids, token_ids)
-
-    operands = all_queries + [pieces[offset][i] for i in range(4) for offset in offsets] + [bias]
-    vmem = pl.BlockSpec(memory_space=pltpu.VMEM)
+            piece = pieces[offset]
+            if bit == 0 and offset:
+                piece, *all_queries = lax.optimization_barrier((piece, *all_queries))
+            pieces[offset ^ (1 << bit)] = swap(piece, 1 << bit)
+
+    operands = all_queries + [pieces[offset] for offset in offsets] + [bias]
     partials = pl.pallas_call(
         functools.partial(attend_kernel, far, near),
-        out_shape=[jax.ShapeDtypeStruct((local_rows, WIDTH + LANES), jnp.bfloat16)] * far,
+        out_shape=[pltpu.VMEM((local_rows, WIDTH + LANES), jnp.bfloat16)] * far,
         in_specs=[vmem] * len(operands),
         out_specs=[vmem] * far,
         compiler_params=pltpu.CompilerParams(vmem_limit_bytes=32 * 2**20),
-    )(*operands)
+    )(*held(pltpu.VMEM, operands))
     parts = [partials[0]] + [swap(partials[i], far_offsets[i]) for i in range(1, far)]
     return pl.pallas_call(
         merge_kernel,
         out_shape=jax.ShapeDtypeStruct((local_rows, WIDTH), jnp.bfloat16),
         in_specs=[vmem] * far,
         out_specs=vmem,
-    )(*parts)
+        compiler_params=pltpu.CompilerParams(vmem_limit_bytes=16 * 2**20),
+    )(*held(pltpu.VMEM, parts))
 
 
 def solution(mesh):

time: 33.6 us -> 26.9 us (0.80)
  local copies, waits for them, and re-layouts: 4.42 us -> 0.01 us
  starting transfers between devices: 15.4 us -> 11.7 us
  waiting for transfers between devices: 8.7 us -> 10.9 us
  other arithmetic: 0.75 us -> 0 us
    unnamed x20 -> x2, local copies, waits for them, and re-layouts: 4.25 us -> 0.01 us
    ppermute x18 -> x9, starting transfers between devices: 15.4 us -> 11.7 us  [swap(): lax.ppermute(x, 'rows', [(i, i ^ offset) for i in range(lax.axis_size('ro...]
    ppermute x18 -> x9, waiting for transfers between devices: 8.7 us -> 10.9 us  [swap(): lax.ppermute(x, 'rows', [(i, i ^ offset) for i in range(lax.axis_size('ro...]
    pallas_call x1 -> x2, Pallas kernels: 2.16 us -> 3.2 us  [the longest x1 2.15 us: shards(): pl.pallas_call(functools.partial(attend_kernel, far, near), out_shape=[pl...]
    pallas_call x1, Pallas kernels: 1.8 us -> 0.93 us  [shards(): pl.pallas_call(merge_kernel, out_shape=jax.ShapeDtypeStruct((local_rows,...]
    reduce_sum x3 -> x0, other arithmetic: 0.53 us -> none  [tree_bias(): jnp.sum(jnp.where(walker[:, None] == columns[None, :], parents[None, :],...]
  transfers between devices with their start and end apart: 18 -> 9, of which waited for: 5 -> 6; matrix products, arithmetic and copies ran while one was open for 3% -> 0% of each run, Pallas kernels for 0% -> 0%
where the time goes in v2:
time: 26.9 us; the launch traced here: 26.7 us
  starting transfers between devices  11.7 us (43%)
  waiting for transfers between devices  10.9 us (41%)
  Pallas kernels  4.13 us (15%)
    ppermute x9, starting transfers between devices, swap(): lax.ppermute(x, 'rows', [(i, i ^ offset) for i in range(lax.axis_size('ro...  11.7 us
    ppermute x9, waiting for transfers between devices, swap(): lax.ppermute(x, 'rows', [(i, i ^ offset) for i in range(lax.axis_size('ro...  10.9 us
    pallas_call x1, Pallas kernels, shards(): pl.pallas_call(functools.partial(attend_kernel, far, near), out_shape=[pl...  2.15 us
    pallas_call x1, Pallas kernels, shards(): pl.pallas_call(functools.partial(prepare_kernel, near), out_shape=[pltpu....  1.05 us
    pallas_call x1, Pallas kernels, shards(): pl.pallas_call(merge_kernel, out_shape=jax.ShapeDtypeStruct((local_rows,...  0.93 us
  transfers between devices with their start and end apart: 9, of which 6 were waited for; matrix products, arithmetic and copies ran while one was open for 0% of the time, Pallas kernels for 0%

profile of v2, /device:TPU:0, one launch (start us, length us, event | category | flops | bytes accessed | tf_op | source)
XLA Modules:
  0.0 26.7 jit_solution(124604093393994532)
XLA Ops:
  0.0 0.0 copy-start
  0.0 1.0 %shard_map.64 = (bf16[8,3072]{1,0:T(8,128)(2,1)S(1)}, bf16[144,1024]{1,0:T(8,128)(2,1)S(1)}, f32[32,32]{1,0:T(8,128)S(1)}) custom-call(bf16[8,3072]{1,0:T(8,128)(2,1)} %queries.1, bf16[64,1024]{1,0:T(8,128)(2,1)} %prefix_keys.1, bf16[64,1024]{1,0:T(8,128)(2,1)} %prefix_values.1, bf16[8,1024]{1,0:T(8,128)(2,1)} %tree_keys.1, bf16[8,1024]{1,0:T(8,128)(2,1)} %tree_values.1, ...), custom_call_target="tpu_custom_call" | custom-call | tf_op jit(solution)/shard_map/pallas_call | solution.py:160
  1.1 3.0 %collective-permute-start = (bf16[144,1024]{1,0:T(8,128)(2,1)S(1)}, bf16[144,1024]{1,0:T(8,128)(2,1)S(1)}, u32[]{:S(2)}, u32[]{:S(2)}) collective-permute-start(bf16[144,1024]{1,0:T(8,128)(2,1)S(1)} %get-tuple-element.17.refs_4_), channel_id=1, source_target_pairs={{0,2},{1,3},{2,0},{3,1},{4,6},{5,7},{6,4},{7,5},{8,10},{9,11},{10,... | collective-permute-start | bytes 884744 | tf_op jit(solution)/shard_map/ppermute | solution.py:145
  4.1 0.0 copy-done
  4.1 1.6 %collective-permute-start.1 = (bf16[8,3072]{1,0:T(8,128)(2,1)S(1)}, bf16[8,3072]{1,0:T(8,128)(2,1)S(1)}, u32[]{:S(2)}, u32[]{:S(2)}) collective-permute-start(bf16[8,3072]{1,0:T(8,128)(2,1)S(1)} %copy-done), channel_id=1, source_target_pairs={{0,4},{1,5},{2,6},{3,7},{4,0},{5,1},{6,2},{7,3},{8,12},{9,13},{10,... | collective-permute-start | bytes 147464 | tf_op jit(solution)/shard_map/ppermute | solution.py:145
  5.7 2.5 %collective-permute-start.3 = (bf16[8,3072]{1,0:T(8,128)(2,1)S(1)}, bf16[8,3072]{1,0:T(8,128)(2,1)S(1)}, u32[]{:S(2)}, u32[]{:S(2)}) collective-permute-start(bf16[8,3072]{1,0:T(8,128)(2,1)S(1)} %copy-done), channel_id=1, source_target_pairs={{0,12},{1,13},{2,14},{3,15},{4,8},{5,9},{6,10},{7,11},{8,4},{9,5},... | collective-permute-start | bytes 147464 | tf_op jit(solution)/shard_map/ppermute | solution.py:145
  8.1 0.1 collective-permute-start.2
  8.3 0.0 collective-permute-start.4
  8.3 0.0 collective-permute-done.1.refs_1_
  8.3 3.6 %collective-permute-done.3.refs_3_ = bf16[8,3072]{1,0:T(8,128)(2,1)S(1)} collective-permute-done((bf16[8,3072]{1,0:T(8,128)(2,1)S(1)}, bf16[8,3072]{1,0:T(8,128)(2,1)S(1)}, u32[]{:S(2)}, u32[]{:S(2)}) %collective-permute-start.3) | collective-permute-done | bytes 49184 | tf_op jit(solution)/shard_map/ppermute | solution.py:145
  11.9 1.8 %collective-permute-done.2.refs_2_ = bf16[8,3072]{1,0:T(8,128)(2,1)S(1)} collective-permute-done((bf16[8,3072]{1,0:T(8,128)(2,1)S(1)}, bf16[8,3072]{1,0:T(8,128)(2,1)S(1)}, u32[]{:S(2)}, u32[]{:S(2)}) %collective-permute-start.2) | collective-permute-done | bytes 49184 | tf_op jit(solution)/shard_map/ppermute | solution.py:145
  13.7 0.0 collective-permute-done.refs_6_
  13.7 0.0 collective-permute-start.5
  13.7 0.0 collective-permute-done.4.refs_5_
  13.7 1.6 %collective-permute-done.5.refs_7_ = bf16[144,1024]{1,0:T(8,128)(2,1)S(1)} collective-permute-done((bf16[144,1024]{1,0:T(8,128)(2,1)S(1)}, bf16[144,1024]{1,0:T(8,128)(2,1)S(1)}, u32[]{:S(2)}, u32[]{:S(2)}) %collective-permute-start.5) | collective-permute-done | bytes 294944 | tf_op jit(solution)/shard_map/ppermute | solution.py:145
  15.2 2.2 %shard_map.65 = (bf16[8,3200]{1,0:T(8,128)(2,1)S(1)}, bf16[8,3200]{1,0:T(8,128)(2,1)S(1)}, bf16[8,3200]{1,0:T(8,128)(2,1)S(1)}, bf16[8,3200]{1,0:T(8,128)(2,1)S(1)}) custom-call(bf16[8,3072]{1,0:T(8,128)(2,1)S(1)} %get-tuple-element.19.refs_0_, bf16[8,3072]{1,0:T(8,128)(2,1)S(1)} %collective-permute-done.1.refs_1_, ...), custom_call_target="tpu_custom_call" | custom-call | tf_op jit(solution)/shard_map/pallas_call | solution.py:187
  17.4 0.3 %collective-permute-start.6 = (bf16[8,3200]{1,0:T(8,128)(2,1)S(1)}, bf16[8,3200]{1,0:T(8,128)(2,1)S(1)}, u32[]{:S(2)}, u32[]{:S(2)}) collective-permute-start(bf16[8,3200]{1,0:T(8,128)(2,1)S(1)} %get-tuple-element.26), channel_id=1, source_target_pairs={{0,4},{1,5},{2,6},{3,7},{4,0},{5,1},{6,2},{7,3},{8,12},{9,13},{10,... | collective-permute-start | bytes 153608 | tf_op jit(solution)/shard_map/ppermute | solution.py:145
  17.7 2.1 %collective-permute-start.7 = (bf16[8,3200]{1,0:T(8,128)(2,1)S(1)}, bf16[8,3200]{1,0:T(8,128)(2,1)S(1)}, u32[]{:S(2)}, u32[]{:S(2)}) collective-permute-start(bf16[8,3200]{1,0:T(8,128)(2,1)S(1)} %get-tuple-element.27), channel_id=1, source_target_pairs={{0,8},{1,9},{2,10},{3,11},{4,12},{5,13},{6,14},{7,15},{8,0},{9,1},... | collective-permute-start | bytes 153608 | tf_op jit(solution)/shard_map/ppermute | solution.py:145
  19.9 2.0 %collective-permute-start.8 = (bf16[8,3200]{1,0:T(8,128)(2,1)S(1)}, bf16[8,3200]{1,0:T(8,128)(2,1)S(1)}, u32[]{:S(2)}, u32[]{:S(2)}) collective-permute-start(bf16[8,3200]{1,0:T(8,128)(2,1)S(1)} %get-tuple-element.28), channel_id=1, source_target_pairs={{0,12},{1,13},{2,14},{3,15},{4,8},{5,9},{6,10},{7,11},{8,4},{9,5},... | collective-permute-start | bytes 153608 | tf_op jit(solution)/shard_map/ppermute | solution.py:145
  21.9 0.3 %collective-permute-done.6.refs_1_ = bf16[8,3200]{1,0:T(8,128)(2,1)S(1)} collective-permute-done((bf16[8,3200]{1,0:T(8,128)(2,1)S(1)}, bf16[8,3200]{1,0:T(8,128)(2,1)S(1)}, u32[]{:S(2)}, u32[]{:S(2)}) %collective-permute-start.6) | collective-permute-done | bytes 51232 | tf_op jit(solution)/shard_map/ppermute | solution.py:145
  22.1 1.4 %collective-permute-done.7.refs_2_ = bf16[8,3200]{1,0:T(8,128)(2,1)S(1)} collective-permute-done((bf16[8,3200]{1,0:T(8,128)(2,1)S(1)}, bf16[8,3200]{1,0:T(8,128)(2,1)S(1)}, u32[]{:S(2)}, u32[]{:S(2)}) %collective-permute-start.7) | collective-permute-done | bytes 51232 | tf_op jit(solution)/shard_map/ppermute | solution.py:145
  23.5 2.3 %collective-permute-done.8.refs_3_ = bf16[8,3200]{1,0:T(8,128)(2,1)S(1)} collective-permute-done((bf16[8,3200]{1,0:T(8,128)(2,1)S(1)}, bf16[8,3200]{1,0:T(8,128)(2,1)S(1)}, u32[]{:S(2)}, u32[]{:S(2)}) %collective-permute-start.8) | collective-permute-done | bytes 51232 | tf_op jit(solution)/shard_map/ppermute | solution.py:145
  25.8 0.9 %shard_map.66 = bf16[8,3072]{1,0:T(8,128)(2,1)} custom-call(bf16[8,3200]{1,0:T(8,128)(2,1)S(1)} %get-tuple-element.25.refs_0_, bf16[8,3200]{1,0:T(8,128)(2,1)S(1)} %collective-permute-done.6.refs_1_, bf16[8,3200]{1,0:T(8,128)(2,1)S(1)} %collective-permute-done.7.refs_2_, bf16[8,3200]{1,0:T(8,128)(2,1)S(1)} %collective-permute-done.8.refs_3_), custom_call_target="tpu_custom_call" | custom-call | tf_op jit(solution)/shard_map/pallas_call | solution.py:195
Async XLA Ops:
  0.0 4.1 %copy-start = (bf16[8,3072]{1,0:T(8,128)(2,1)S(1)}, bf16[8,3072]{1,0:T(8,128)(2,1)}, u32[]{:S(2)}) copy-start(bf16[8,3072]{1,0:T(8,128)(2,1)} %queries.1) | copy-start | bytes 147460
  1.1 12.6 %collective-permute-start = (bf16[144,1024]{1,0:T(8,128)(2,1)S(1)}, bf16[144,1024]{1,0:T(8,128)(2,1)S(1)}, u32[]{:S(2)}, u32[]{:S(2)}) collective-permute-start(bf16[144,1024]{1,0:T(8,128)(2,1)S(1)} %get-tuple-element.17.refs_4_), channel_id=1, source_target_pairs={{0,2},{1,3},{2,0},{3,1},{4,6},{5,7},{6,4},{7,5},{8,10},{9,11},{10,... | collective-permute-start | bytes 884744 | tf_op jit(solution)/shard_map/ppermute | solution.py:145
  4.1 4.2 %collective-permute-start.1 = (bf16[8,3072]{1,0:T(8,128)(2,1)S(1)}, bf16[8,3072]{1,0:T(8,128)(2,1)S(1)}, u32[]{:S(2)}, u32[]{:S(2)}) collective-permute-start(bf16[8,3072]{1,0:T(8,128)(2,1)S(1)} %copy-done), channel_id=1, source_target_pairs={{0,4},{1,5},{2,6},{3,7},{4,0},{5,1},{6,2},{7,3},{8,12},{9,13},{10,... | collective-permute-start | bytes 147464 | tf_op jit(solution)/shard_map/ppermute | solution.py:145
  5.7 6.2 %collective-permute-start.3 = (bf16[8,3072]{1,0:T(8,128)(2,1)S(1)}, bf16[8,3072]{1,0:T(8,128)(2,1)S(1)}, u32[]{:S(2)}, u32[]{:S(2)}) collective-permute-start(bf16[8,3072]{1,0:T(8,128)(2,1)S(1)} %copy-done), channel_id=1, source_target_pairs={{0,12},{1,13},{2,14},{3,15},{4,8},{5,9},{6,10},{7,11},{8,4},{9,5},... | collective-permute-start | bytes 147464 | tf_op jit(solution)/shard_map/ppermute | solution.py:145
  8.1 5.5 %collective-permute-start.2 = (bf16[8,3072]{1,0:T(8,128)(2,1)S(1)}, bf16[8,3072]{1,0:T(8,128)(2,1)S(1)}, u32[]{:S(2)}, u32[]{:S(2)}) collective-permute-start(bf16[8,3072]{1,0:T(8,128)(2,1)S(1)} %copy-done), channel_id=1, source_target_pairs={{0,8},{1,9},{2,10},{3,11},{4,12},{5,13},{6,14},{7,15},{8,0},{9,1},... | collective-permute-start | bytes 147464 | tf_op jit(solution)/shard_map/ppermute | solution.py:145
  8.3 5.4 %collective-permute-start.4 = (bf16[144,1024]{1,0:T(8,128)(2,1)S(1)}, bf16[144,1024]{1,0:T(8,128)(2,1)S(1)}, u32[]{:S(2)}, u32[]{:S(2)}) collective-permute-start(bf16[144,1024]{1,0:T(8,128)(2,1)S(1)} %get-tuple-element.17.refs_4_), channel_id=1, source_target_pairs={{0,1},{1,0},{2,3},{3,2},{4,5},{5,4},{6,7},{7,6},{8,9},{9,8},{10,11... | collective-permute-start | bytes 884744 | tf_op jit(solution)/shard_map/ppermute | solution.py:145
  13.7 1.6 %collective-permute-start.5 = (bf16[144,1024]{1,0:T(8,128)(2,1)S(1)}, bf16[144,1024]{1,0:T(8,128)(2,1)S(1)}, u32[]{:S(2)}, u32[]{:S(2)}) collective-permute-start(bf16[144,1024]{1,0:T(8,128)(2,1)S(1)} %collective-permute-done.refs_6_), channel_id=1, source_target_pairs={{0,1},{1,0},{2,3},{3,2},{4,5},{5,4},{6,7},{7,6},{8,9},{9,8},{10,11... | collective-permute-start | bytes 884744 | tf_op jit(solution)/shard_map/ppermute | solution.py:145
  17.4 4.7 %collective-permute-start.6 = (bf16[8,3200]{1,0:T(8,128)(2,1)S(1)}, bf16[8,3200]{1,0:T(8,128)(2,1)S(1)}, u32[]{:S(2)}, u32[]{:S(2)}) collective-permute-start(bf16[8,3200]{1,0:T(8,128)(2,1)S(1)} %get-tuple-element.26), channel_id=1, source_target_pairs={{0,4},{1,5},{2,6},{3,7},{4,0},{5,1},{6,2},{7,3},{8,12},{9,13},{10,... | collective-permute-start | bytes 153608 | tf_op jit(solution)/shard_map/ppermute | solution.py:145
  17.7 5.8 %collective-permute-start.7 = (bf16[8,3200]{1,0:T(8,128)(2,1)S(1)}, bf16[8,3200]{1,0:T(8,128)(2,1)S(1)}, u32[]{:S(2)}, u32[]{:S(2)}) collective-permute-start(bf16[8,3200]{1,0:T(8,128)(2,1)S(1)} %get-tuple-element.27), channel_id=1, source_target_pairs={{0,8},{1,9},{2,10},{3,11},{4,12},{5,13},{6,14},{7,15},{8,0},{9,1},... | collective-permute-start | bytes 153608 | tf_op jit(solution)/shard_map/ppermute | solution.py:145
  19.9 5.9 %collective-permute-start.8 = (bf16[8,3200]{1,0:T(8,128)(2,1)S(1)}, bf16[8,3200]{1,0:T(8,128)(2,1)S(1)}, u32[]{:S(2)}, u32[]{:S(2)}) collective-permute-start(bf16[8,3200]{1,0:T(8,128)(2,1)S(1)} %get-tuple-element.28), channel_id=1, source_target_pairs={{0,12},{1,13},{2,14},{3,15},{4,8},{5,9},{6,10},{7,11},{8,4},{9,5},... | collective-permute-start | bytes 153608 | tf_op jit(solution)/shard_map/ppermute | solution.py:145

commit v3 on v2

v3 whole, which is shorter than its diff:
```python
import functools

import jax
import jax.numpy as jnp
from jax import lax
from jax.experimental import pallas as pl
from jax.experimental.pallas import tpu as pltpu
from jax.sharding import PartitionSpec as P

QUERY_HEADS = 24
KV_HEADS = 8
HEAD_DIM = 128
TREE_DEPTH = 4
GROUPS = QUERY_HEADS // KV_HEADS
WIDTH = QUERY_HEADS * HEAD_DIM
LANES = 128
STRIDE = 32
NT = (((1,), (1,)), ((), ()))


def prepare_kernel(
    queries, prefix_keys, prefix_values, tree_keys, tree_values,
    own_queries, own, tree_scratch, sems,
):
    slab = prefix_keys.shape[0]
    copies = [
        pltpu.make_async_copy(tree_keys, tree_scratch.at[0], sems.at[0]),
        pltpu.make_async_copy(tree_values, tree_scratch.at[1], sems.at[1]),
        pltpu.make_async_copy(prefix_keys, own.at[:slab], sems.at[2]),
        pltpu.make_async_copy(prefix_values, own.at[slab : 2 * slab], sems.at[3]),
        pltpu.make_async_copy(queries, own_queries, sems.at[4]),
    ]
    for copy in copies:
        copy.start()
    for copy in copies:
        copy.wait()
    both = jnp.concatenate(
        [tree_scratch[0].astype(jnp.float32), tree_scratch[1].astype(jnp.float32)], axis=0
    ).astype(own.dtype)
    own[2 * slab :] = both


def mask_kernel(near, local_rows, parents, bias):
    position = lax.axis_index("rows")
    rows, tokens = bias.shape
    slot = lax.broadcasted_iota(jnp.int32, (rows, 1), 0)
    walker = (position ^ (slot // local_rows * near)) * local_rows + slot % local_rows
    slot = lax.broadcasted_iota(jnp.int32, (1, tokens), 1)
    token = (position ^ (slot // local_rows)) * local_rows + slot % local_rows
    columns = lax.broadcasted_iota(jnp.int32, (rows, parents.shape[1]), 1)
    parent = parents[...]
    allowed = walker == token
    for _ in range(TREE_DEPTH - 1):
        walker = jnp.sum(jnp.where(walker == columns, parent, 0), axis=1, keepdims=True)
        allowed = allowed | (walker == token)
    bias[...] = jnp.where(allowed, 0.0, -jnp.inf)


def attend_kernel(owners, *refs):
    queries, outs = refs[:owners], refs[-owners:]
    blocks, bias_ref = refs[owners : -owners - 1], refs[-owners - 1]
    local_rows = queries[0].shape[0]
    rows = owners * local_rows
    slab = (blocks[0].shape[0] - 2 * local_rows) // 2
    key_parts = [ref.at[:slab] for ref in blocks]
    value_parts = [ref.at[slab : 2 * slab] for ref in blocks]
    tree_parts = [ref.at[2 * slab :] for ref in blocks]

    bias = jnp.concatenate([bias_ref[...]] * GROUPS, axis=0)
    every_query = jnp.concatenate([ref[...].astype(jnp.float32) for ref in queries], axis=0).astype(jnp.bfloat16)
    trees = [ref[...].astype(jnp.float32) for ref in tree_parts]
    tree_keys = jnp.concatenate([tree[:local_rows] for tree in trees], axis=0).astype(jnp.bfloat16)
    tree_values = jnp.concatenate([tree[local_rows:] for tree in trees], axis=0).astype(jnp.bfloat16)
    heads = [slice(head * HEAD_DIM, (head + 1) * HEAD_DIM) for head in range(QUERY_HEADS)]
    scores = []
    for head in range(KV_HEADS):
        query = jnp.concatenate([every_query[:, heads[head * GROUPS + g]] for g in range(GROUPS)], axis=0)
        keys = jnp.concatenate([ref[:, heads[head]] for ref in key_parts], axis=0)
        slab_scores = lax.dot_general(query, keys, NT, preferred_element_type=jnp.float32)
        tree_scores = lax.dot_general(query, tree_keys[:, heads[head]], NT, preferred_element_type=jnp.float32)
        scores.append((slab_scores * HEAD_DIM ** (-0.5), tree_scores * HEAD_DIM ** (-0.5) + bias))
    weights = []
    for slab_scores, tree_scores in scores:
        maxima = jnp.maximum(
            jnp.max(slab_scores, axis=1, keepdims=True), jnp.max(tree_scores, axis=1, keepdims=True)
        )
        slab_weights = jnp.exp(slab_scores - maxima)
        tree_weights = jnp.exp(tree_scores - maxima)
        masses = jnp.sum(slab_weights, axis=1, keepdims=True) + jnp.sum(tree_weights, axis=1, keepdims=True)
        weights.append(
            (slab_weights.astype(jnp.bfloat16), tree_weights.astype(jnp.bfloat16), masses, maxima + jnp.log(masses))
        )
    lane = lax.broadcasted_iota(jnp.int32, (rows, LANES), 1)
    stats = jnp.zeros((rows, LANES), jnp.float32)
    for head, (slab_weights, tree_weights, masses, level) in enumerate(weights):
        values = jnp.concatenate([ref[:, heads[head]] for ref in value_parts], axis=0)
        weighted = jnp.dot(slab_weights, values, preferred_element_type=jnp.float32) + jnp.dot(
            tree_weights, tree_values[:, heads[head]], preferred_element_type=jnp.float32
        )
        weighted = weighted * (1.0 / masses)
        for g in range(GROUPS):
            query_head = head * GROUPS + g
            here = (lane % STRIDE == query_head) & (lane < 3 * STRIDE)
            stats = jnp.where(here, level[g * rows : (g + 1) * rows], stats)
            for owner in range(owners):
                first = g * rows + owner * local_rows
                outs[owner][:, heads[query_head]] = weighted[first : first + local_rows].astype(jnp.bfloat16)
    high = stats.astype(jnp.bfloat16).astype(jnp.float32)
    left = stats - high
    middle = left.astype(jnp.bfloat16).astype(jnp.float32)
    low = left - middle
    sent = jnp.where(lane < STRIDE, high, jnp.where(lane < 2 * STRIDE, middle, low))
    for owner in range(owners):
        outs[owner][:, WIDTH:] = sent[owner * local_rows : (owner + 1) * local_rows].astype(jnp.bfloat16)


def merge_kernel(*refs):
    parts, out = refs[:-1], refs[-1]
    levels = []
    for part in parts:
        terms = part[:, WIDTH:].astype(jnp.float32)
        levels.append(
            terms[:, :STRIDE] + terms[:, STRIDE : 2 * STRIDE] + terms[:, 2 * STRIDE : 3 * STRIDE]
        )
    top = functools.reduce(jnp.maximum, levels)
    shares = [jnp.exp(level - top) for level in levels]
    whole = 1.0 / functools.reduce(jnp.add, shares)
    shares = [share * whole for share in shares]
    for head in range(QUERY_HEADS):
        wide = slice(head * HEAD_DIM, (head + 1) * HEAD_DIM)
        total = functools.reduce(
            jnp.add,
            [
                share[:, head : head + 1] * part[:, wide].astype(jnp.float32)
                for share, part in zip(shares, parts)
            ],
        )
        out[:, wide] = total.astype(out.dtype)


def held(memory, arrays):
    return [pltpu.with_memory_space_constraint(x, memory) for x in arrays]


def swap(x, offset):
    return lax.ppermute(x, "rows", [(i, i ^ offset) for i in range(lax.axis_size("rows"))])


def after(x, *earlier):
    return lax.optimization_barrier((x, *earlier))


def shards(queries, prefix_keys, prefix_values, tree_keys, tree_values, parents):
    size = lax.axis_size("rows")
    bits = size.bit_length() - 1
    near_bits = (bits + 1) // 2
    near = 2**near_bits
    far = size // near
    local_rows = queries.shape[0]
    slab, row_width = prefix_keys.shape
    far_offsets = [near * i for i in range(far)]
    far_order = far_offsets[-1:] + far_offsets[1:-1]
    vmem = pl.BlockSpec(memory_space=pltpu.VMEM)
    hbm = pl.BlockSpec(memory_space=pltpu.HBM)
    params = pltpu.CompilerParams(vmem_limit_bytes=16 * 2**20)
    own_queries, own = pl.pallas_call(
        prepare_kernel,
        out_shape=[
            pltpu.VMEM(queries.shape, queries.dtype),
            pltpu.VMEM((2 * (slab + local_rows), row_width), prefix_keys.dtype),
        ],
        in_specs=[hbm] * 5,
        out_specs=[vmem] * 2,
        scratch_shapes=[
            pltpu.VMEM((2,) + tree_keys.shape, tree_keys.dtype),
            pltpu.SemaphoreType.DMA((5,)),
        ],
        compiler_params=params,
    )(*held(pltpu.HBM, [queries, prefix_keys, prefix_values, tree_keys, tree_values]))
    bias = pl.pallas_call(
        functools.partial(mask_kernel, near, local_rows),
        out_shape=pltpu.VMEM((far * local_rows, near * local_rows), jnp.float32),
        in_specs=[vmem],
        out_specs=vmem,
        compiler_params=params,
    )(parents[None, :])

    all_queries = {0: own_queries}
    for offset in far_order:
        all_queries[offset] = swap(queries, offset)
    pieces = {0: own}
    for bit in reversed(range(near_bits)):
        for offset in list(pieces):
            piece = pieces[offset]
            if bit == 0 and offset:
                piece, *waited = after(piece, *all_queries.values())
                all_queries = dict(zip(all_queries, waited))
            pieces[offset ^ (1 << bit)] = swap(piece, 1 << bit)
    operands = (
        [all_queries[offset] for offset in far_offsets] + [pieces[offset] for offset in range(near)] + [bias]
    )
    partials = pl.pallas_call(
        functools.partial(attend_kernel, far),
        out_shape=[pltpu.VMEM((local_rows, WIDTH + LANES), jnp.bfloat16)] * far,
        in_specs=[vmem] * len(operands),
        out_specs=[vmem] * far,
        compiler_params=params,
    )(*held(pltpu.VMEM, operands))
    parts = [partials[0]]
    for offset in far_order:
        parts.append(swap(partials[far_offsets.index(offset)], offset))
    return pl.pallas_call(
        merge_kernel,
        out_shape=jax.ShapeDtypeStruct((local_rows, WIDTH), jnp.bfloat16),
        in_specs=[vmem] * far,
        out_specs=vmem,
        compiler_params=params,
    )(*held(pltpu.VMEM, parts))


def solution(mesh):
    placed = (
        P(("group", "rows"), None),
        P(("group", "rows"), None),
        P(("group", "rows"), None),
        P(("group", "rows"), None),
        P(("group", "rows"), None),
        P("group"),
    )
    return jax.shard_map(
        shards, mesh=mesh, in_specs=placed, out_specs=P(("group", "rows"), None), check_vma=False
    )
```

time: 26.9 us -> 24.1 us (0.90)
  waiting for transfers between devices: 10.9 us -> 8.35 us
  Pallas kernels: 4.13 us -> 2.99 us
  local copies, waits for them, and re-layouts: 0.01 us -> 0.58 us
    ppermute x9, waiting for transfers between devices: 10.9 us -> 8.35 us  [swap(): lax.ppermute(x, 'rows', [(i, i ^ offset) for i in range(lax.axis_size('ro...]
    pallas_call x2 -> x3, Pallas kernels: 3.2 us -> 2.06 us  [the longest x1 1.05 us: shards(): pl.pallas_call(prepare_kernel, out_shape=[pltpu.VMEM(queries.shape, queri...]
    unnamed x2 -> x4, local copies, waits for them, and re-layouts: 0.01 us -> 0.58 us
    ppermute x9, starting transfers between devices: 11.7 us -> 11.9 us  [swap(): lax.ppermute(x, 'rows', [(i, i ^ offset) for i in range(lax.axis_size('ro...]
  transfers between devices with their start and end apart: 9 -> 9, of which waited for: 6 -> 6; matrix products, arithmetic and copies ran while one was open for 0% -> 0% of each run, Pallas kernels for 0% -> 1%
where the time goes in v3:
time: 24.1 us; the launch traced here: 23.9 us
  starting transfers between devices  11.9 us (49%)
  waiting for transfers between devices  8.35 us (35%)
  Pallas kernels  2.99 us (12%)
  local copies, waits for them, and re-layouts  0.58 us (2%)
    ppermute x9, starting transfers between devices, swap(): lax.ppermute(x, 'rows', [(i, i ^ offset) for i in range(lax.axis_size('ro...  11.9 us
    ppermute x9, waiting for transfers between devices, swap(): lax.ppermute(x, 'rows', [(i, i ^ offset) for i in range(lax.axis_size('ro...  8.35 us
    pallas_call x1, Pallas kernels, shards(): pl.pallas_call(prepare_kernel, out_shape=[pltpu.VMEM(queries.shape, queri...  1.05 us
    pallas_call x1, Pallas kernels, shards(): pl.pallas_call(merge_kernel, out_shape=jax.ShapeDtypeStruct((local_rows,...  0.93 us
    pallas_call x1, Pallas kernels, shards(): pl.pallas_call(functools.partial(attend_kernel, far), out_shape=[pltpu.VM...  0.75 us
    unnamed x4, local copies, waits for them, and re-layouts  0.58 us
  transfers between devices with their start and end apart: 9, of which 6 were waited for; matrix products, arithmetic and copies ran while one was open for 0% of the time, Pallas kernels for 1%

profile of v3, /device:TPU:0, one launch (start us, length us, event | category | flops | bytes accessed | tf_op | source)
XLA Modules:
  0.0 23.9 jit_solution(13119453507561171132)
XLA Ops:
  0.0 0.0 copy-start.1
  0.0 1.0 %shard_map.64 = (bf16[8,3072]{1,0:T(8,128)(2,1)S(1)}, bf16[144,1024]{1,0:T(8,128)(2,1)S(1)}) custom-call(bf16[8,3072]{1,0:T(8,128)(2,1)} %queries.1, bf16[64,1024]{1,0:T(8,128)(2,1)} %prefix_keys.1, bf16[64,1024]{1,0:T(8,128)(2,1)} %prefix_values.1, bf16[8,1024]{1,0:T(8,128)(2,1)} %tree_keys.1, bf16[8,1024]{1,0:T(8,128)(2,1)} %tree_values.1), custom_call_target="tpu_custom_call" | custom-call | tf_op jit(solution)/shard_map/pallas_call | solution.py:166
  1.1 3.0 %collective-permute-start = (bf16[144,1024]{1,0:T(8,128)(2,1)S(1)}, bf16[144,1024]{1,0:T(8,128)(2,1)S(1)}, u32[]{:S(2)}, u32[]{:S(2)}) collective-permute-start(bf16[144,1024]{1,0:T(8,128)(2,1)S(1)} %get-tuple-element.16.refs_4_), channel_id=1, source_target_pairs={{0,2},{1,3},{2,0},{3,1},{4,6},{5,7},{6,4},{7,5},{8,10},{9,11},{10,... | collective-permute-start | bytes 884744 | tf_op jit(solution)/shard_map/ppermute | solution.py:146
  4.1 0.0 copy-done.1
  4.1 3.6 %collective-permute-start.1 = (bf16[8,3072]{1,0:T(8,128)(2,1)S(1)}, bf16[8,3072]{1,0:T(8,128)(2,1)S(1)}, u32[]{:S(2)}, u32[]{:S(2)}) collective-permute-start(bf16[8,3072]{1,0:T(8,128)(2,1)S(1)} %copy-done.1), channel_id=1, source_target_pairs={{0,12},{1,13},{2,14},{3,15},{4,8},{5,9},{6,10},{7,11},{8,4},{9,5},... | collective-permute-start | bytes 147464 | tf_op jit(solution)/shard_map/ppermute | solution.py:146
  7.7 0.0 collective-permute-start.3
  7.7 0.8 %collective-permute-start.2 = (bf16[8,3072]{1,0:T(8,128)(2,1)S(1)}, bf16[8,3072]{1,0:T(8,128)(2,1)S(1)}, u32[]{:S(2)}, u32[]{:S(2)}) collective-permute-start(bf16[8,3072]{1,0:T(8,128)(2,1)S(1)} %copy-done.1), channel_id=1, source_target_pairs={{0,4},{1,5},{2,6},{3,7},{4,0},{5,1},{6,2},{7,3},{8,12},{9,13},{10,... | collective-permute-start | bytes 147464 | tf_op jit(solution)/shard_map/ppermute | solution.py:146
  8.5 0.0 collective-permute-start.4
  8.5 2.0 %collective-permute-done.1.refs_3_ = bf16[8,3072]{1,0:T(8,128)(2,1)S(1)} collective-permute-done((bf16[8,3072]{1,0:T(8,128)(2,1)S(1)}, bf16[8,3072]{1,0:T(8,128)(2,1)S(1)}, u32[]{:S(2)}, u32[]{:S(2)}) %collective-permute-start.1) | collective-permute-done | bytes 49184 | tf_op jit(solution)/shard_map/ppermute | solution.py:146
  10.5 2.2 %collective-permute-done.3.refs_2_ = bf16[8,3072]{1,0:T(8,128)(2,1)S(1)} collective-permute-done((bf16[8,3072]{1,0:T(8,128)(2,1)S(1)}, bf16[8,3072]{1,0:T(8,128)(2,1)S(1)}, u32[]{:S(2)}, u32[]{:S(2)}) %collective-permute-start.3) | collective-permute-done | bytes 49184 | tf_op jit(solution)/shard_map/ppermute | solution.py:146
  12.7 0.0 collective-permute-done.2.refs_1_
  12.7 0.0 collective-permute-done.refs_6_
  12.7 0.0 copy-start
  12.7 0.1 collective-permute-start.5
  12.8 0.6 %copy-done = s32[128]{0:T(128)S(1)} copy-done((s32[128]{0:T(128)S(1)}, s32[128]{0:T(128)}, u32[]{:S(2)}) %copy-start) | copy-done | bytes 536
  13.4 0.3 %shard_map.65.refs_8_ = f32[32,32]{1,0:T(8,128)S(1)} custom-call(s32[1,128]{1,0:T(1,128)S(1)} %bitcast.1), custom_call_target="tpu_custom_call" | custom-call | tf_op jit(solution)/shard_map/pallas_call | solution.py:180
  13.6 0.0 collective-permute-done.4.refs_5_
  13.6 0.7 %collective-permute-done.5.refs_7_ = bf16[144,1024]{1,0:T(8,128)(2,1)S(1)} collective-permute-done((bf16[144,1024]{1,0:T(8,128)(2,1)S(1)}, bf16[144,1024]{1,0:T(8,128)(2,1)S(1)}, u32[]{:S(2)}, u32[]{:S(2)}) %collective-permute-start.5) | collective-permute-done | bytes 294944 | tf_op jit(solution)/shard_map/ppermute | solution.py:146
  14.3 0.7 %shard_map.66 = (bf16[8,3200]{1,0:T(8,128)(2,1)S(1)}, bf16[8,3200]{1,0:T(8,128)(2,1)S(1)}, bf16[8,3200]{1,0:T(8,128)(2,1)S(1)}, bf16[8,3200]{1,0:T(8,128)(2,1)S(1)}) custom-call(bf16[8,3072]{1,0:T(8,128)(2,1)S(1)} %get-tuple-element.18.refs_0_, bf16[8,3072]{1,0:T(8,128)(2,1)S(1)} %collective-permute-done.2.refs_1_, ...), custom_call_target="tpu_custom_call" | custom-call | tf_op jit(solution)/shard_map/pallas_call | solution.py:202
  15.1 2.2 %collective-permute-start.6 = (bf16[8,3200]{1,0:T(8,128)(2,1)S(1)}, bf16[8,3200]{1,0:T(8,128)(2,1)S(1)}, u32[]{:S(2)}, u32[]{:S(2)}) collective-permute-start(bf16[8,3200]{1,0:T(8,128)(2,1)S(1)} %get-tuple-element.24), channel_id=1, source_target_pairs={{0,12},{1,13},{2,14},{3,15},{4,8},{5,9},{6,10},{7,11},{8,4},{9,5},... | collective-permute-start | bytes 153608 | tf_op jit(solution)/shard_map/ppermute | solution.py:146
  17.3 0.4 %collective-permute-start.7 = (bf16[8,3200]{1,0:T(8,128)(2,1)S(1)}, bf16[8,3200]{1,0:T(8,128)(2,1)S(1)}, u32[]{:S(2)}, u32[]{:S(2)}) collective-permute-start(bf16[8,3200]{1,0:T(8,128)(2,1)S(1)} %get-tuple-element.25), channel_id=1, source_target_pairs={{0,4},{1,5},{2,6},{3,7},{4,0},{5,1},{6,2},{7,3},{8,12},{9,13},{10,... | collective-permute-start | bytes 153608 | tf_op jit(solution)/shard_map/ppermute | solution.py:146
  17.7 1.9 %collective-permute-start.8 = (bf16[8,3200]{1,0:T(8,128)(2,1)S(1)}, bf16[8,3200]{1,0:T(8,128)(2,1)S(1)}, u32[]{:S(2)}, u32[]{:S(2)}) collective-permute-start(bf16[8,3200]{1,0:T(8,128)(2,1)S(1)} %get-tuple-element.26), channel_id=1, source_target_pairs={{0,8},{1,9},{2,10},{3,11},{4,12},{5,13},{6,14},{7,15},{8,0},{9,1},... | collective-permute-start | bytes 153608 | tf_op jit(solution)/shard_map/ppermute | solution.py:146
  19.6 1.9 %collective-permute-done.6.refs_1_ = bf16[8,3200]{1,0:T(8,128)(2,1)S(1)} collective-permute-done((bf16[8,3200]{1,0:T(8,128)(2,1)S(1)}, bf16[8,3200]{1,0:T(8,128)(2,1)S(1)}, u32[]{:S(2)}, u32[]{:S(2)}) %collective-permute-start.6) | collective-permute-done | bytes 51232 | tf_op jit(solution)/shard_map/ppermute | solution.py:146
  21.5 1.0 %collective-permute-done.7.refs_2_ = bf16[8,3200]{1,0:T(8,128)(2,1)S(1)} collective-permute-done((bf16[8,3200]{1,0:T(8,128)(2,1)S(1)}, bf16[8,3200]{1,0:T(8,128)(2,1)S(1)}, u32[]{:S(2)}, u32[]{:S(2)}) %collective-permute-start.7) | collective-permute-done | bytes 51232 | tf_op jit(solution)/shard_map/ppermute | solution.py:146
  22.5 0.5 %collective-permute-done.8.refs_3_ = bf16[8,3200]{1,0:T(8,128)(2,1)S(1)} collective-permute-done((bf16[8,3200]{1,0:T(8,128)(2,1)S(1)}, bf16[8,3200]{1,0:T(8,128)(2,1)S(1)}, u32[]{:S(2)}, u32[]{:S(2)}) %collective-permute-start.8) | collective-permute-done | bytes 51232 | tf_op jit(solution)/shard_map/ppermute | solution.py:146
  23.0 0.9 %shard_map.67 = bf16[8,3072]{1,0:T(8,128)(2,1)} custom-call(bf16[8,3200]{1,0:T(8,128)(2,1)S(1)} %get-tuple-element.23.refs_0_, bf16[8,3200]{1,0:T(8,128)(2,1)S(1)} %collective-permute-done.6.refs_1_, bf16[8,3200]{1,0:T(8,128)(2,1)S(1)} %collective-permute-done.7.refs_2_, bf16[8,3200]{1,0:T(8,128)(2,1)S(1)} %collective-permute-done.8.refs_3_), custom_call_target="tpu_custom_call" | custom-call | tf_op jit(solution)/shard_map/pallas_call | solution.py:212
Async XLA Ops:
  0.0 4.1 %copy-start.1 = (bf16[8,3072]{1,0:T(8,128)(2,1)S(1)}, bf16[8,3072]{1,0:T(8,128)(2,1)}, u32[]{:S(2)}) copy-start(bf16[8,3072]{1,0:T(8,128)(2,1)} %queries.1) | copy-start | bytes 147460
  1.1 11.6 %collective-permute-start = (bf16[144,1024]{1,0:T(8,128)(2,1)S(1)}, bf16[144,1024]{1,0:T(8,128)(2,1)S(1)}, u32[]{:S(2)}, u32[]{:S(2)}) collective-permute-start(bf16[144,1024]{1,0:T(8,128)(2,1)S(1)} %get-tuple-element.16.refs_4_), channel_id=1, source_target_pairs={{0,2},{1,3},{2,0},{3,1},{4,6},{5,7},{6,4},{7,5},{8,10},{9,11},{10,... | collective-permute-start | bytes 884744 | tf_op jit(solution)/shard_map/ppermute | solution.py:146
  4.1 6.4 %collective-permute-start.1 = (bf16[8,3072]{1,0:T(8,128)(2,1)S(1)}, bf16[8,3072]{1,0:T(8,128)(2,1)S(1)}, u32[]{:S(2)}, u32[]{:S(2)}) collective-permute-start(bf16[8,3072]{1,0:T(8,128)(2,1)S(1)} %copy-done.1), channel_id=1, source_target_pairs={{0,12},{1,13},{2,14},{3,15},{4,8},{5,9},{6,10},{7,11},{8,4},{9,5},... | collective-permute-start | bytes 147464 | tf_op jit(solution)/shard_map/ppermute | solution.py:146
  7.7 5.0 %collective-permute-start.3 = (bf16[8,3072]{1,0:T(8,128)(2,1)S(1)}, bf16[8,3072]{1,0:T(8,128)(2,1)S(1)}, u32[]{:S(2)}, u32[]{:S(2)}) collective-permute-start(bf16[8,3072]{1,0:T(8,128)(2,1)S(1)} %copy-done.1), channel_id=1, source_target_pairs={{0,8},{1,9},{2,10},{3,11},{4,12},{5,13},{6,14},{7,15},{8,0},{9,1},... | collective-permute-start | bytes 147464 | tf_op jit(solution)/shard_map/ppermute | solution.py:146
  7.7 5.0 %collective-permute-start.2 = (bf16[8,3072]{1,0:T(8,128)(2,1)S(1)}, bf16[8,3072]{1,0:T(8,128)(2,1)S(1)}, u32[]{:S(2)}, u32[]{:S(2)}) collective-permute-start(bf16[8,3072]{1,0:T(8,128)(2,1)S(1)} %copy-done.1), channel_id=1, source_target_pairs={{0,4},{1,5},{2,6},{3,7},{4,0},{5,1},{6,2},{7,3},{8,12},{9,13},{10,... | collective-permute-start | bytes 147464 | tf_op jit(solution)/shard_map/ppermute | solution.py:146
  8.5 5.1 %collective-permute-start.4 = (bf16[144,1024]{1,0:T(8,128)(2,1)S(1)}, bf16[144,1024]{1,0:T(8,128)(2,1)S(1)}, u32[]{:S(2)}, u32[]{:S(2)}) collective-permute-start(bf16[144,1024]{1,0:T(8,128)(2,1)S(1)} %get-tuple-element.16.refs_4_), channel_id=1, source_target_pairs={{0,1},{1,0},{2,3},{3,2},{4,5},{5,4},{6,7},{7,6},{8,9},{9,8},{10,11... | collective-permute-start | bytes 884744 | tf_op jit(solution)/shard_map/ppermute | solution.py:146
  12.7 0.7 %copy-start = (s32[128]{0:T(128)S(1)}, s32[128]{0:T(128)}, u32[]{:S(2)}) copy-start(s32[128]{0:T(128)} %param.11) | copy-start | bytes 1540
  12.7 1.6 %collective-permute-start.5 = (bf16[144,1024]{1,0:T(8,128)(2,1)S(1)}, bf16[144,1024]{1,0:T(8,128)(2,1)S(1)}, u32[]{:S(2)}, u32[]{:S(2)}) collective-permute-start(bf16[144,1024]{1,0:T(8,128)(2,1)S(1)} %collective-permute-done.refs_6_), channel_id=1, source_target_pairs={{0,1},{1,0},{2,3},{3,2},{4,5},{5,4},{6,7},{7,6},{8,9},{9,8},{10,11... | collective-permute-start | bytes 884744 | tf_op jit(solution)/shard_map/ppermute | solution.py:146
  15.1 6.4 %collective-permute-start.6 = (bf16[8,3200]{1,0:T(8,128)(2,1)S(1)}, bf16[8,3200]{1,0:T(8,128)(2,1)S(1)}, u32[]{:S(2)}, u32[]{:S(2)}) collective-permute-start(bf16[8,3200]{1,0:T(8,128)(2,1)S(1)} %get-tuple-element.24), channel_id=1, source_target_pairs={{0,12},{1,13},{2,14},{3,15},{4,8},{5,9},{6,10},{7,11},{8,4},{9,5},... | collective-permute-start | bytes 153608 | tf_op jit(solution)/shard_map/ppermute | solution.py:146
  17.3 5.1 %collective-permute-start.7 = (bf16[8,3200]{1,0:T(8,128)(2,1)S(1)}, bf16[8,3200]{1,0:T(8,128)(2,1)S(1)}, u32[]{:S(2)}, u32[]{:S(2)}) collective-permute-start(bf16[8,3200]{1,0:T(8,128)(2,1)S(1)} %get-tuple-element.25), channel_id=1, source_target_pairs={{0,4},{1,5},{2,6},{3,7},{4,0},{5,1},{6,2},{7,3},{8,12},{9,13},{10,... | collective-permute-start | bytes 153608 | tf_op jit(solution)/shard_map/ppermute | solution.py:146
  17.7 5.3 %collective-permute-start.8 = (bf16[8,3200]{1,0:T(8,128)(2,1)S(1)}, bf16[8,3200]{1,0:T(8,128)(2,1)S(1)}, u32[]{:S(2)}, u32[]{:S(2)}) collective-permute-start(bf16[8,3200]{1,0:T(8,128)(2,1)S(1)} %get-tuple-element.26), channel_id=1, source_target_pairs={{0,8},{1,9},{2,10},{3,11},{4,12},{5,13},{6,14},{7,15},{8,0},{9,1},... | collective-permute-start | bytes 153608 | tf_op jit(solution)/shard_map/ppermute | solution.py:146

commit v4 on v3

v4 whole, which is shorter than its diff:
```python
import functools

import jax
import jax.numpy as jnp
from jax import lax
from jax.experimental import pallas as pl
from jax.experimental.pallas import tpu as pltpu
from jax.sharding import PartitionSpec as P

QUERY_HEADS = 24
KV_HEADS = 8
HEAD_DIM = 128
TREE_DEPTH = 4
GROUPS = QUERY_HEADS // KV_HEADS
WIDTH = QUERY_HEADS * HEAD_DIM
LANES = 128
STRIDE = 32
NT = (((1,), (1,)), ((), ()))
HEADS = [slice(head * HEAD_DIM, (head + 1) * HEAD_DIM) for head in range(QUERY_HEADS)]


def prepare_kernel(
    queries, prefix_keys, prefix_values, tree_keys, tree_values, own_queries, keys, rest, tree_scratch, sems
):
    slab = prefix_values.shape[0]
    copies = [
        pltpu.make_async_copy(tree_keys, tree_scratch.at[0], sems.at[0]),
        pltpu.make_async_copy(tree_values, tree_scratch.at[1], sems.at[1]),
        pltpu.make_async_copy(prefix_values, rest.at[:slab], sems.at[2]),
        pltpu.make_async_copy(prefix_keys, keys, sems.at[3]),
        pltpu.make_async_copy(queries, own_queries, sems.at[4]),
    ]
    for copy in copies:
        copy.start()
    for copy in copies:
        copy.wait()
    both = [tree_scratch[0].astype(jnp.float32), tree_scratch[1].astype(jnp.float32)]
    rest[slab:] = jnp.concatenate(both, axis=0).astype(rest.dtype)


def stack_kernel(*refs):
    blocks, out = refs[:-1], refs[-1]
    first = 0
    for block in blocks:
        out[first : first + block.shape[0]] = block[...]
        first += block.shape[0]


def chosen(index, values):
    picked = jnp.full(index.shape, values[0], jnp.int32)
    for place in range(1, len(values)):
        picked = jnp.where(index == place, values[place], picked)
    return picked


def mask_kernel(owner_offsets, token_offsets, local_rows, parents, bias):
    position = lax.axis_index("rows")
    rows, columns = bias.shape
    block = columns // len(token_offsets)
    slab = block - 2 * local_rows
    slot = lax.broadcasted_iota(jnp.int32, (rows, 1), 0)
    walker = (position ^ chosen(slot // local_rows, owner_offsets)) * local_rows + slot % local_rows
    slot = lax.broadcasted_iota(jnp.int32, (1, columns), 1)
    within = slot % block - slab
    token = (position ^ chosen(slot // block, token_offsets)) * local_rows + within
    is_tree = (within >= 0) & (within < local_rows)
    candidates = lax.broadcasted_iota(jnp.int32, (rows, parents.shape[1]), 1)
    parent = parents[...]
    allowed = walker == token
    for _ in range(TREE_DEPTH - 1):
        walker = jnp.sum(jnp.where(walker == candidates, parent, 0), axis=1, keepdims=True)
        allowed = allowed | (walker == token)
    bias[...] = jnp.where((allowed & is_tree) | (within < 0), 0.0, -jnp.inf)


def block_rows(parts, local_rows):
    keys, values = [], []
    for slab_keys, rest in parts:
        slab = slab_keys.shape[0]
        tree = rest[slab:]
        halves = tree.astype(jnp.float32)
        turned = jnp.concatenate([halves[local_rows:], halves[:local_rows]], axis=0)
        keys += [slab_keys[...], tree]
        values += [rest[:slab], turned.astype(jnp.bfloat16)]
    return keys, values


def bundle_parts(bundle, last_rest, count, slab, local_rows):
    block = slab + 2 * local_rows
    rests = [bundle.at[count * slab + i * block : count * slab + (i + 1) * block] for i in range(count - 1)]
    return [(bundle.at[i * slab : (i + 1) * slab], rest) for i, rest in enumerate(rests + [last_rest])]


def across(x, lanes):
    if x.shape[1] == 1:
        return x
    copies = -(-lanes // x.shape[1])
    return jnp.concatenate([x] * copies, axis=1)[:, :lanes]


def attend(queries, parts, bias, maxima_before):
    key_parts, value_parts = block_rows(parts, queries[0].shape[0])
    bias = jnp.concatenate([bias] * GROUPS, axis=0)
    every_query = jnp.concatenate([ref[...].astype(jnp.float32) for ref in queries], axis=0).astype(jnp.bfloat16)
    scores = []
    for head in range(KV_HEADS):
        query = jnp.concatenate([every_query[:, HEADS[head * GROUPS + g]] for g in range(GROUPS)], axis=0)
        keys = jnp.concatenate([part[:, HEADS[head]] for part in key_parts], axis=0)
        products = lax.dot_general(query, keys, NT, preferred_element_type=jnp.float32)
        scores.append(products * HEAD_DIM ** (-0.5) + bias)
    weights = []
    for head in range(KV_HEADS):
        maxima = jnp.max(scores[head], axis=1, keepdims=True)
        if maxima_before is not None:
            maxima = jnp.maximum(maxima, maxima_before[head])
        exps = jnp.exp(scores[head] - across(maxima, scores[head].shape[1]))
        weights.append((exps.astype(jnp.bfloat16), maxima, jnp.sum(exps, axis=1, keepdims=True)))
    for head, (rounded, maxima, masses) in enumerate(weights):
        values = jnp.concatenate([part[:, HEADS[head]] for part in value_parts], axis=0)
        yield head, maxima, masses, jnp.dot(rounded, values, preferred_element_type=jnp.float32)


def early_kernel(owners, count, slab, *refs):
    queries, refs, (maxima_out, masses_out, weighted_out) = refs[:owners], refs[owners:-3], refs[-3:]
    bundle, last_rest, bias_ref = refs
    parts = bundle_parts(bundle, last_rest, count, slab, queries[0].shape[0])
    for head, maxima, masses, weighted in attend(queries, parts, bias_ref[...], None):
        maxima_out[head] = jnp.broadcast_to(maxima, weighted.shape)
        masses_out[head] = jnp.broadcast_to(masses, weighted.shape)
        weighted_out[head] = weighted


def late_kernel(owners, count, slab, *refs):
    queries, outs, refs = refs[:owners], refs[-owners:], refs[owners:-owners]
    bundle, last_rest, bias_ref, maxima_in, masses_in, weighted_in = refs
    local_rows = queries[0].shape[0]
    parts = bundle_parts(bundle, last_rest, count, slab, local_rows)
    rows = owners * local_rows
    lane = lax.broadcasted_iota(jnp.int32, (rows, LANES), 1)
    stats = jnp.zeros((rows, LANES), jnp.float32)
    for head, maxima, masses, weighted in attend(queries, parts, bias_ref[...], maxima_in):
        shrink = jnp.exp(maxima_in[head] - maxima)
        masses = masses + masses_in[head] * shrink
        weighted = (weighted + weighted_in[head] * shrink) * (1.0 / masses)
        level = maxima + jnp.log(masses)
        for g in range(GROUPS):
            query_head = head * GROUPS + g
            here = (lane % STRIDE == query_head) & (lane < 3 * STRIDE)
            stats = jnp.where(here, level[g * rows : (g + 1) * rows], stats)
            for owner in range(owners):
                first = g * rows + owner * local_rows
                outs[owner][:, HEADS[query_head]] = weighted[first : first + local_rows].astype(jnp.bfloat16)
    high = stats.astype(jnp.bfloat16).astype(jnp.float32)
    left = stats - high
    middle = left.astype(jnp.bfloat16).astype(jnp.float32)
    low = left - middle
    sent = jnp.where(lane < STRIDE, high, jnp.where(lane < 2 * STRIDE, middle, low))
    for owner in range(owners):
        outs[owner][:, WIDTH:] = sent[owner * local_rows : (owner + 1) * local_rows].astype(jnp.bfloat16)


def merge_kernel(*refs):
    parts, out = refs[:-1], refs[-1]
    levels = []
    for part in parts:
        terms = part[:, WIDTH:].astype(jnp.float32)
        levels.append(terms + pltpu.roll(terms, LANES - STRIDE, 1) + pltpu.roll(terms, LANES - 2 * STRIDE, 1))
    top = functools.reduce(jnp.maximum, levels)
    shares = [jnp.exp(level - top) for level in levels]
    whole = 1.0 / functools.reduce(jnp.add, shares)
    shares = [share * whole for share in shares]
    for head in range(QUERY_HEADS):
        total = functools.reduce(
            jnp.add,
            [
                share[:, head : head + 1] * part[:, HEADS[head]].astype(jnp.float32)
                for share, part in zip(shares, parts)
            ],
        )
        out[:, HEADS[head]] = total.astype(out.dtype)


def held(memory, arrays):
    return [pltpu.with_memory_space_constraint(x, memory) for x in arrays]


def swap(x, offset):
    return lax.ppermute(x, "rows", [(i, i ^ offset) for i in range(lax.axis_size("rows"))])


def after(x, *earlier):
    return lax.optimization_barrier((x, *earlier))


def shards(queries, prefix_keys, prefix_values, tree_keys, tree_values, parents):
    size = lax.axis_size("rows")
    bits = size.bit_length() - 1
    near_bits = (bits + 1) // 2
    near = 2**near_bits
    far = size // near
    local_rows = queries.shape[0]
    slab, row_width = prefix_keys.shape
    far_offsets = [near * i for i in range(far)]
    far_order = far_offsets[2:] + far_offsets[1:2]
    vmem = pl.BlockSpec(memory_space=pltpu.VMEM)
    hbm = pl.BlockSpec(memory_space=pltpu.HBM)
    params = pltpu.CompilerParams(vmem_limit_bytes=16 * 2**20)
    own_queries, own_keys, own_rest = pl.pallas_call(
        prepare_kernel,
        out_shape=[
            pltpu.VMEM(queries.shape, queries.dtype),
            pltpu.VMEM((slab, row_width), prefix_keys.dtype),
            pltpu.VMEM((slab + 2 * local_rows, row_width), prefix_keys.dtype),
        ],
        in_specs=[hbm] * 5,
        out_specs=[vmem] * 3,
        scratch_shapes=[
            pltpu.VMEM((2,) + tree_keys.shape, tree_keys.dtype),
            pltpu.SemaphoreType.DMA((5,)),
        ],
        compiler_params=params,
    )(*held(pltpu.HBM, [queries, prefix_keys, prefix_values, tree_keys, tree_values]))

    owner_offsets = [0] + far_order
    key_pieces, rest_pieces = {0: prefix_keys}, {0: own_rest}
    for bit in reversed(range(1, near_bits)):
        for offset in list(key_pieces):
            key_pieces[offset ^ (1 << bit)] = swap(key_pieces[offset], 1 << bit)
            rest_pieces[offset ^ (1 << bit)] = swap(rest_pieces[offset], 1 << bit)
    key_pieces[0] = own_keys
    block_offsets = list(key_pieces)
    sibling_offsets = [offset ^ 1 for offset in block_offsets]
    masks = [
        pl.pallas_call(
            functools.partial(mask_kernel, owner_offsets, offsets, local_rows),
            out_shape=pltpu.VMEM((far * local_rows, len(offsets) * (slab + 2 * local_rows)), jnp.float32),
            in_specs=[vmem],
            out_specs=vmem,
            compiler_params=params,
        )(parents[None, :])
        for offsets in (block_offsets, sibling_offsets)
    ]
    all_queries = {0: own_queries}
    for offset in far_order:
        sent = own_queries
        if offset == far_order[-1]:
            sent, key_pieces[near // 2] = after(sent, key_pieces[near // 2])
        all_queries[offset] = swap(sent, offset)
    gathered = [all_queries[offset] for offset in owner_offsets]
    blocks = list(key_pieces.values()) + list(rest_pieces.values())[:-1]
    bundle = pl.pallas_call(
        stack_kernel,
        out_shape=pltpu.VMEM((sum(block.shape[0] for block in blocks), row_width), prefix_keys.dtype),
        in_specs=[vmem] * len(blocks),
        out_specs=vmem,
        compiler_params=params,
    )(*held(pltpu.VMEM, blocks))
    last_rest = list(rest_pieces.values())[-1]
    far_bundle, far_rest = swap(bundle, 1), swap(last_rest, 1)
    count = len(block_offsets)
    operands = gathered + [bundle, last_rest, masks[0]]
    early_shape = (KV_HEADS, GROUPS * far * local_rows)
    state = pl.pallas_call(
        functools.partial(early_kernel, far, count, slab),
        out_shape=[
            pltpu.VMEM(early_shape + (HEAD_DIM,), jnp.float32),
        ]
        * 3,
        in_specs=[vmem] * len(operands),
        out_specs=[vmem] * 3,
        compiler_params=params,
        cost_estimate=pl.CostEstimate(flops=10999999999, bytes_accessed=36000000, transcendentals=0),
    )(*held(pltpu.VMEM, operands))
    operands = gathered + [far_bundle, far_rest, masks[1], *state]
    partials = pl.pallas_call(
        functools.partial(late_kernel, far, count, slab),
        out_shape=[pltpu.VMEM((local_rows, WIDTH + LANES), jnp.bfloat16)] * far,
        in_specs=[vmem] * len(operands),
        out_specs=[vmem] * far,
        compiler_params=params,
    )(*held(pltpu.VMEM, operands))
    parts = [partials[0]]
    for offset in far_order:
        parts.append(swap(partials[owner_offsets.index(offset)], offset))
    return pl.pallas_call(
        merge_kernel,
        out_shape=jax.ShapeDtypeStruct((local_rows, WIDTH), jnp.bfloat16),
        in_specs=[vmem] * far,
        out_specs=vmem,
        compiler_params=params,
    )(*held(pltpu.VMEM, parts))


def solution(mesh):
    placed = (
        P(("group", "rows"), None),
        P(("group", "rows"), None),
        P(("group", "rows"), None),
        P(("group", "rows"), None),
        P(("group", "rows"), None),
        P("group"),
    )
    return jax.shard_map(
        shards, mesh=mesh, in_specs=placed, out_specs=P(("group", "rows"), None), check_vma=False
    )
```

time: 24.1 us -> 22.9 us (0.950)
  waiting for transfers between devices: 8.35 us -> 6.91 us
  Pallas kernels: 2.99 us -> 3.8 us
  local copies, waits for them, and re-layouts: 0.58 us -> 0.01 us
    ppermute x9 -> x10, waiting for transfers between devices: 8.35 us -> 6.91 us  [swap(): lax.ppermute(x, 'rows', [(i, i ^ offset) for i in range(lax.axis_size('ro...]
    pallas_call x2 -> x5, Pallas kernels: 1.01 us -> 1.83 us  [the longest x1 0.68 us: shards(): pl.pallas_call(functools.partial(late_kernel, far, count, slab), out_shap...]
    unnamed x4 -> x2, local copies, waits for them, and re-layouts: 0.58 us -> 0.01 us
    ppermute x9 -> x10, starting transfers between devices: 11.9 us -> 11.8 us  [swap(): lax.ppermute(x, 'rows', [(i, i ^ offset) for i in range(lax.axis_size('ro...]
  transfers between devices with their start and end apart: 9 -> 10, of which waited for: 6 -> 4; matrix products, arithmetic and copies ran while one was open for 0% -> 0% of each run, Pallas kernels for 1% -> 10%
where the time goes in v4:
time: 22.9 us; the launch traced here: 22.6 us
  starting transfers between devices  11.8 us (52%)
  waiting for transfers between devices  6.91 us (30%)
  Pallas kernels  3.8 us (17%)
    ppermute x10, starting transfers between devices, swap(): lax.ppermute(x, 'rows', [(i, i ^ offset) for i in range(lax.axis_size('ro...  11.8 us
    ppermute x10, waiting for transfers between devices, swap(): lax.ppermute(x, 'rows', [(i, i ^ offset) for i in range(lax.axis_size('ro...  6.91 us
    pallas_call x1, Pallas kernels, shards(): pl.pallas_call(prepare_kernel, out_shape=[pltpu.VMEM(queries.shape, queri...  1.05 us
    pallas_call x1, Pallas kernels, shards(): pl.pallas_call(merge_kernel, out_shape=jax.ShapeDtypeStruct((local_rows,...  0.93 us
    pallas_call x1, Pallas kernels, shards(): pl.pallas_call(functools.partial(late_kernel, far, count, slab), out_shap...  0.68 us
    pallas_call x1, Pallas kernels, shards(): pl.pallas_call(functools.partial(early_kernel, far, count, slab), out_sha...  0.57 us
    pallas_call x2, Pallas kernels, shards(): pl.pallas_call(functools.partial(mask_kernel, owner_offsets, offsets, loc...  0.55 us
  transfers between devices with their start and end apart: 10, of which 4 were waited for; matrix products, arithmetic and copies ran while one was open for 0% of the time, Pallas kernels for 10%

profile of v4, /device:TPU:0, one launch (start us, length us, event | category | flops | bytes accessed | tf_op | source)
XLA Modules:
  0.0 22.6 jit_solution(1611557248752802911)
XLA Ops:
  0.0 3.0 %collective-permute-start.2 = (bf16[64,1024]{1,0:T(8,128)(2,1)}, bf16[64,1024]{1,0:T(8,128)(2,1)S(1)}, u32[]{:S(2)}, u32[]{:S(2)}) collective-permute-start(bf16[64,1024]{1,0:T(8,128)(2,1)} %prefix_keys.1), channel_id=1, source_target_pairs={{0,2},{1,3},{2,0},{3,1},{4,6},{5,7},{6,4},{7,5},{8,10},{9,11},{10,... | collective-permute-start | bytes 393224 | tf_op jit(solution)/shard_map/ppermute | solution.py:188
  3.0 1.0 %shard_map.64 = (bf16[8,3072]{1,0:T(8,128)(2,1)S(1)}, bf16[64,1024]{1,0:T(8,128)(2,1)S(1)}, bf16[80,1024]{1,0:T(8,128)(2,1)S(1)}) custom-call(bf16[8,3072]{1,0:T(8,128)(2,1)} %queries.1, bf16[64,1024]{1,0:T(8,128)(2,1)} %prefix_keys.1, bf16[64,1024]{1,0:T(8,128)(2,1)} %prefix_values.1, bf16[8,1024]{1,0:T(8,128)(2,1)} %tree_keys.1, bf16[8,1024]{1,0:T(8,128)(2,1)} %tree_values.1), custom_call_target="tpu_custom_call" | custom-call | tf_op jit(solution)/shard_map/pallas_call | solution.py:208
  4.0 0.1 collective-permute-start.5
  4.1 0.0 copy-start
  4.1 3.1 %collective-permute-start = (bf16[8,3072]{1,0:T(8,128)(2,1)S(1)}, bf16[8,3072]{1,0:T(8,128)(2,1)S(1)}, u32[]{:S(2)}, u32[]{:S(2)}) collective-permute-start(bf16[8,3072]{1,0:T(8,128)(2,1)S(1)} %get-tuple-element.18.refs_0_), channel_id=1, source_target_pairs={{0,8},{1,9},{2,10},{3,11},{4,12},{5,13},{6,14},{7,15},{8,0},{9,1},... | collective-permute-start | bytes 147464 | tf_op jit(solution)/shard_map/ppermute | solution.py:188
  7.2 1.3 %collective-permute-start.1 = (bf16[8,3072]{1,0:T(8,128)(2,1)S(1)}, bf16[8,3072]{1,0:T(8,128)(2,1)S(1)}, u32[]{:S(2)}, u32[]{:S(2)}) collective-permute-start(bf16[8,3072]{1,0:T(8,128)(2,1)S(1)} %get-tuple-element.18.refs_0_), channel_id=1, source_target_pairs={{0,12},{1,13},{2,14},{3,15},{4,8},{5,9},{6,10},{7,11},{8,4},{9,5},... | collective-permute-start | bytes 147464 | tf_op jit(solution)/shard_map/ppermute | solution.py:188
  8.5 0.0 collective-permute-done.2.refs_1_
  8.5 0.6 %collective-permute-start.3 = (bf16[8,3072]{1,0:T(8,128)(2,1)S(1)}, bf16[8,3072]{1,0:T(8,128)(2,1)S(1)}, u32[]{:S(2)}, u32[]{:S(2)}) collective-permute-start(bf16[8,3072]{1,0:T(8,128)(2,1)S(1)} %get-tuple-element.18.refs_0_), channel_id=1, source_target_pairs={{0,4},{1,5},{2,6},{3,7},{4,0},{5,1},{6,2},{7,3},{8,12},{9,13},{10,... | collective-permute-start | bytes 147464 | tf_op jit(solution)/shard_map/ppermute | solution.py:188
  9.1 0.0 copy-done
  9.1 0.3 %shard_map.67.refs_6_ = f32[32,160]{1,0:T(8,128)S(1)} custom-call(s32[1,128]{1,0:T(1,128)S(1)} %bitcast.1), custom_call_target="tpu_custom_call" | custom-call | tf_op jit(solution)/shard_map/pallas_call | solution.py:234
  9.4 0.3 %shard_map.66.refs_6_ = f32[32,160]{1,0:T(8,128)S(1)} custom-call(s32[1,128]{1,0:T(1,128)S(1)} %bitcast.2), custom_call_target="tpu_custom_call" | custom-call | tf_op jit(solution)/shard_map/pallas_call | solution.py:234
  9.7 0.1 collective-permute-start.4
  9.8 0.4 %collective-permute-done.5.refs_5_ = bf16[80,1024]{1,0:T(8,128)(2,1)S(1)} collective-permute-done((bf16[80,1024]{1,0:T(8,128)(2,1)S(1)}, bf16[80,1024]{1,0:T(8,128)(2,1)S(1)}, u32[]{:S(2)}, u32[]{:S(2)}) %collective-permute-start.5) | collective-permute-done | bytes 163872 | tf_op jit(solution)/shard_map/ppermute | solution.py:188
  10.2 0.1 collective-permute-start.6
  10.3 0.0 collective-permute-done.refs_1_
  10.3 2.8 %collective-permute-done.1.refs_2_ = bf16[8,3072]{1,0:T(8,128)(2,1)S(1)} collective-permute-done((bf16[8,3072]{1,0:T(8,128)(2,1)S(1)}, bf16[8,3072]{1,0:T(8,128)(2,1)S(1)}, u32[]{:S(2)}, u32[]{:S(2)}) %collective-permute-start.1) | collective-permute-done | bytes 49184 | tf_op jit(solution)/shard_map/ppermute | solution.py:188
  13.2 0.0 collective-permute-done.3.refs_3_
  13.2 0.6 %shard_map.68 = (f32[8,96,128]{2,1,0:T(8,128)S(1)}, f32[8,96,128]{2,1,0:T(8,128)S(1)}, f32[8,96,128]{2,1,0:T(8,128)S(1)}) custom-call(bf16[8,3072]{1,0:T(8,128)(2,1)S(1)} %get-tuple-element.18.refs_0_, bf16[8,3072]{1,0:T(8,128)(2,1)S(1)} %collective-permute-done.refs_1_, bf16[8,3072]{1,0:T(8,128)(2,1)S(1)} %collective-permute-done.1.refs_2_, ...), custom_call_target="tpu_custom_call" | custom-call | flops 10999999488 | bytes 36000000 | tf_op jit(solution)/shard_map/pallas_call | solution.py:263
  13.7 0.0 collective-permute-done.6.refs_5_
  13.8 0.0 collective-permute-done.4.refs_4_
  13.8 0.7 %shard_map.69 = (bf16[8,3200]{1,0:T(8,128)(2,1)S(1)}, bf16[8,3200]{1,0:T(8,128)(2,1)S(1)}, bf16[8,3200]{1,0:T(8,128)(2,1)S(1)}, bf16[8,3200]{1,0:T(8,128)(2,1)S(1)}) custom-call(bf16[8,3072]{1,0:T(8,128)(2,1)S(1)} %get-tuple-element.18.refs_0_, bf16[8,3072]{1,0:T(8,128)(2,1)S(1)} %collective-permute-done.refs_1_, ...), custom_call_target="tpu_custom_call" | custom-call | tf_op jit(solution)/shard_map/pallas_call | solution.py:275
  14.4 1.2 %collective-permute-start.7 = (bf16[8,3200]{1,0:T(8,128)(2,1)S(1)}, bf16[8,3200]{1,0:T(8,128)(2,1)S(1)}, u32[]{:S(2)}, u32[]{:S(2)}) collective-permute-start(bf16[8,3200]{1,0:T(8,128)(2,1)S(1)} %get-tuple-element.26), channel_id=1, source_target_pairs={{0,8},{1,9},{2,10},{3,11},{4,12},{5,13},{6,14},{7,15},{8,0},{9,1},... | collective-permute-start | bytes 153608 | tf_op jit(solution)/shard_map/ppermute | solution.py:188
  15.7 1.3 %collective-permute-start.8 = (bf16[8,3200]{1,0:T(8,128)(2,1)S(1)}, bf16[8,3200]{1,0:T(8,128)(2,1)S(1)}, u32[]{:S(2)}, u32[]{:S(2)}) collective-permute-start(bf16[8,3200]{1,0:T(8,128)(2,1)S(1)} %get-tuple-element.27), channel_id=1, source_target_pairs={{0,12},{1,13},{2,14},{3,15},{4,8},{5,9},{6,10},{7,11},{8,4},{9,5},... | collective-permute-start | bytes 153608 | tf_op jit(solution)/shard_map/ppermute | solution.py:188
  16.9 1.1 %collective-permute-start.9 = (bf16[8,3200]{1,0:T(8,128)(2,1)S(1)}, bf16[8,3200]{1,0:T(8,128)(2,1)S(1)}, u32[]{:S(2)}, u32[]{:S(2)}) collective-permute-start(bf16[8,3200]{1,0:T(8,128)(2,1)S(1)} %get-tuple-element.28), channel_id=1, source_target_pairs={{0,4},{1,5},{2,6},{3,7},{4,0},{5,1},{6,2},{7,3},{8,12},{9,13},{10,... | collective-permute-start | bytes 153608 | tf_op jit(solution)/shard_map/ppermute | solution.py:188
  18.0 2.7 %collective-permute-done.7.refs_1_ = bf16[8,3200]{1,0:T(8,128)(2,1)S(1)} collective-permute-done((bf16[8,3200]{1,0:T(8,128)(2,1)S(1)}, bf16[8,3200]{1,0:T(8,128)(2,1)S(1)}, u32[]{:S(2)}, u32[]{:S(2)}) %collective-permute-start.7) | collective-permute-done | bytes 51232 | tf_op jit(solution)/shard_map/ppermute | solution.py:188
  20.7 1.0 %collective-permute-done.8.refs_2_ = bf16[8,3200]{1,0:T(8,128)(2,1)S(1)} collective-permute-done((bf16[8,3200]{1,0:T(8,128)(2,1)S(1)}, bf16[8,3200]{1,0:T(8,128)(2,1)S(1)}, u32[]{:S(2)}, u32[]{:S(2)}) %collective-permute-start.8) | collective-permute-done | bytes 51232 | tf_op jit(solution)/shard_map/ppermute | solution.py:188
  21.7 0.0 collective-permute-done.9.refs_3_
  21.7 0.9 %shard_map.70 = bf16[8,3072]{1,0:T(8,128)(2,1)} custom-call(bf16[8,3200]{1,0:T(8,128)(2,1)S(1)} %get-tuple-element.25.refs_0_, bf16[8,3200]{1,0:T(8,128)(2,1)S(1)} %collective-permute-done.7.refs_1_, bf16[8,3200]{1,0:T(8,128)(2,1)S(1)} %collective-permute-done.8.refs_2_, bf16[8,3200]{1,0:T(8,128)(2,1)S(1)} %collective-permute-done.9.refs_3_), custom_call_target="tpu_custom_call" | custom-call | tf_op jit(solution)/shard_map/pallas_call | solution.py:285
  (1 shorter events, 0.0 us)
Async XLA Ops:
  0.0 8.5 %collective-permute-start.2 = (bf16[64,1024]{1,0:T(8,128)(2,1)}, bf16[64,1024]{1,0:T(8,128)(2,1)S(1)}, u32[]{:S(2)}, u32[]{:S(2)}) collective-permute-start(bf16[64,1024]{1,0:T(8,128)(2,1)} %prefix_keys.1), channel_id=1, source_target_pairs={{0,2},{1,3},{2,0},{3,1},{4,6},{5,7},{6,4},{7,5},{8,10},{9,11},{10,... | collective-permute-start | bytes 393224 | tf_op jit(solution)/shard_map/ppermute | solution.py:188
  4.0 6.2 %collective-permute-start.5 = (bf16[80,1024]{1,0:T(8,128)(2,1)S(1)}, bf16[80,1024]{1,0:T(8,128)(2,1)S(1)}, u32[]{:S(2)}, u32[]{:S(2)}) collective-permute-start(bf16[80,1024]{1,0:T(8,128)(2,1)S(1)} %get-tuple-element.21.refs_2_), channel_id=1, source_target_pairs={{0,2},{1,3},{2,0},{3,1},{4,6},{5,7},{6,4},{7,5},{8,10},{9,11},{10,... | collective-permute-start | bytes 491528 | tf_op jit(solution)/shard_map/ppermute | solution.py:188
  4.1 5.0 %copy-start = (s32[128]{0:T(128)S(1)}, s32[128]{0:T(128)}, u32[]{:S(2)}) copy-start(s32[128]{0:T(128)} %param.11) | copy-start | bytes 1540
  4.1 6.2 %collective-permute-start = (bf16[8,3072]{1,0:T(8,128)(2,1)S(1)}, bf16[8,3072]{1,0:T(8,128)(2,1)S(1)}, u32[]{:S(2)}, u32[]{:S(2)}) collective-permute-start(bf16[8,3072]{1,0:T(8,128)(2,1)S(1)} %get-tuple-element.18.refs_0_), channel_id=1, source_target_pairs={{0,8},{1,9},{2,10},{3,11},{4,12},{5,13},{6,14},{7,15},{8,0},{9,1},... | collective-permute-start | bytes 147464 | tf_op jit(solution)/shard_map/ppermute | solution.py:188
  7.2 6.0 %collective-permute-start.1 = (bf16[8,3072]{1,0:T(8,128)(2,1)S(1)}, bf16[8,3072]{1,0:T(8,128)(2,1)S(1)}, u32[]{:S(2)}, u32[]{:S(2)}) collective-permute-start(bf16[8,3072]{1,0:T(8,128)(2,1)S(1)} %get-tuple-element.18.refs_0_), channel_id=1, source_target_pairs={{0,12},{1,13},{2,14},{3,15},{4,8},{5,9},{6,10},{7,11},{8,4},{9,5},... | collective-permute-start | bytes 147464 | tf_op jit(solution)/shard_map/ppermute | solution.py:188
  8.5 4.6 %collective-permute-start.3 = (bf16[8,3072]{1,0:T(8,128)(2,1)S(1)}, bf16[8,3072]{1,0:T(8,128)(2,1)S(1)}, u32[]{:S(2)}, u32[]{:S(2)}) collective-permute-start(bf16[8,3072]{1,0:T(8,128)(2,1)S(1)} %get-tuple-element.18.refs_0_), channel_id=1, source_target_pairs={{0,4},{1,5},{2,6},{3,7},{4,0},{5,1},{6,2},{7,3},{8,12},{9,13},{10,... | collective-permute-start | bytes 147464 | tf_op jit(solution)/shard_map/ppermute | solution.py:188
  9.7 4.0 %collective-permute-start.4 = (bf16[208,1024]{1,0:T(8,128)(2,1)S(1)}, bf16[208,1024]{1,0:T(8,128)(2,1)S(1)}, u32[]{:S(2)}, u32[]{:S(2)}) collective-permute-start(bf16[208,1024]{1,0:T(8,128)(2,1)S(1)} %shard_map.65.refs_4_), channel_id=1, source_target_pairs={{0,1},{1,0},{2,3},{3,2},{4,5},{5,4},{6,7},{7,6},{8,9},{9,8},{10,11... | collective-permute-start | bytes 1277960 | tf_op jit(solution)/shard_map/ppermute | solution.py:188
  10.2 3.6 %collective-permute-start.6 = (bf16[80,1024]{1,0:T(8,128)(2,1)S(1)}, bf16[80,1024]{1,0:T(8,128)(2,1)S(1)}, u32[]{:S(2)}, u32[]{:S(2)}) collective-permute-start(bf16[80,1024]{1,0:T(8,128)(2,1)S(1)} %collective-permute-done.5.refs_5_), channel_id=1, source_target_pairs={{0,1},{1,0},{2,3},{3,2},{4,5},{5,4},{6,7},{7,6},{8,9},{9,8},{10,11... | collective-permute-start | bytes 491528 | tf_op jit(solution)/shard_map/ppermute | solution.py:188
  14.4 6.2 %collective-permute-start.7 = (bf16[8,3200]{1,0:T(8,128)(2,1)S(1)}, bf16[8,3200]{1,0:T(8,128)(2,1)S(1)}, u32[]{:S(2)}, u32[]{:S(2)}) collective-permute-start(bf16[8,3200]{1,0:T(8,128)(2,1)S(1)} %get-tuple-element.26), channel_id=1, source_target_pairs={{0,8},{1,9},{2,10},{3,11},{4,12},{5,13},{6,14},{7,15},{8,0},{9,1},... | collective-permute-start | bytes 153608 | tf_op jit(solution)/shard_map/ppermute | solution.py:188
  15.7 6.0 %collective-permute-start.8 = (bf16[8,3200]{1,0:T(8,128)(2,1)S(1)}, bf16[8,3200]{1,0:T(8,128)(2,1)S(1)}, u32[]{:S(2)}, u32[]{:S(2)}) collective-permute-start(bf16[8,3200]{1,0:T(8,128)(2,1)S(1)} %get-tuple-element.27), channel_id=1, source_target_pairs={{0,12},{1,13},{2,14},{3,15},{4,8},{5,9},{6,10},{7,11},{8,4},{9,5},... | collective-permute-start | bytes 153608 | tf_op jit(solution)/shard_map/ppermute | solution.py:188
  16.9 4.8 %collective-permute-start.9 = (bf16[8,3200]{1,0:T(8,128)(2,1)S(1)}, bf16[8,3200]{1,0:T(8,128)(2,1)S(1)}, u32[]{:S(2)}, u32[]{:S(2)}) collective-permute-start(bf16[8,3200]{1,0:T(8,128)(2,1)S(1)} %get-tuple-element.28), channel_id=1, source_target_pairs={{0,4},{1,5},{2,6},{3,7},{4,0},{5,1},{6,2},{7,3},{8,12},{9,13},{10,... | collective-permute-start | bytes 153608 | tf_op jit(solution)/shard_map/ppermute | solution.py:188

commit v5 on v4

v5 whole, which is shorter than its diff:
```python
import functools

import jax
import jax.numpy as jnp
from jax import lax
from jax.experimental import pallas as pl
from jax.experimental.pallas import tpu as pltpu
from jax.sharding import PartitionSpec as P

QUERY_HEADS = 24
KV_HEADS = 8
HEAD_DIM = 128
TREE_DEPTH = 4
GROUPS = QUERY_HEADS // KV_HEADS
WIDTH = QUERY_HEADS * HEAD_DIM
LANES = 128
STRIDE = 32
CHUNKS = 4
NT = (((1,), (1,)), ((), ()))
HEADS = [slice(head * HEAD_DIM, (head + 1) * HEAD_DIM) for head in range(QUERY_HEADS)]


def rest_kernel(prefix_values, tree_keys, tree_values, rest, tree_scratch, sems):
    slab = prefix_values.shape[0]
    chunk = slab // CHUNKS
    copies = [
        pltpu.make_async_copy(tree_keys, tree_scratch.at[0], sems.at[0]),
        pltpu.make_async_copy(tree_values, tree_scratch.at[1], sems.at[1]),
    ]
    for place in range(CHUNKS):
        rows = slice(place * chunk, (place + 1) * chunk)
        copies.append(pltpu.make_async_copy(prefix_values.at[rows], rest.at[rows], sems.at[2 + place]))
    for copy in copies:
        copy.start()
    for copy in copies:
        copy.wait()
    trees = [tree_scratch[0].astype(jnp.float32), tree_scratch[1].astype(jnp.float32)]
    local_rows = (rest.shape[0] - slab) // 2
    for head in range(KV_HEADS):
        rows = slice(head * local_rows, (head + 1) * local_rows)
        both = jnp.concatenate([tree[rows] for tree in trees], axis=0)
        rest[slab:, HEADS[head]] = both.astype(rest.dtype)


def stack_kernel(*refs):
    blocks, out = refs[:-1], refs[-1]
    first = 0
    for block in blocks:
        out[first : first + block.shape[0]] = block[...]
        first += block.shape[0]


def chosen(index, values):
    picked = jnp.full(index.shape, values[0], jnp.int32)
    for place in range(1, len(values)):
        picked = jnp.where(index == place, values[place], picked)
    return picked


def mask_kernel(owner_offsets, token_offsets, local_rows, parents, bias):
    position = lax.axis_index("rows")
    rows, columns = bias.shape
    block = columns // len(token_offsets)
    slab = block - 2 * local_rows
    slot = lax.broadcasted_iota(jnp.int32, (rows, 1), 0)
    walker = (position ^ chosen(slot // local_rows, owner_offsets)) * local_rows + slot % local_rows
    slot = lax.broadcasted_iota(jnp.int32, (1, columns), 1)
    within = slot % block - slab
    token = (position ^ chosen(slot // block, token_offsets)) * local_rows + within
    is_tree = (within >= 0) & (within < local_rows)
    candidates = lax.broadcasted_iota(jnp.int32, (rows, parents.shape[1]), 1)
    parent = parents[...]
    allowed = walker == token
    for _ in range(TREE_DEPTH - 1):
        walker = jnp.sum(jnp.where(walker == candidates, parent, 0), axis=1, keepdims=True)
        allowed = allowed | (walker == token)
    bias[...] = jnp.where((allowed & is_tree) | (within < 0), 0.0, -jnp.inf)


def block_rows(parts, local_rows):
    keys, values = [], []
    for slab_keys, rest in parts:
        slab = slab_keys.shape[0]
        tree = rest[slab:]
        halves = tree.astype(jnp.float32)
        turned = jnp.concatenate([halves[local_rows:], halves[:local_rows]], axis=0)
        keys += [slab_keys[...], tree]
        values += [rest[:slab], turned.astype(jnp.bfloat16)]
    return keys, values


def bundle_parts(bundle, last_rest, count, slab, local_rows):
    block = slab + 2 * local_rows
    rests = [bundle.at[count * slab + i * block : count * slab + (i + 1) * block] for i in range(count - 1)]
    return [(bundle.at[i * slab : (i + 1) * slab], rest) for i, rest in enumerate(rests + [last_rest])]


def rows_kernel(*refs):
    blocks, out = refs[:-1], refs[-1]
    rows = blocks[0].shape[0]
    for place in range(0, len(blocks), 2):
        both = [block[...].astype(jnp.float32) for block in blocks[place : place + 2]]
        out[place * rows : (place + 2) * rows] = jnp.concatenate(both, axis=0).astype(out.dtype)


def attend_kernel(owners, count, slab, queries, near_bundle, near_rest, far_bundle, far_rest, bias_ref, *outs):
    rows = queries.shape[0]
    local_rows = rows // owners
    parts = bundle_parts(near_bundle, near_rest, count, slab, local_rows)
    parts += bundle_parts(far_bundle, far_rest, count, slab, local_rows)
    key_parts, value_parts = block_rows(parts, local_rows)
    bias = jnp.concatenate([bias_ref[...]] * GROUPS, axis=0)
    scores = []
    for head in range(KV_HEADS):
        query = jnp.concatenate([queries[:, HEADS[head * GROUPS + g]] for g in range(GROUPS)], axis=0)
        keys = jnp.concatenate([part[:, HEADS[head]] for part in key_parts], axis=0)
        products = lax.dot_general(query, keys, NT, preferred_element_type=jnp.float32)
        scores.append(products * HEAD_DIM ** (-0.5) + bias)
    weights = []
    for head in range(KV_HEADS):
        maxima = jnp.max(scores[head], axis=1, keepdims=True)
        exps = jnp.exp(scores[head] - maxima)
        masses = jnp.sum(exps, axis=1, keepdims=True)
        weights.append((exps.astype(jnp.bfloat16), maxima + jnp.log(masses), 1.0 / masses))
    lane = lax.broadcasted_iota(jnp.int32, (rows, LANES), 1)
    stats = jnp.zeros((rows, LANES), jnp.float32)
    for head, (rounded, level, inverse) in enumerate(weights):
        values = jnp.concatenate([part[:, HEADS[head]] for part in value_parts], axis=0)
        weighted = jnp.dot(rounded, values, preferred_element_type=jnp.float32) * inverse
        for g in range(GROUPS):
            query_head = head * GROUPS + g
            here = (lane % STRIDE == query_head) & (lane < 3 * STRIDE)
            stats = jnp.where(here, level[g * rows : (g + 1) * rows], stats)
            for owner in range(owners):
                first = g * rows + owner * local_rows
                outs[owner][:, HEADS[query_head]] = weighted[first : first + local_rows].astype(jnp.bfloat16)
    high = stats.astype(jnp.bfloat16).astype(jnp.float32)
    left = stats - high
    middle = left.astype(jnp.bfloat16).astype(jnp.float32)
    low = left - middle
    sent = jnp.where(lane < STRIDE, high, jnp.where(lane < 2 * STRIDE, middle, low))
    for owner in range(owners):
        outs[owner][:, WIDTH:] = sent[owner * local_rows : (owner + 1) * local_rows].astype(jnp.bfloat16)


def merge_kernel(*refs):
    parts, out = refs[:-1], refs[-1]
    levels = []
    for part in parts:
        terms = part[:, WIDTH:].astype(jnp.float32)
        levels.append(terms + pltpu.roll(terms, LANES - STRIDE, 1) + pltpu.roll(terms, LANES - 2 * STRIDE, 1))
    top = functools.reduce(jnp.maximum, levels)
    shares = [jnp.exp(level - top) for level in levels]
    whole = 1.0 / functools.reduce(jnp.add, shares)
    shares = [share * whole for share in shares]
    for head in range(QUERY_HEADS):
        total = functools.reduce(
            jnp.add,
            [
                share[:, head : head + 1] * part[:, HEADS[head]].astype(jnp.float32)
                for share, part in zip(shares, parts)
            ],
        )
        out[:, HEADS[head]] = total.astype(out.dtype)


def held(memory, arrays):
    return [pltpu.with_memory_space_constraint(x, memory) for x in arrays]


def swap(x, offset):
    return lax.ppermute(x, "rows", [(i, i ^ offset) for i in range(lax.axis_size("rows"))])


def by_head(x):
    return jnp.transpose(x.reshape(-1, KV_HEADS, HEAD_DIM), (1, 0, 2)).reshape(-1, HEAD_DIM)


def after(x, *earlier):
    return lax.optimization_barrier((x, *earlier))


def shards(queries, prefix_keys, prefix_values, tree_keys, tree_values, parents):
    size = lax.axis_size("rows")
    bits = size.bit_length() - 1
    near_bits = (bits + 1) // 2
    near = 2**near_bits
    far = size // near
    local_rows = queries.shape[0]
    slab, row_width = prefix_keys.shape
    far_offsets = [near * i for i in range(far)]
    far_order = far_offsets[:0:-1]
    vmem = pl.BlockSpec(memory_space=pltpu.VMEM)
    hbm = pl.BlockSpec(memory_space=pltpu.HBM)
    params = pltpu.CompilerParams(vmem_limit_bytes=16 * 2**20)
    own_rest = pl.pallas_call(
        rest_kernel,
        out_shape=pltpu.VMEM((slab + 2 * local_rows, row_width), prefix_values.dtype),
        in_specs=[hbm] * 3,
        out_specs=vmem,
        scratch_shapes=[
            pltpu.VMEM((2, KV_HEADS * local_rows, HEAD_DIM), tree_keys.dtype),
            pltpu.SemaphoreType.DMA((2 + CHUNKS,)),
        ],
        compiler_params=params,
    )(*held(pltpu.HBM, [prefix_values, by_head(tree_keys), by_head(tree_values)]))

    owner_offsets = [0] + far_order
    key_pieces, rest_pieces = {0: prefix_keys}, {0: own_rest}
    for bit in reversed(range(1, near_bits)):
        for offset in list(key_pieces):
            key_pieces[offset ^ (1 << bit)] = swap(key_pieces[offset], 1 << bit)
            rest_pieces[offset ^ (1 << bit)] = swap(rest_pieces[offset], 1 << bit)
    block_offsets = list(key_pieces)
    sibling_offsets = [offset ^ 1 for offset in block_offsets]
    mask = pl.pallas_call(
        functools.partial(mask_kernel, owner_offsets, block_offsets + sibling_offsets, local_rows),
        out_shape=pltpu.VMEM((far * local_rows, near * (slab + 2 * local_rows)), jnp.float32),
        in_specs=[vmem],
        out_specs=vmem,
        compiler_params=params,
    )(parents[None, :])
    all_queries = {0: queries}
    for offset in far_order:
        sent = queries
        if offset == far_order[-1]:
            sent, key_pieces[near // 2] = after(sent, key_pieces[near // 2])
        all_queries[offset] = swap(sent, offset)
    gathered = pl.pallas_call(
        rows_kernel,
        out_shape=pltpu.VMEM((far * local_rows, WIDTH), queries.dtype),
        in_specs=[vmem] * far,
        out_specs=vmem,
        compiler_params=params,
        cost_estimate=pl.CostEstimate(flops=10999999999, bytes_accessed=36000000, transcendentals=0),
    )(*held(pltpu.VMEM, [all_queries[offset] for offset in owner_offsets]))
    blocks = list(key_pieces.values()) + list(rest_pieces.values())[:-1]
    bundle = pl.pallas_call(
        stack_kernel,
        out_shape=pltpu.VMEM((sum(block.shape[0] for block in blocks), row_width), prefix_keys.dtype),
        in_specs=[vmem] * len(blocks),
        out_specs=vmem,
        compiler_params=params,
    )(*held(pltpu.VMEM, blocks))
    last_rest = list(rest_pieces.values())[-1]
    far_bundle, far_rest = swap(bundle, 1), swap(last_rest, 1)
    count = len(block_offsets)
    operands = [gathered, bundle, last_rest, far_bundle, far_rest, mask]
    partials = pl.pallas_call(
        functools.partial(attend_kernel, far, count, slab),
        out_shape=[pltpu.VMEM((local_rows, WIDTH + LANES), jnp.bfloat16)] * far,
        in_specs=[vmem] * len(operands),
        out_specs=[vmem] * far,
        compiler_params=params,
    )(*held(pltpu.VMEM, operands))
    parts = [partials[0]]
    for offset in far_offsets[2:] + far_offsets[1:2]:
        parts.append(swap(partials[owner_offsets.index(offset)], offset))
    return pl.pallas_call(
        merge_kernel,
        out_shape=jax.ShapeDtypeStruct((local_rows, WIDTH), jnp.bfloat16),
        in_specs=[vmem] * far,
        out_specs=vmem,
        compiler_params=params,
    )(*held(pltpu.VMEM, parts))


def solution(mesh):
    placed = (
        P(("group", "rows"), None),
        P(("group", "rows"), None),
        P(("group", "rows"), None),
        P(("group", "rows"), None),
        P(("group", "rows"), None),
        P("group"),
    )
    return jax.shard_map(
        shards, mesh=mesh, in_specs=placed, out_specs=P(("group", "rows"), None), check_vma=False
    )
```

time: 22.9 us -> 22.5 us (0.983)
  Pallas kernels: 3.8 us -> 2.88 us
  waiting for transfers between devices: 6.91 us -> 7.42 us
    pallas_call x5 -> x4, Pallas kernels: 2.85 us -> 1.93 us  [the longest x1 0.93 us: shards(): pl.pallas_call(rest_kernel, out_shape=pltpu.VMEM((slab + 2 * local_rows,...]
    ppermute x10, waiting for transfers between devices: 6.91 us -> 7.42 us  [swap(): lax.ppermute(x, 'rows', [(i, i ^ offset) for i in range(lax.axis_size('ro...]
  transfers between devices with their start and end apart: 10 -> 10, of which waited for: 4 -> 5; matrix products, arithmetic and copies ran while one was open for 0% -> 0% of each run, Pallas kernels for 10% -> 6%
where the time goes in v5:
time: 22.5 us; the launch traced here: 22.3 us
  starting transfers between devices  11.9 us (53%)
  waiting for transfers between devices  7.42 us (33%)
  Pallas kernels  2.88 us (13%)
    ppermute x10, starting transfers between devices, swap(): lax.ppermute(x, 'rows', [(i, i ^ offset) for i in range(lax.axis_size('ro...  11.9 us
    ppermute x10, waiting for transfers between devices, swap(): lax.ppermute(x, 'rows', [(i, i ^ offset) for i in range(lax.axis_size('ro...  7.42 us
    pallas_call x1, Pallas kernels, shards(): pl.pallas_call(rest_kernel, out_shape=pltpu.VMEM((slab + 2 * local_rows,...  0.93 us
    pallas_call x1, Pallas kernels, shards(): pl.pallas_call(merge_kernel, out_shape=jax.ShapeDtypeStruct((local_rows,...  0.93 us
    pallas_call x1, Pallas kernels, shards(): pl.pallas_call(functools.partial(attend_kernel, far, count, slab), out_sh...  0.7 us
  transfers between devices with their start and end apart: 10, of which 5 were waited for; matrix products, arithmetic and copies ran while one was open for 0% of the time, Pallas kernels for 6%

profile of v5, /device:TPU:0, one launch (start us, length us, event | category | flops | bytes accessed | tf_op | source)
XLA Modules:
  0.0 22.3 jit_solution(10777526767076414226)
XLA Ops:
  0.0 3.0 %collective-permute-start.2 = (bf16[64,1024]{1,0:T(8,128)(2,1)}, bf16[64,1024]{1,0:T(8,128)(2,1)S(1)}, u32[]{:S(2)}, u32[]{:S(2)}) collective-permute-start(bf16[64,1024]{1,0:T(8,128)(2,1)} %refs_0_.3), channel_id=1, source_target_pairs={{0,2},{1,3},{2,0},{3,1},{4,6},{5,7},{6,4},{7,5},{8,10},{9,11},{10,... | collective-permute-start | bytes 393224 | tf_op jit(solution)/shard_map/ppermute | solution.py:172
  3.0 0.0 copy-start.2
  3.0 0.0 copy-start
  3.0 0.9 %shard_map.65.refs_2_ = bf16[80,1024]{1,0:T(8,128)(2,1)S(1)} custom-call(bf16[64,1024]{1,0:T(8,128)(2,1)} %prefix_values.1, bf16[64,128]{1,0:T(8,128)(2,1)} %bitcast.12, bf16[64,128]{1,0:T(8,128)(2,1)} %bitcast.13), custom_call_target="tpu_custom_call" | custom-call | tf_op jit(solution)/shard_map/pallas_call | solution.py:196
  3.9 0.0 copy-start.1
  3.9 0.1 collective-permute-start.4
  4.0 0.0 copy-done.2
  4.0 3.1 %collective-permute-start.1 = (bf16[8,3072]{1,0:T(8,128)(2,1)S(1)}, bf16[8,3072]{1,0:T(8,128)(2,1)S(1)}, u32[]{:S(2)}, u32[]{:S(2)}) collective-permute-start(bf16[8,3072]{1,0:T(8,128)(2,1)S(1)} %copy-done.2), channel_id=1, source_target_pairs={{0,8},{1,9},{2,10},{3,11},{4,12},{5,13},{6,14},{7,15},{8,0},{9,1},... | collective-permute-start | bytes 147464 | tf_op jit(solution)/shard_map/ppermute | solution.py:172
  7.1 1.3 %collective-permute-start = (bf16[8,3072]{1,0:T(8,128)(2,1)S(1)}, bf16[8,3072]{1,0:T(8,128)(2,1)S(1)}, u32[]{:S(2)}, u32[]{:S(2)}) collective-permute-start(bf16[8,3072]{1,0:T(8,128)(2,1)S(1)} %copy-done.2), channel_id=1, source_target_pairs={{0,12},{1,13},{2,14},{3,15},{4,8},{5,9},{6,10},{7,11},{8,4},{9,5},... | collective-permute-start | bytes 147464 | tf_op jit(solution)/shard_map/ppermute | solution.py:172
  8.4 0.0 collective-permute-done.2.refs_1_
  8.4 0.8 %collective-permute-start.3 = (bf16[8,3072]{1,0:T(8,128)(2,1)S(1)}, bf16[8,3072]{1,0:T(8,128)(2,1)S(1)}, u32[]{:S(2)}, u32[]{:S(2)}) collective-permute-start(bf16[8,3072]{1,0:T(8,128)(2,1)S(1)} %copy-done.2), channel_id=1, source_target_pairs={{0,4},{1,5},{2,6},{3,7},{4,0},{5,1},{6,2},{7,3},{8,12},{9,13},{10,... | collective-permute-start | bytes 147464 | tf_op jit(solution)/shard_map/ppermute | solution.py:172
  9.2 0.0 copy-done.1
  9.2 0.3 %shard_map.67.bias_ref = f32[32,320]{1,0:T(8,128)S(1)} custom-call(s32[1,128]{1,0:T(1,128)S(1)} %bitcast.11), custom_call_target="tpu_custom_call" | custom-call | tf_op jit(solution)/shard_map/pallas_call | solution.py:216
  9.5 0.0 copy-done
  9.6 0.1 collective-permute-start.5
  9.7 0.5 %collective-permute-done.4.near_rest = bf16[80,1024]{1,0:T(8,128)(2,1)S(1)} collective-permute-done((bf16[80,1024]{1,0:T(8,128)(2,1)S(1)}, bf16[80,1024]{1,0:T(8,128)(2,1)S(1)}, u32[]{:S(2)}, u32[]{:S(2)}) %collective-permute-start.4) | collective-permute-done | bytes 163872 | tf_op jit(solution)/shard_map/ppermute | solution.py:172
  10.2 0.0 collective-permute-start.6
  10.2 0.0 collective-permute-done.1.refs_2_
  10.2 2.9 %collective-permute-done.refs_1_ = bf16[8,3072]{1,0:T(8,128)(2,1)S(1)} collective-permute-done((bf16[8,3072]{1,0:T(8,128)(2,1)S(1)}, bf16[8,3072]{1,0:T(8,128)(2,1)S(1)}, u32[]{:S(2)}, u32[]{:S(2)}) %collective-permute-start) | collective-permute-done | bytes 49184 | tf_op jit(solution)/shard_map/ppermute | solution.py:172
  13.1 0.0 collective-permute-done.3.refs_3_
  13.1 0.0 collective-permute-done.6.far_rest
  13.1 0.0 collective-permute-done.5.far_bundle
  13.1 0.7 %shard_map.68 = (bf16[8,3200]{1,0:T(8,128)(2,1)S(1)}, bf16[8,3200]{1,0:T(8,128)(2,1)S(1)}, bf16[8,3200]{1,0:T(8,128)(2,1)S(1)}, bf16[8,3200]{1,0:T(8,128)(2,1)S(1)}) custom-call(bf16[32,3072]{1,0:T(8,128)(2,1)S(1)} %shard_map.64.queries, bf16[208,1024]{1,0:T(8,128)(2,1)S(1)} %shard_map.66.near_bundle, bf16[80,1024]{1,0:T(8,128)(2,1)S(1)} %collective-permute-done.4.near_rest, ...), custom_call_target="tpu_custom_call" | custom-call | tf_op jit(solution)/shard_map/pallas_call | solution.py:249
  13.8 1.4 %collective-permute-start.7 = (bf16[8,3200]{1,0:T(8,128)(2,1)S(1)}, bf16[8,3200]{1,0:T(8,128)(2,1)S(1)}, u32[]{:S(2)}, u32[]{:S(2)}) collective-permute-start(bf16[8,3200]{1,0:T(8,128)(2,1)S(1)} %get-tuple-element.14), channel_id=1, source_target_pairs={{0,8},{1,9},{2,10},{3,11},{4,12},{5,13},{6,14},{7,15},{8,0},{9,1},... | collective-permute-start | bytes 153608 | tf_op jit(solution)/shard_map/ppermute | solution.py:172
  15.2 1.3 %collective-permute-start.8 = (bf16[8,3200]{1,0:T(8,128)(2,1)S(1)}, bf16[8,3200]{1,0:T(8,128)(2,1)S(1)}, u32[]{:S(2)}, u32[]{:S(2)}) collective-permute-start(bf16[8,3200]{1,0:T(8,128)(2,1)S(1)} %get-tuple-element.15), channel_id=1, source_target_pairs={{0,12},{1,13},{2,14},{3,15},{4,8},{5,9},{6,10},{7,11},{8,4},{9,5},... | collective-permute-start | bytes 153608 | tf_op jit(solution)/shard_map/ppermute | solution.py:172
  16.5 0.8 %collective-permute-start.9 = (bf16[8,3200]{1,0:T(8,128)(2,1)S(1)}, bf16[8,3200]{1,0:T(8,128)(2,1)S(1)}, u32[]{:S(2)}, u32[]{:S(2)}) collective-permute-start(bf16[8,3200]{1,0:T(8,128)(2,1)S(1)} %get-tuple-element.16), channel_id=1, source_target_pairs={{0,4},{1,5},{2,6},{3,7},{4,0},{5,1},{6,2},{7,3},{8,12},{9,13},{10,... | collective-permute-start | bytes 153608 | tf_op jit(solution)/shard_map/ppermute | solution.py:172
  17.4 2.8 %collective-permute-done.7.refs_1_ = bf16[8,3200]{1,0:T(8,128)(2,1)S(1)} collective-permute-done((bf16[8,3200]{1,0:T(8,128)(2,1)S(1)}, bf16[8,3200]{1,0:T(8,128)(2,1)S(1)}, u32[]{:S(2)}, u32[]{:S(2)}) %collective-permute-start.7) | collective-permute-done | bytes 51232 | tf_op jit(solution)/shard_map/ppermute | solution.py:172
  20.2 1.0 %collective-permute-done.8.refs_2_ = bf16[8,3200]{1,0:T(8,128)(2,1)S(1)} collective-permute-done((bf16[8,3200]{1,0:T(8,128)(2,1)S(1)}, bf16[8,3200]{1,0:T(8,128)(2,1)S(1)}, u32[]{:S(2)}, u32[]{:S(2)}) %collective-permute-start.8) | collective-permute-done | bytes 51232 | tf_op jit(solution)/shard_map/ppermute | solution.py:172
  21.2 0.1 collective-permute-done.9.refs_3_
  21.4 0.9 %shard_map.69 = bf16[8,3072]{1,0:T(8,128)(2,1)} custom-call(bf16[8,3200]{1,0:T(8,128)(2,1)S(1)} %get-tuple-element.13.refs_0_, bf16[8,3200]{1,0:T(8,128)(2,1)S(1)} %collective-permute-done.7.refs_1_, bf16[8,3200]{1,0:T(8,128)(2,1)S(1)} %collective-permute-done.8.refs_2_, bf16[8,3200]{1,0:T(8,128)(2,1)S(1)} %collective-permute-done.9.refs_3_), custom_call_target="tpu_custom_call" | custom-call | tf_op jit(solution)/shard_map/pallas_call | solution.py:259
  (2 shorter events, 0.0 us)
Async XLA Ops:
  0.0 8.4 %collective-permute-start.2 = (bf16[64,1024]{1,0:T(8,128)(2,1)}, bf16[64,1024]{1,0:T(8,128)(2,1)S(1)}, u32[]{:S(2)}, u32[]{:S(2)}) collective-permute-start(bf16[64,1024]{1,0:T(8,128)(2,1)} %refs_0_.3), channel_id=1, source_target_pairs={{0,2},{1,3},{2,0},{3,1},{4,6},{5,7},{6,4},{7,5},{8,10},{9,11},{10,... | collective-permute-start | bytes 393224 | tf_op jit(solution)/shard_map/ppermute | solution.py:172
  3.0 1.0 %copy-start.2 = (bf16[8,3072]{1,0:T(8,128)(2,1)S(1)}, bf16[8,3072]{1,0:T(8,128)(2,1)}, u32[]{:S(2)}) copy-start(bf16[8,3072]{1,0:T(8,128)(2,1)} %refs_0_.2) | copy-start | bytes 147460
  3.0 6.6 %copy-start = (bf16[64,1024]{1,0:T(8,128)(2,1)S(1)}, bf16[64,1024]{1,0:T(8,128)(2,1)}, u32[]{:S(2)}) copy-start(bf16[64,1024]{1,0:T(8,128)(2,1)} %refs_0_.3) | copy-start | bytes 393220
  3.9 5.3 %copy-start.1 = (s32[128]{0:T(128)S(1)}, s32[128]{0:T(128)}, u32[]{:S(2)}) copy-start(s32[128]{0:T(128)} %param.11) | copy-start | bytes 1540
  3.9 6.3 %collective-permute-start.4 = (bf16[80,1024]{1,0:T(8,128)(2,1)S(1)}, bf16[80,1024]{1,0:T(8,128)(2,1)S(1)}, u32[]{:S(2)}, u32[]{:S(2)}) collective-permute-start(bf16[80,1024]{1,0:T(8,128)(2,1)S(1)} %shard_map.65.refs_2_), channel_id=1, source_target_pairs={{0,2},{1,3},{2,0},{3,1},{4,6},{5,7},{6,4},{7,5},{8,10},{9,11},{10,... | collective-permute-start | bytes 491528 | tf_op jit(solution)/shard_map/ppermute | solution.py:172
  4.0 6.2 %collective-permute-start.1 = (bf16[8,3072]{1,0:T(8,128)(2,1)S(1)}, bf16[8,3072]{1,0:T(8,128)(2,1)S(1)}, u32[]{:S(2)}, u32[]{:S(2)}) collective-permute-start(bf16[8,3072]{1,0:T(8,128)(2,1)S(1)} %copy-done.2), channel_id=1, source_target_pairs={{0,8},{1,9},{2,10},{3,11},{4,12},{5,13},{6,14},{7,15},{8,0},{9,1},... | collective-permute-start | bytes 147464 | tf_op jit(solution)/shard_map/ppermute | solution.py:172
  7.1 6.0 %collective-permute-start = (bf16[8,3072]{1,0:T(8,128)(2,1)S(1)}, bf16[8,3072]{1,0:T(8,128)(2,1)S(1)}, u32[]{:S(2)}, u32[]{:S(2)}) collective-permute-start(bf16[8,3072]{1,0:T(8,128)(2,1)S(1)} %copy-done.2), channel_id=1, source_target_pairs={{0,12},{1,13},{2,14},{3,15},{4,8},{5,9},{6,10},{7,11},{8,4},{9,5},... | collective-permute-start | bytes 147464 | tf_op jit(solution)/shard_map/ppermute | solution.py:172
  8.4 4.6 %collective-permute-start.3 = (bf16[8,3072]{1,0:T(8,128)(2,1)S(1)}, bf16[8,3072]{1,0:T(8,128)(2,1)S(1)}, u32[]{:S(2)}, u32[]{:S(2)}) collective-permute-start(bf16[8,3072]{1,0:T(8,128)(2,1)S(1)} %copy-done.2), channel_id=1, source_target_pairs={{0,4},{1,5},{2,6},{3,7},{4,0},{5,1},{6,2},{7,3},{8,12},{9,13},{10,... | collective-permute-start | bytes 147464 | tf_op jit(solution)/shard_map/ppermute | solution.py:172
  9.6 3.5 %collective-permute-start.5 = (bf16[208,1024]{1,0:T(8,128)(2,1)S(1)}, bf16[208,1024]{1,0:T(8,128)(2,1)S(1)}, u32[]{:S(2)}, u32[]{:S(2)}) collective-permute-start(bf16[208,1024]{1,0:T(8,128)(2,1)S(1)} %shard_map.66.near_bundle), channel_id=1, source_target_pairs={{0,1},{1,0},{2,3},{3,2},{4,5},{5,4},{6,7},{7,6},{8,9},{9,8},{10,11... | collective-permute-start | bytes 1277960 | tf_op jit(solution)/shard_map/ppermute | solution.py:172
  10.2 2.9 %collective-permute-start.6 = (bf16[80,1024]{1,0:T(8,128)(2,1)S(1)}, bf16[80,1024]{1,0:T(8,128)(2,1)S(1)}, u32[]{:S(2)}, u32[]{:S(2)}) collective-permute-start(bf16[80,1024]{1,0:T(8,128)(2,1)S(1)} %collective-permute-done.4.near_rest), channel_id=1, source_target_pairs={{0,1},{1,0},{2,3},{3,2},{4,5},{5,4},{6,7},{7,6},{8,9},{9,8},{10,11... | collective-permute-start | bytes 491528 | tf_op jit(solution)/shard_map/ppermute | solution.py:172
  13.8 6.4 %collective-permute-start.7 = (bf16[8,3200]{1,0:T(8,128)(2,1)S(1)}, bf16[8,3200]{1,0:T(8,128)(2,1)S(1)}, u32[]{:S(2)}, u32[]{:S(2)}) collective-permute-start(bf16[8,3200]{1,0:T(8,128)(2,1)S(1)} %get-tuple-element.14), channel_id=1, source_target_pairs={{0,8},{1,9},{2,10},{3,11},{4,12},{5,13},{6,14},{7,15},{8,0},{9,1},... | collective-permute-start | bytes 153608 | tf_op jit(solution)/shard_map/ppermute | solution.py:172
  15.2 6.1 %collective-permute-start.8 = (bf16[8,3200]{1,0:T(8,128)(2,1)S(1)}, bf16[8,3200]{1,0:T(8,128)(2,1)S(1)}, u32[]{:S(2)}, u32[]{:S(2)}) collective-permute-start(bf16[8,3200]{1,0:T(8,128)(2,1)S(1)} %get-tuple-element.15), channel_id=1, source_target_pairs={{0,12},{1,13},{2,14},{3,15},{4,8},{5,9},{6,10},{7,11},{8,4},{9,5},... | collective-permute-start | bytes 153608 | tf_op jit(solution)/shard_map/ppermute | solution.py:172
  16.5 4.9 %collective-permute-start.9 = (bf16[8,3200]{1,0:T(8,128)(2,1)S(1)}, bf16[8,3200]{1,0:T(8,128)(2,1)S(1)}, u32[]{:S(2)}, u32[]{:S(2)}) collective-permute-start(bf16[8,3200]{1,0:T(8,128)(2,1)S(1)} %get-tuple-element.16), channel_id=1, source_target_pairs={{0,4},{1,5},{2,6},{3,7},{4,0},{5,1},{6,2},{7,3},{8,12},{9,13},{10,... | collective-permute-start | bytes 153608 | tf_op jit(solution)/shard_map/ppermute | solution.py:172

commit v6 on v5

--- a/solution.py
+++ b/solution.py
@@ -188,8 +188,8 @@
     far = size // near
     local_rows = queries.shape[0]
     slab, row_width = prefix_keys.shape
-    far_offsets = [near * i for i in range(far)]
-    far_order = far_offsets[:0:-1]
+    far_offsets = [0] + [near * i | 1 for i in range(1, far)]
+    far_order = far_offsets[2:] + far_offsets[1:2]
     vmem = pl.BlockSpec(memory_space=pltpu.VMEM)
     hbm = pl.BlockSpec(memory_space=pltpu.HBM)
     params = pltpu.CompilerParams(vmem_limit_bytes=16 * 2**20)
@@ -209,8 +209,9 @@
     key_pieces, rest_pieces = {0: prefix_keys}, {0: own_rest}
     for bit in reversed(range(1, near_bits)):
         for offset in list(key_pieces):
-            key_pieces[offset ^ (1 << bit)] = swap(key_pieces[offset], 1 << bit)
-            rest_pieces[offset ^ (1 << bit)] = swap(rest_pieces[offset], 1 << bit)
+            step = 1 << bit
+            key_pieces[offset ^ step] = swap(key_pieces[offset], step)
+            rest_pieces[offset ^ step] = swap(rest_pieces[offset], step)
     block_offsets = list(key_pieces)
     sibling_offsets = [offset ^ 1 for offset in block_offsets]
     mask = pl.pallas_call(
@@ -224,7 +225,7 @@
     for offset in far_order:
         sent = queries
         if offset == far_order[-1]:
-            sent, key_pieces[near // 2] = after(sent, key_pieces[near // 2])
+            sent, key_pieces[block_offsets[-1]] = after(sent, key_pieces[block_offsets[-1]])
         all_queries[offset] = swap(sent, offset)
     gathered = pl.pallas_call(
         rows_kernel,
@@ -254,7 +255,7 @@
         compiler_params=params,
     )(*held(pltpu.VMEM, operands))
     parts = [partials[0]]
-    for offset in far_offsets[2:] + far_offsets[1:2]:
+    for offset in far_offsets[-1:] + far_offsets[1:-1]:
         parts.append(swap(partials[owner_offsets.index(offset)], offset))
     return pl.pallas_call(
         merge_kernel,

time: 22.5 us -> 21.8 us (0.969)
  the two profiles are of different devices: /device:TPU:0 before, /device:TPU:1 now
where the time goes in v6:
time: 21.8 us; the launch traced here: 21.7 us
  starting transfers between devices  12.8 us (59%)
  waiting for transfers between devices  5.92 us (27%)
  Pallas kernels  2.88 us (13%)
    ppermute x10, starting transfers between devices, swap(): lax.ppermute(x, 'rows', [(i, i ^ offset) for i in range(lax.axis_size('ro...  12.8 us
    ppermute x10, waiting for transfers between devices, swap(): lax.ppermute(x, 'rows', [(i, i ^ offset) for i in range(lax.axis_size('ro...  5.92 us
    pallas_call x1, Pallas kernels, shards(): pl.pallas_call(rest_kernel, out_shape=pltpu.VMEM((slab + 2 * local_rows,...  0.93 us
    pallas_call x1, Pallas kernels, shards(): pl.pallas_call(merge_kernel, out_shape=jax.ShapeDtypeStruct((local_rows,...  0.93 us
    pallas_call x1, Pallas kernels, shards(): pl.pallas_call(functools.partial(attend_kernel, far, count, slab), out_sh...  0.7 us
  transfers between devices with their start and end apart: 10, of which 3 were waited for; matrix products, arithmetic and copies ran while one was open for 0% of the time, Pallas kernels for 6%

profile of v6, /device:TPU:1, one launch (start us, length us, event | category | flops | bytes accessed | tf_op | source)
XLA Modules:
  0.0 21.7 jit_solution(2940630483336402397)
XLA Ops:
  0.0 2.1 %collective-permute-start.2 = (bf16[64,1024]{1,0:T(8,128)(2,1)}, bf16[64,1024]{1,0:T(8,128)(2,1)S(1)}, u32[]{:S(2)}, u32[]{:S(2)}) collective-permute-start(bf16[64,1024]{1,0:T(8,128)(2,1)} %refs_0_.3), channel_id=1, source_target_pairs={{0,2},{1,3},{2,0},{3,1},{4,6},{5,7},{6,4},{7,5},{8,10},{9,11},{10,... | collective-permute-start | bytes 393224 | tf_op jit(solution)/shard_map/ppermute | solution.py:172
  2.1 0.0 copy-start.2
  2.1 0.0 copy-start
  2.1 0.9 %shard_map.65.refs_2_ = bf16[80,1024]{1,0:T(8,128)(2,1)S(1)} custom-call(bf16[64,1024]{1,0:T(8,128)(2,1)} %prefix_values.1, bf16[64,128]{1,0:T(8,128)(2,1)} %bitcast.12, bf16[64,128]{1,0:T(8,128)(2,1)} %bitcast.13), custom_call_target="tpu_custom_call" | custom-call | tf_op jit(solution)/shard_map/pallas_call | solution.py:196
  3.0 0.0 copy-start.1
  3.0 0.1 collective-permute-start.4
  3.1 0.0 copy-done.2
  3.1 4.6 %collective-permute-start.1 = (bf16[8,3072]{1,0:T(8,128)(2,1)S(1)}, bf16[8,3072]{1,0:T(8,128)(2,1)S(1)}, u32[]{:S(2)}, u32[]{:S(2)}) collective-permute-start(bf16[8,3072]{1,0:T(8,128)(2,1)S(1)} %copy-done.2), channel_id=1, source_target_pairs={{0,13},{1,12},{2,15},{3,14},{4,9},{5,8},{6,11},{7,10},{8,5},{9,4},... | collective-permute-start | bytes 147464 | tf_op jit(solution)/shard_map/ppermute | solution.py:172
  7.8 0.0 collective-permute-start
  7.8 0.0 collective-permute-done.2.refs_1_
  7.8 1.1 %collective-permute-start.3 = (bf16[8,3072]{1,0:T(8,128)(2,1)S(1)}, bf16[8,3072]{1,0:T(8,128)(2,1)S(1)}, u32[]{:S(2)}, u32[]{:S(2)}) collective-permute-start(bf16[8,3072]{1,0:T(8,128)(2,1)S(1)} %copy-done.2), channel_id=1, source_target_pairs={{0,5},{1,4},{2,7},{3,6},{4,1},{5,0},{6,3},{7,2},{8,13},{9,12},{10,... | collective-permute-start | bytes 147464 | tf_op jit(solution)/shard_map/ppermute | solution.py:172
  8.9 0.0 copy-done.1
  8.9 0.3 %shard_map.67.bias_ref = f32[32,320]{1,0:T(8,128)S(1)} custom-call(s32[1,128]{1,0:T(1,128)S(1)} %bitcast.11), custom_call_target="tpu_custom_call" | custom-call | tf_op jit(solution)/shard_map/pallas_call | solution.py:217
  9.2 0.0 copy-done
  9.2 0.1 collective-permute-start.5
  9.3 0.0 collective-permute-done.4.near_rest
  9.3 0.9 %collective-permute-start.6 = (bf16[80,1024]{1,0:T(8,128)(2,1)S(1)}, bf16[80,1024]{1,0:T(8,128)(2,1)S(1)}, u32[]{:S(2)}, u32[]{:S(2)}) collective-permute-start(bf16[80,1024]{1,0:T(8,128)(2,1)S(1)} %collective-permute-done.4.near_rest), channel_id=1, source_target_pairs={{0,1},{1,0},{2,3},{3,2},{4,5},{5,4},{6,7},{7,6},{8,9},{9,8},{10,11... | collective-permute-start | bytes 491528 | tf_op jit(solution)/shard_map/ppermute | solution.py:172
  10.2 0.0 collective-permute-done.1.refs_2_
  10.2 1.9 %collective-permute-done.refs_1_ = bf16[8,3072]{1,0:T(8,128)(2,1)S(1)} collective-permute-done((bf16[8,3072]{1,0:T(8,128)(2,1)S(1)}, bf16[8,3072]{1,0:T(8,128)(2,1)S(1)}, u32[]{:S(2)}, u32[]{:S(2)}) %collective-permute-start) | collective-permute-done | bytes 49184 | tf_op jit(solution)/shard_map/ppermute | solution.py:172
  12.2 0.0 collective-permute-done.3.refs_3_
  12.2 0.0 collective-permute-done.6.far_rest
  12.2 0.0 collective-permute-done.5.far_bundle
  12.2 0.7 %shard_map.68 = (bf16[8,3200]{1,0:T(8,128)(2,1)S(1)}, bf16[8,3200]{1,0:T(8,128)(2,1)S(1)}, bf16[8,3200]{1,0:T(8,128)(2,1)S(1)}, bf16[8,3200]{1,0:T(8,128)(2,1)S(1)}) custom-call(bf16[32,3072]{1,0:T(8,128)(2,1)S(1)} %shard_map.64.queries, bf16[208,1024]{1,0:T(8,128)(2,1)S(1)} %shard_map.66.near_bundle, bf16[80,1024]{1,0:T(8,128)(2,1)S(1)} %collective-permute-done.4.near_rest, ...), custom_call_target="tpu_custom_call" | custom-call | tf_op jit(solution)/shard_map/pallas_call | solution.py:250
  12.9 3.1 %collective-permute-start.7 = (bf16[8,3200]{1,0:T(8,128)(2,1)S(1)}, bf16[8,3200]{1,0:T(8,128)(2,1)S(1)}, u32[]{:S(2)}, u32[]{:S(2)}) collective-permute-start(bf16[8,3200]{1,0:T(8,128)(2,1)S(1)} %get-tuple-element.14), channel_id=1, source_target_pairs={{0,13},{1,12},{2,15},{3,14},{4,9},{5,8},{6,11},{7,10},{8,5},{9,4},... | collective-permute-start | bytes 153608 | tf_op jit(solution)/shard_map/ppermute | solution.py:172
  16.0 0.0 collective-permute-start.8
  16.0 0.8 %collective-permute-start.9 = (bf16[8,3200]{1,0:T(8,128)(2,1)S(1)}, bf16[8,3200]{1,0:T(8,128)(2,1)S(1)}, u32[]{:S(2)}, u32[]{:S(2)}) collective-permute-start(bf16[8,3200]{1,0:T(8,128)(2,1)S(1)} %get-tuple-element.16), channel_id=1, source_target_pairs={{0,9},{1,8},{2,11},{3,10},{4,13},{5,12},{6,15},{7,14},{8,1},{9,0},... | collective-permute-start | bytes 153608 | tf_op jit(solution)/shard_map/ppermute | solution.py:172
  16.8 2.1 %collective-permute-done.7.refs_1_ = bf16[8,3200]{1,0:T(8,128)(2,1)S(1)} collective-permute-done((bf16[8,3200]{1,0:T(8,128)(2,1)S(1)}, bf16[8,3200]{1,0:T(8,128)(2,1)S(1)}, u32[]{:S(2)}, u32[]{:S(2)}) %collective-permute-start.7) | collective-permute-done | bytes 51232 | tf_op jit(solution)/shard_map/ppermute | solution.py:172
  18.9 1.8 %collective-permute-done.8.refs_2_ = bf16[8,3200]{1,0:T(8,128)(2,1)S(1)} collective-permute-done((bf16[8,3200]{1,0:T(8,128)(2,1)S(1)}, bf16[8,3200]{1,0:T(8,128)(2,1)S(1)}, u32[]{:S(2)}, u32[]{:S(2)}) %collective-permute-start.8) | collective-permute-done | bytes 51232 | tf_op jit(solution)/shard_map/ppermute | solution.py:172
  20.8 0.0 collective-permute-done.9.refs_3_
  20.8 0.9 %shard_map.69 = bf16[8,3072]{1,0:T(8,128)(2,1)} custom-call(bf16[8,3200]{1,0:T(8,128)(2,1)S(1)} %get-tuple-element.13.refs_0_, bf16[8,3200]{1,0:T(8,128)(2,1)S(1)} %collective-permute-done.7.refs_1_, bf16[8,3200]{1,0:T(8,128)(2,1)S(1)} %collective-permute-done.8.refs_2_, bf16[8,3200]{1,0:T(8,128)(2,1)S(1)} %collective-permute-done.9.refs_3_), custom_call_target="tpu_custom_call" | custom-call | tf_op jit(solution)/shard_map/pallas_call | solution.py:260
  (2 shorter events, 0.0 us)
Async XLA Ops:
  0.0 7.8 %collective-permute-start.2 = (bf16[64,1024]{1,0:T(8,128)(2,1)}, bf16[64,1024]{1,0:T(8,128)(2,1)S(1)}, u32[]{:S(2)}, u32[]{:S(2)}) collective-permute-start(bf16[64,1024]{1,0:T(8,128)(2,1)} %refs_0_.3), channel_id=1, source_target_pairs={{0,2},{1,3},{2,0},{3,1},{4,6},{5,7},{6,4},{7,5},{8,10},{9,11},{10,... | collective-permute-start | bytes 393224 | tf_op jit(solution)/shard_map/ppermute | solution.py:172
  2.1 1.0 %copy-start.2 = (bf16[8,3072]{1,0:T(8,128)(2,1)S(1)}, bf16[8,3072]{1,0:T(8,128)(2,1)}, u32[]{:S(2)}) copy-start(bf16[8,3072]{1,0:T(8,128)(2,1)} %refs_0_.2) | copy-start | bytes 147460
  2.1 7.1 %copy-start = (bf16[64,1024]{1,0:T(8,128)(2,1)S(1)}, bf16[64,1024]{1,0:T(8,128)(2,1)}, u32[]{:S(2)}) copy-start(bf16[64,1024]{1,0:T(8,128)(2,1)} %refs_0_.3) | copy-start | bytes 393220
  3.0 5.9 %copy-start.1 = (s32[128]{0:T(128)S(1)}, s32[128]{0:T(128)}, u32[]{:S(2)}) copy-start(s32[128]{0:T(128)} %param.11) | copy-start | bytes 1540
  3.0 6.3 %collective-permute-start.4 = (bf16[80,1024]{1,0:T(8,128)(2,1)S(1)}, bf16[80,1024]{1,0:T(8,128)(2,1)S(1)}, u32[]{:S(2)}, u32[]{:S(2)}) collective-permute-start(bf16[80,1024]{1,0:T(8,128)(2,1)S(1)} %shard_map.65.refs_2_), channel_id=1, source_target_pairs={{0,2},{1,3},{2,0},{3,1},{4,6},{5,7},{6,4},{7,5},{8,10},{9,11},{10,... | collective-permute-start | bytes 491528 | tf_op jit(solution)/shard_map/ppermute | solution.py:172
  3.1 7.1 %collective-permute-start.1 = (bf16[8,3072]{1,0:T(8,128)(2,1)S(1)}, bf16[8,3072]{1,0:T(8,128)(2,1)S(1)}, u32[]{:S(2)}, u32[]{:S(2)}) collective-permute-start(bf16[8,3072]{1,0:T(8,128)(2,1)S(1)} %copy-done.2), channel_id=1, source_target_pairs={{0,13},{1,12},{2,15},{3,14},{4,9},{5,8},{6,11},{7,10},{8,5},{9,4},... | collective-permute-start | bytes 147464 | tf_op jit(solution)/shard_map/ppermute | solution.py:172
  7.8 4.4 %collective-permute-start = (bf16[8,3072]{1,0:T(8,128)(2,1)S(1)}, bf16[8,3072]{1,0:T(8,128)(2,1)S(1)}, u32[]{:S(2)}, u32[]{:S(2)}) collective-permute-start(bf16[8,3072]{1,0:T(8,128)(2,1)S(1)} %copy-done.2), channel_id=1, source_target_pairs={{0,9},{1,8},{2,11},{3,10},{4,13},{5,12},{6,15},{7,14},{8,1},{9,0},... | collective-permute-start | bytes 147464 | tf_op jit(solution)/shard_map/ppermute | solution.py:172
  7.8 4.4 %collective-permute-start.3 = (bf16[8,3072]{1,0:T(8,128)(2,1)S(1)}, bf16[8,3072]{1,0:T(8,128)(2,1)S(1)}, u32[]{:S(2)}, u32[]{:S(2)}) collective-permute-start(bf16[8,3072]{1,0:T(8,128)(2,1)S(1)} %copy-done.2), channel_id=1, source_target_pairs={{0,5},{1,4},{2,7},{3,6},{4,1},{5,0},{6,3},{7,2},{8,13},{9,12},{10,... | collective-permute-start | bytes 147464 | tf_op jit(solution)/shard_map/ppermute | solution.py:172
  9.2 3.0 %collective-permute-start.5 = (bf16[208,1024]{1,0:T(8,128)(2,1)S(1)}, bf16[208,1024]{1,0:T(8,128)(2,1)S(1)}, u32[]{:S(2)}, u32[]{:S(2)}) collective-permute-start(bf16[208,1024]{1,0:T(8,128)(2,1)S(1)} %shard_map.66.near_bundle), channel_id=1, source_target_pairs={{0,1},{1,0},{2,3},{3,2},{4,5},{5,4},{6,7},{7,6},{8,9},{9,8},{10,11... | collective-permute-start | bytes 1277960 | tf_op jit(solution)/shard_map/ppermute | solution.py:172
  9.3 2.9 %collective-permute-start.6 = (bf16[80,1024]{1,0:T(8,128)(2,1)S(1)}, bf16[80,1024]{1,0:T(8,128)(2,1)S(1)}, u32[]{:S(2)}, u32[]{:S(2)}) collective-permute-start(bf16[80,1024]{1,0:T(8,128)(2,1)S(1)} %collective-permute-done.4.near_rest), channel_id=1, source_target_pairs={{0,1},{1,0},{2,3},{3,2},{4,5},{5,4},{6,7},{7,6},{8,9},{9,8},{10,11... | collective-permute-start | bytes 491528 | tf_op jit(solution)/shard_map/ppermute | solution.py:172
  12.9 6.0 %collective-permute-start.7 = (bf16[8,3200]{1,0:T(8,128)(2,1)S(1)}, bf16[8,3200]{1,0:T(8,128)(2,1)S(1)}, u32[]{:S(2)}, u32[]{:S(2)}) collective-permute-start(bf16[8,3200]{1,0:T(8,128)(2,1)S(1)} %get-tuple-element.14), channel_id=1, source_target_pairs={{0,13},{1,12},{2,15},{3,14},{4,9},{5,8},{6,11},{7,10},{8,5},{9,4},... | collective-permute-start | bytes 153608 | tf_op jit(solution)/shard_map/ppermute | solution.py:172
  16.0 4.8 %collective-permute-start.8 = (bf16[8,3200]{1,0:T(8,128)(2,1)S(1)}, bf16[8,3200]{1,0:T(8,128)(2,1)S(1)}, u32[]{:S(2)}, u32[]{:S(2)}) collective-permute-start(bf16[8,3200]{1,0:T(8,128)(2,1)S(1)} %get-tuple-element.15), channel_id=1, source_target_pairs={{0,5},{1,4},{2,7},{3,6},{4,1},{5,0},{6,3},{7,2},{8,13},{9,12},{10,... | collective-permute-start | bytes 153608 | tf_op jit(solution)/shard_map/ppermute | solution.py:172
  16.0 4.8 %collective-permute-start.9 = (bf16[8,3200]{1,0:T(8,128)(2,1)S(1)}, bf16[8,3200]{1,0:T(8,128)(2,1)S(1)}, u32[]{:S(2)}, u32[]{:S(2)}) collective-permute-start(bf16[8,3200]{1,0:T(8,128)(2,1)S(1)} %get-tuple-element.16), channel_id=1, source_target_pairs={{0,9},{1,8},{2,11},{3,10},{4,13},{5,12},{6,15},{7,14},{8,1},{9,0},... | collective-permute-start | bytes 153608 | tf_op jit(solution)/shard_map/ppermute | solution.py:172

commit v7 on v6

--- a/solution.py
+++ b/solution.py
@@ -15,21 +15,18 @@
 WIDTH = QUERY_HEADS * HEAD_DIM
 LANES = 128
 STRIDE = 32
-CHUNKS = 4
 NT = (((1,), (1,)), ((), ()))
+SCHEDULE_LAST = pl.CostEstimate(flops=3 * 10**10, bytes_accessed=10**8, transcendentals=0)
 HEADS = [slice(head * HEAD_DIM, (head + 1) * HEAD_DIM) for head in range(QUERY_HEADS)]
 
 
 def rest_kernel(prefix_values, tree_keys, tree_values, rest, tree_scratch, sems):
     slab = prefix_values.shape[0]
-    chunk = slab // CHUNKS
     copies = [
         pltpu.make_async_copy(tree_keys, tree_scratch.at[0], sems.at[0]),
         pltpu.make_async_copy(tree_values, tree_scratch.at[1], sems.at[1]),
+        pltpu.make_async_copy(prefix_values, rest.at[:slab], sems.at[2]),
     ]
-    for place in range(CHUNKS):
-        rows = slice(place * chunk, (place + 1) * chunk)
-        copies.append(pltpu.make_async_copy(prefix_values.at[rows], rest.at[rows], sems.at[2 + place]))
     for copy in copies:
         copy.start()
     for copy in copies:
@@ -133,14 +130,14 @@
             stats = jnp.where(here, level[g * rows : (g + 1) * rows], stats)
             for owner in range(owners):
                 first = g * rows + owner * local_rows
-                outs[owner][:, HEADS[query_head]] = weighted[first : first + local_rows].astype(jnp.bfloat16)
+                outs[owner][:, HEADS[query_head]] = weighted[first : first + local_rows].astype(outs[owner].dtype)
     high = stats.astype(jnp.bfloat16).astype(jnp.float32)
     left = stats - high
     middle = left.astype(jnp.bfloat16).astype(jnp.float32)
     low = left - middle
     sent = jnp.where(lane < STRIDE, high, jnp.where(lane < 2 * STRIDE, middle, low))
     for owner in range(owners):
-        outs[owner][:, WIDTH:] = sent[owner * local_rows : (owner + 1) * local_rows].astype(jnp.bfloat16)
+        outs[owner][:, WIDTH:] = sent[owner * local_rows : (owner + 1) * local_rows].astype(outs[owner].dtype)
 
 
 def merge_kernel(*refs):
@@ -154,13 +151,10 @@
     whole = 1.0 / functools.reduce(jnp.add, shares)
     shares = [share * whole for share in shares]
     for head in range(QUERY_HEADS):
-        total = functools.reduce(
-            jnp.add,
-            [
-                share[:, head : head + 1] * part[:, HEADS[head]].astype(jnp.float32)
-                for share, part in zip(shares, parts)
-            ],
-        )
+        own = parts[0][:, HEADS[head]].astype(jnp.float32)
+        total = own
+        for share, part in zip(shares[1:], parts[1:]):
+            total = total + share[:, head : head + 1] * (part[:, HEADS[head]].astype(jnp.float32) - own)
         out[:, HEADS[head]] = total.astype(out.dtype)
 
 
@@ -200,7 +194,7 @@
         out_specs=vmem,
         scratch_shapes=[
             pltpu.VMEM((2, KV_HEADS * local_rows, HEAD_DIM), tree_keys.dtype),
-            pltpu.SemaphoreType.DMA((2 + CHUNKS,)),
+            pltpu.SemaphoreType.DMA((3,)),
         ],
         compiler_params=params,
     )(*held(pltpu.HBM, [prefix_values, by_head(tree_keys), by_head(tree_values)]))
@@ -233,7 +227,7 @@
         in_specs=[vmem] * far,
         out_specs=vmem,
         compiler_params=params,
-        cost_estimate=pl.CostEstimate(flops=10999999999, bytes_accessed=36000000, transcendentals=0),
+        cost_estimate=SCHEDULE_LAST,
     )(*held(pltpu.VMEM, [all_queries[offset] for offset in owner_offsets]))
     blocks = list(key_pieces.values()) + list(rest_pieces.values())[:-1]
     bundle = pl.pallas_call(
@@ -249,7 +243,10 @@
     operands = [gathered, bundle, last_rest, far_bundle, far_rest, mask]
     partials = pl.pallas_call(
         functools.partial(attend_kernel, far, count, slab),
-        out_shape=[pltpu.VMEM((local_rows, WIDTH + LANES), jnp.bfloat16)] * far,
+        out_shape=[
+            pltpu.VMEM((local_rows, WIDTH + LANES), jnp.bfloat16 if offset else jnp.float32)
+            for offset in owner_offsets
+        ],
         in_specs=[vmem] * len(operands),
         out_specs=[vmem] * far,
         compiler_params=params,

time: 21.8 us -> 21.8 us (level)
  no operation moved by 1% of the time
where the time goes in v7:
time: 21.8 us; the launch traced here: 21.7 us
  starting transfers between devices  12.7 us (58%)
  waiting for transfers between devices  5.95 us (27%)
  Pallas kernels  2.93 us (13%)
    ppermute x10, starting transfers between devices, swap(): lax.ppermute(x, 'rows', [(i, i ^ offset) for i in range(lax.axis_size('ro...  12.7 us
    ppermute x10, waiting for transfers between devices, swap(): lax.ppermute(x, 'rows', [(i, i ^ offset) for i in range(lax.axis_size('ro...  5.95 us
    pallas_call x1, Pallas kernels, shards(): pl.pallas_call(rest_kernel, out_shape=pltpu.VMEM((slab + 2 * local_rows,...  1.01 us
    pallas_call x1, Pallas kernels, shards(): pl.pallas_call(merge_kernel, out_shape=jax.ShapeDtypeStruct((local_rows,...  0.9 us
    pallas_call x1, Pallas kernels, shards(): pl.pallas_call(functools.partial(attend_kernel, far, count, slab), out_sh...  0.7 us
  transfers between devices with their start and end apart: 10, of which 3 were waited for; matrix products, arithmetic and copies ran while one was open for 0% of the time, Pallas kernels for 6%

profile of v7, /device:TPU:1, one launch (start us, length us, event | category | flops | bytes accessed | tf_op | source)
XLA Modules:
  0.0 21.7 jit_solution(10477315766269579953)
XLA Ops:
  0.0 2.1 %collective-permute-start.2 = (bf16[64,1024]{1,0:T(8,128)(2,1)}, bf16[64,1024]{1,0:T(8,128)(2,1)S(1)}, u32[]{:S(2)}, u32[]{:S(2)}) collective-permute-start(bf16[64,1024]{1,0:T(8,128)(2,1)} %refs_0_.3), channel_id=1, source_target_pairs={{0,2},{1,3},{2,0},{3,1},{4,6},{5,7},{6,4},{7,5},{8,10},{9,11},{10,... | collective-permute-start | bytes 393224 | tf_op jit(solution)/shard_map/ppermute | solution.py:166
  2.1 0.0 copy-start.2
  2.1 0.0 copy-start
  2.1 1.0 %shard_map.65.refs_2_ = bf16[80,1024]{1,0:T(8,128)(2,1)S(1)} custom-call(bf16[64,1024]{1,0:T(8,128)(2,1)} %prefix_values.1, bf16[64,128]{1,0:T(8,128)(2,1)} %bitcast.12, bf16[64,128]{1,0:T(8,128)(2,1)} %bitcast.13), custom_call_target="tpu_custom_call" | custom-call | tf_op jit(solution)/shard_map/pallas_call | solution.py:190
  3.1 0.0 copy-start.1
  3.1 0.1 collective-permute-start.4
  3.2 0.0 copy-done.2
  3.2 4.6 %collective-permute-start.1 = (bf16[8,3072]{1,0:T(8,128)(2,1)S(1)}, bf16[8,3072]{1,0:T(8,128)(2,1)S(1)}, u32[]{:S(2)}, u32[]{:S(2)}) collective-permute-start(bf16[8,3072]{1,0:T(8,128)(2,1)S(1)} %copy-done.2), channel_id=1, source_target_pairs={{0,13},{1,12},{2,15},{3,14},{4,9},{5,8},{6,11},{7,10},{8,5},{9,4},... | collective-permute-start | bytes 147464 | tf_op jit(solution)/shard_map/ppermute | solution.py:166
  7.8 0.0 collective-permute-start
  7.8 0.0 collective-permute-done.2.refs_1_
  7.8 1.0 %collective-permute-start.3 = (bf16[8,3072]{1,0:T(8,128)(2,1)S(1)}, bf16[8,3072]{1,0:T(8,128)(2,1)S(1)}, u32[]{:S(2)}, u32[]{:S(2)}) collective-permute-start(bf16[8,3072]{1,0:T(8,128)(2,1)S(1)} %copy-done.2), channel_id=1, source_target_pairs={{0,5},{1,4},{2,7},{3,6},{4,1},{5,0},{6,3},{7,2},{8,13},{9,12},{10,... | collective-permute-start | bytes 147464 | tf_op jit(solution)/shard_map/ppermute | solution.py:166
  8.8 0.0 copy-done.1
  8.8 0.3 %shard_map.67.bias_ref = f32[32,320]{1,0:T(8,128)S(1)} custom-call(s32[1,128]{1,0:T(1,128)S(1)} %bitcast.11), custom_call_target="tpu_custom_call" | custom-call | tf_op jit(solution)/shard_map/pallas_call | solution.py:211
  9.1 0.0 copy-done
  9.2 0.1 collective-permute-start.5
  9.2 0.0 collective-permute-done.4.near_rest
  9.2 1.0 %collective-permute-start.6 = (bf16[80,1024]{1,0:T(8,128)(2,1)S(1)}, bf16[80,1024]{1,0:T(8,128)(2,1)S(1)}, u32[]{:S(2)}, u32[]{:S(2)}) collective-permute-start(bf16[80,1024]{1,0:T(8,128)(2,1)S(1)} %collective-permute-done.4.near_rest), channel_id=1, source_target_pairs={{0,1},{1,0},{2,3},{3,2},{4,5},{5,4},{6,7},{7,6},{8,9},{9,8},{10,11... | collective-permute-start | bytes 491528 | tf_op jit(solution)/shard_map/ppermute | solution.py:166
  10.2 0.0 collective-permute-done.1.refs_2_
  10.2 2.0 %collective-permute-done.refs_1_ = bf16[8,3072]{1,0:T(8,128)(2,1)S(1)} collective-permute-done((bf16[8,3072]{1,0:T(8,128)(2,1)S(1)}, bf16[8,3072]{1,0:T(8,128)(2,1)S(1)}, u32[]{:S(2)}, u32[]{:S(2)}) %collective-permute-start) | collective-permute-done | bytes 49184 | tf_op jit(solution)/shard_map/ppermute | solution.py:166
  12.3 0.0 collective-permute-done.3.refs_3_
  12.3 0.0 collective-permute-done.6.far_rest
  12.3 0.0 collective-permute-done.5.far_bundle
  12.3 0.7 %shard_map.68 = (f32[8,3200]{1,0:T(8,128)S(1)}, bf16[8,3200]{1,0:T(8,128)(2,1)S(1)}, bf16[8,3200]{1,0:T(8,128)(2,1)S(1)}, bf16[8,3200]{1,0:T(8,128)(2,1)S(1)}) custom-call(bf16[32,3072]{1,0:T(8,128)(2,1)S(1)} %shard_map.64.queries, bf16[208,1024]{1,0:T(8,128)(2,1)S(1)} %shard_map.66.near_bundle, bf16[80,1024]{1,0:T(8,128)(2,1)S(1)} %collective-permute-done.4.near_rest, ...), custom_call_target="tpu_custom_call" | custom-call | tf_op jit(solution)/shard_map/pallas_call | solution.py:244
  13.0 3.1 %collective-permute-start.7 = (bf16[8,3200]{1,0:T(8,128)(2,1)S(1)}, bf16[8,3200]{1,0:T(8,128)(2,1)S(1)}, u32[]{:S(2)}, u32[]{:S(2)}) collective-permute-start(bf16[8,3200]{1,0:T(8,128)(2,1)S(1)} %get-tuple-element.14), channel_id=1, source_target_pairs={{0,13},{1,12},{2,15},{3,14},{4,9},{5,8},{6,11},{7,10},{8,5},{9,4},... | collective-permute-start | bytes 153608 | tf_op jit(solution)/shard_map/ppermute | solution.py:166
  16.1 0.0 collective-permute-start.8
  16.1 0.8 %collective-permute-start.9 = (bf16[8,3200]{1,0:T(8,128)(2,1)S(1)}, bf16[8,3200]{1,0:T(8,128)(2,1)S(1)}, u32[]{:S(2)}, u32[]{:S(2)}) collective-permute-start(bf16[8,3200]{1,0:T(8,128)(2,1)S(1)} %get-tuple-element.16), channel_id=1, source_target_pairs={{0,9},{1,8},{2,11},{3,10},{4,13},{5,12},{6,15},{7,14},{8,1},{9,0},... | collective-permute-start | bytes 153608 | tf_op jit(solution)/shard_map/ppermute | solution.py:166
  16.9 2.1 %collective-permute-done.7.refs_1_ = bf16[8,3200]{1,0:T(8,128)(2,1)S(1)} collective-permute-done((bf16[8,3200]{1,0:T(8,128)(2,1)S(1)}, bf16[8,3200]{1,0:T(8,128)(2,1)S(1)}, u32[]{:S(2)}, u32[]{:S(2)}) %collective-permute-start.7) | collective-permute-done | bytes 51232 | tf_op jit(solution)/shard_map/ppermute | solution.py:166
  19.0 1.8 %collective-permute-done.8.refs_2_ = bf16[8,3200]{1,0:T(8,128)(2,1)S(1)} collective-permute-done((bf16[8,3200]{1,0:T(8,128)(2,1)S(1)}, bf16[8,3200]{1,0:T(8,128)(2,1)S(1)}, u32[]{:S(2)}, u32[]{:S(2)}) %collective-permute-start.8) | collective-permute-done | bytes 51232 | tf_op jit(solution)/shard_map/ppermute | solution.py:166
  20.8 0.0 collective-permute-done.9.refs_3_
  20.8 0.9 %shard_map.69 = bf16[8,3072]{1,0:T(8,128)(2,1)} custom-call(f32[8,3200]{1,0:T(8,128)S(1)} %get-tuple-element.13.refs_0_, bf16[8,3200]{1,0:T(8,128)(2,1)S(1)} %collective-permute-done.7.refs_1_, bf16[8,3200]{1,0:T(8,128)(2,1)S(1)} %collective-permute-done.8.refs_2_, bf16[8,3200]{1,0:T(8,128)(2,1)S(1)} %collective-permute-done.9.refs_3_), custom_call_target="tpu_custom_call" | custom-call | tf_op jit(solution)/shard_map/pallas_call | solution.py:257
  (2 shorter events, 0.0 us)
Async XLA Ops:
  0.0 7.8 %collective-permute-start.2 = (bf16[64,1024]{1,0:T(8,128)(2,1)}, bf16[64,1024]{1,0:T(8,128)(2,1)S(1)}, u32[]{:S(2)}, u32[]{:S(2)}) collective-permute-start(bf16[64,1024]{1,0:T(8,128)(2,1)} %refs_0_.3), channel_id=1, source_target_pairs={{0,2},{1,3},{2,0},{3,1},{4,6},{5,7},{6,4},{7,5},{8,10},{9,11},{10,... | collective-permute-start | bytes 393224 | tf_op jit(solution)/shard_map/ppermute | solution.py:166
  2.1 1.1 %copy-start.2 = (bf16[8,3072]{1,0:T(8,128)(2,1)S(1)}, bf16[8,3072]{1,0:T(8,128)(2,1)}, u32[]{:S(2)}) copy-start(bf16[8,3072]{1,0:T(8,128)(2,1)} %refs_0_.2) | copy-start | bytes 147460
  2.1 7.0 %copy-start = (bf16[64,1024]{1,0:T(8,128)(2,1)S(1)}, bf16[64,1024]{1,0:T(8,128)(2,1)}, u32[]{:S(2)}) copy-start(bf16[64,1024]{1,0:T(8,128)(2,1)} %refs_0_.3) | copy-start | bytes 393220
  3.1 5.7 %copy-start.1 = (s32[128]{0:T(128)S(1)}, s32[128]{0:T(128)}, u32[]{:S(2)}) copy-start(s32[128]{0:T(128)} %param.11) | copy-start | bytes 1540
  3.1 6.1 %collective-permute-start.4 = (bf16[80,1024]{1,0:T(8,128)(2,1)S(1)}, bf16[80,1024]{1,0:T(8,128)(2,1)S(1)}, u32[]{:S(2)}, u32[]{:S(2)}) collective-permute-start(bf16[80,1024]{1,0:T(8,128)(2,1)S(1)} %shard_map.65.refs_2_), channel_id=1, source_target_pairs={{0,2},{1,3},{2,0},{3,1},{4,6},{5,7},{6,4},{7,5},{8,10},{9,11},{10,... | collective-permute-start | bytes 491528 | tf_op jit(solution)/shard_map/ppermute | solution.py:166
  3.2 7.1 %collective-permute-start.1 = (bf16[8,3072]{1,0:T(8,128)(2,1)S(1)}, bf16[8,3072]{1,0:T(8,128)(2,1)S(1)}, u32[]{:S(2)}, u32[]{:S(2)}) collective-permute-start(bf16[8,3072]{1,0:T(8,128)(2,1)S(1)} %copy-done.2), channel_id=1, source_target_pairs={{0,13},{1,12},{2,15},{3,14},{4,9},{5,8},{6,11},{7,10},{8,5},{9,4},... | collective-permute-start | bytes 147464 | tf_op jit(solution)/shard_map/ppermute | solution.py:166
  7.8 4.4 %collective-permute-start = (bf16[8,3072]{1,0:T(8,128)(2,1)S(1)}, bf16[8,3072]{1,0:T(8,128)(2,1)S(1)}, u32[]{:S(2)}, u32[]{:S(2)}) collective-permute-start(bf16[8,3072]{1,0:T(8,128)(2,1)S(1)} %copy-done.2), channel_id=1, source_target_pairs={{0,9},{1,8},{2,11},{3,10},{4,13},{5,12},{6,15},{7,14},{8,1},{9,0},... | collective-permute-start | bytes 147464 | tf_op jit(solution)/shard_map/ppermute | solution.py:166
  7.8 4.4 %collective-permute-start.3 = (bf16[8,3072]{1,0:T(8,128)(2,1)S(1)}, bf16[8,3072]{1,0:T(8,128)(2,1)S(1)}, u32[]{:S(2)}, u32[]{:S(2)}) collective-permute-start(bf16[8,3072]{1,0:T(8,128)(2,1)S(1)} %copy-done.2), channel_id=1, source_target_pairs={{0,5},{1,4},{2,7},{3,6},{4,1},{5,0},{6,3},{7,2},{8,13},{9,12},{10,... | collective-permute-start | bytes 147464 | tf_op jit(solution)/shard_map/ppermute | solution.py:166
  9.2 3.1 %collective-permute-start.5 = (bf16[208,1024]{1,0:T(8,128)(2,1)S(1)}, bf16[208,1024]{1,0:T(8,128)(2,1)S(1)}, u32[]{:S(2)}, u32[]{:S(2)}) collective-permute-start(bf16[208,1024]{1,0:T(8,128)(2,1)S(1)} %shard_map.66.near_bundle), channel_id=1, source_target_pairs={{0,1},{1,0},{2,3},{3,2},{4,5},{5,4},{6,7},{7,6},{8,9},{9,8},{10,11... | collective-permute-start | bytes 1277960 | tf_op jit(solution)/shard_map/ppermute | solution.py:166
  9.2 3.0 %collective-permute-start.6 = (bf16[80,1024]{1,0:T(8,128)(2,1)S(1)}, bf16[80,1024]{1,0:T(8,128)(2,1)S(1)}, u32[]{:S(2)}, u32[]{:S(2)}) collective-permute-start(bf16[80,1024]{1,0:T(8,128)(2,1)S(1)} %collective-permute-done.4.near_rest), channel_id=1, source_target_pairs={{0,1},{1,0},{2,3},{3,2},{4,5},{5,4},{6,7},{7,6},{8,9},{9,8},{10,11... | collective-permute-start | bytes 491528 | tf_op jit(solution)/shard_map/ppermute | solution.py:166
  13.0 6.0 %collective-permute-start.7 = (bf16[8,3200]{1,0:T(8,128)(2,1)S(1)}, bf16[8,3200]{1,0:T(8,128)(2,1)S(1)}, u32[]{:S(2)}, u32[]{:S(2)}) collective-permute-start(bf16[8,3200]{1,0:T(8,128)(2,1)S(1)} %get-tuple-element.14), channel_id=1, source_target_pairs={{0,13},{1,12},{2,15},{3,14},{4,9},{5,8},{6,11},{7,10},{8,5},{9,4},... | collective-permute-start | bytes 153608 | tf_op jit(solution)/shard_map/ppermute | solution.py:166
  16.1 4.7 %collective-permute-start.8 = (bf16[8,3200]{1,0:T(8,128)(2,1)S(1)}, bf16[8,3200]{1,0:T(8,128)(2,1)S(1)}, u32[]{:S(2)}, u32[]{:S(2)}) collective-permute-start(bf16[8,3200]{1,0:T(8,128)(2,1)S(1)} %get-tuple-element.15), channel_id=1, source_target_pairs={{0,5},{1,4},{2,7},{3,6},{4,1},{5,0},{6,3},{7,2},{8,13},{9,12},{10,... | collective-permute-start | bytes 153608 | tf_op jit(solution)/shard_map/ppermute | solution.py:166
  16.1 4.7 %collective-permute-start.9 = (bf16[8,3200]{1,0:T(8,128)(2,1)S(1)}, bf16[8,3200]{1,0:T(8,128)(2,1)S(1)}, u32[]{:S(2)}, u32[]{:S(2)}) collective-permute-start(bf16[8,3200]{1,0:T(8,128)(2,1)S(1)} %get-tuple-element.16), channel_id=1, source_target_pairs={{0,9},{1,8},{2,11},{3,10},{4,13},{5,12},{6,15},{7,14},{8,1},{9,0},... | collective-permute-start | bytes 153608 | tf_op jit(solution)/shard_map/ppermute | solution.py:166

commit v8 on v6

--- a/solution.py
+++ b/solution.py
@@ -17,6 +17,7 @@
 STRIDE = 32
 CHUNKS = 4
 NT = (((1,), (1,)), ((), ()))
+SCHEDULE_LAST = pl.CostEstimate(flops=3 * 10**10, bytes_accessed=10**8, transcendentals=0)
 HEADS = [slice(head * HEAD_DIM, (head + 1) * HEAD_DIM) for head in range(QUERY_HEADS)]
 
 
@@ -133,14 +134,14 @@
             stats = jnp.where(here, level[g * rows : (g + 1) * rows], stats)
             for owner in range(owners):
                 first = g * rows + owner * local_rows
-                outs[owner][:, HEADS[query_head]] = weighted[first : first + local_rows].astype(jnp.bfloat16)
+                outs[owner][:, HEADS[query_head]] = weighted[first : first + local_rows].astype(outs[owner].dtype)
     high = stats.astype(jnp.bfloat16).astype(jnp.float32)
     left = stats - high
     middle = left.astype(jnp.bfloat16).astype(jnp.float32)
     low = left - middle
     sent = jnp.where(lane < STRIDE, high, jnp.where(lane < 2 * STRIDE, middle, low))
     for owner in range(owners):
-        outs[owner][:, WIDTH:] = sent[owner * local_rows : (owner + 1) * local_rows].astype(jnp.bfloat16)
+        outs[owner][:, WIDTH:] = sent[owner * local_rows : (owner + 1) * local_rows].astype(outs[owner].dtype)
 
 
 def merge_kernel(*refs):
@@ -233,7 +234,7 @@
         in_specs=[vmem] * far,
         out_specs=vmem,
         compiler_params=params,
-        cost_estimate=pl.CostEstimate(flops=10999999999, bytes_accessed=36000000, transcendentals=0),
+        cost_estimate=SCHEDULE_LAST,
     )(*held(pltpu.VMEM, [all_queries[offset] for offset in owner_offsets]))
     blocks = list(key_pieces.values()) + list(rest_pieces.values())[:-1]
     bundle = pl.pallas_call(
@@ -249,7 +250,10 @@
     operands = [gathered, bundle, last_rest, far_bundle, far_rest, mask]
     partials = pl.pallas_call(
         functools.partial(attend_kernel, far, count, slab),
-        out_shape=[pltpu.VMEM((local_rows, WIDTH + LANES), jnp.bfloat16)] * far,
+        out_shape=[
+            pltpu.VMEM((local_rows, WIDTH + LANES), jnp.bfloat16 if offset else jnp.float32)
+            for offset in owner_offsets
+        ],
         in_specs=[vmem] * len(operands),
         out_specs=[vmem] * far,
         compiler_params=params,

time: 21.8 us -> 21.8 us (level)
  no operation moved by 1% of the time
where the time goes in v8:
time: 21.8 us; the launch traced here: 21.7 us
  starting transfers between devices  12.8 us (59%)
  waiting for transfers between devices  5.92 us (27%)
  Pallas kernels  2.88 us (13%)
    ppermute x10, starting transfers between devices, swap(): lax.ppermute(x, 'rows', [(i, i ^ offset) for i in range(lax.axis_size('ro...  12.8 us
    ppermute x10, waiting for transfers between devices, swap(): lax.ppermute(x, 'rows', [(i, i ^ offset) for i in range(lax.axis_size('ro...  5.92 us
    pallas_call x1, Pallas kernels, shards(): pl.pallas_call(rest_kernel, out_shape=pltpu.VMEM((slab + 2 * local_rows,...  0.93 us
    pallas_call x1, Pallas kernels, shards(): pl.pallas_call(merge_kernel, out_shape=jax.ShapeDtypeStruct((local_rows,...  0.93 us
    pallas_call x1, Pallas kernels, shards(): pl.pallas_call(functools.partial(attend_kernel, far, count, slab), out_sh...  0.7 us
  transfers between devices with their start and end apart: 10, of which 3 were waited for; matrix products, arithmetic and copies ran while one was open for 0% of the time, Pallas kernels for 6%

profile of v8, /device:TPU:1, one launch (start us, length us, event | category | flops | bytes accessed | tf_op | source)
XLA Modules:
  0.0 21.7 jit_solution(2989486466358141365)
XLA Ops:
  0.0 2.1 %collective-permute-start.2 = (bf16[64,1024]{1,0:T(8,128)(2,1)}, bf16[64,1024]{1,0:T(8,128)(2,1)S(1)}, u32[]{:S(2)}, u32[]{:S(2)}) collective-permute-start(bf16[64,1024]{1,0:T(8,128)(2,1)} %refs_0_.3), channel_id=1, source_target_pairs={{0,2},{1,3},{2,0},{3,1},{4,6},{5,7},{6,4},{7,5},{8,10},{9,11},{10,... | collective-permute-start | bytes 393224 | tf_op jit(solution)/shard_map/ppermute | solution.py:173
  2.1 0.0 copy-start.2
  2.1 0.0 copy-start
  2.1 0.9 %shard_map.65.refs_2_ = bf16[80,1024]{1,0:T(8,128)(2,1)S(1)} custom-call(bf16[64,1024]{1,0:T(8,128)(2,1)} %prefix_values.1, bf16[64,128]{1,0:T(8,128)(2,1)} %bitcast.12, bf16[64,128]{1,0:T(8,128)(2,1)} %bitcast.13), custom_call_target="tpu_custom_call" | custom-call | tf_op jit(solution)/shard_map/pallas_call | solution.py:197
  3.0 0.0 copy-start.1
  3.0 0.1 collective-permute-start.4
  3.1 0.0 copy-done.2
  3.1 4.6 %collective-permute-start.1 = (bf16[8,3072]{1,0:T(8,128)(2,1)S(1)}, bf16[8,3072]{1,0:T(8,128)(2,1)S(1)}, u32[]{:S(2)}, u32[]{:S(2)}) collective-permute-start(bf16[8,3072]{1,0:T(8,128)(2,1)S(1)} %copy-done.2), channel_id=1, source_target_pairs={{0,13},{1,12},{2,15},{3,14},{4,9},{5,8},{6,11},{7,10},{8,5},{9,4},... | collective-permute-start | bytes 147464 | tf_op jit(solution)/shard_map/ppermute | solution.py:173
  7.8 0.0 collective-permute-start
  7.8 0.0 collective-permute-done.2.refs_1_
  7.8 1.1 %collective-permute-start.3 = (bf16[8,3072]{1,0:T(8,128)(2,1)S(1)}, bf16[8,3072]{1,0:T(8,128)(2,1)S(1)}, u32[]{:S(2)}, u32[]{:S(2)}) collective-permute-start(bf16[8,3072]{1,0:T(8,128)(2,1)S(1)} %copy-done.2), channel_id=1, source_target_pairs={{0,5},{1,4},{2,7},{3,6},{4,1},{5,0},{6,3},{7,2},{8,13},{9,12},{10,... | collective-permute-start | bytes 147464 | tf_op jit(solution)/shard_map/ppermute | solution.py:173
  8.9 0.0 copy-done.1
  8.9 0.3 %shard_map.67.bias_ref = f32[32,320]{1,0:T(8,128)S(1)} custom-call(s32[1,128]{1,0:T(1,128)S(1)} %bitcast.11), custom_call_target="tpu_custom_call" | custom-call | tf_op jit(solution)/shard_map/pallas_call | solution.py:218
  9.2 0.0 copy-done
  9.2 0.1 collective-permute-start.5
  9.3 0.0 collective-permute-done.4.near_rest
  9.3 0.9 %collective-permute-start.6 = (bf16[80,1024]{1,0:T(8,128)(2,1)S(1)}, bf16[80,1024]{1,0:T(8,128)(2,1)S(1)}, u32[]{:S(2)}, u32[]{:S(2)}) collective-permute-start(bf16[80,1024]{1,0:T(8,128)(2,1)S(1)} %collective-permute-done.4.near_rest), channel_id=1, source_target_pairs={{0,1},{1,0},{2,3},{3,2},{4,5},{5,4},{6,7},{7,6},{8,9},{9,8},{10,11... | collective-permute-start | bytes 491528 | tf_op jit(solution)/shard_map/ppermute | solution.py:173
  10.2 0.0 collective-permute-done.1.refs_2_
  10.2 1.9 %collective-permute-done.refs_1_ = bf16[8,3072]{1,0:T(8,128)(2,1)S(1)} collective-permute-done((bf16[8,3072]{1,0:T(8,128)(2,1)S(1)}, bf16[8,3072]{1,0:T(8,128)(2,1)S(1)}, u32[]{:S(2)}, u32[]{:S(2)}) %collective-permute-start) | collective-permute-done | bytes 49184 | tf_op jit(solution)/shard_map/ppermute | solution.py:173
  12.2 0.0 collective-permute-done.3.refs_3_
  12.2 0.0 collective-permute-done.6.far_rest
  12.2 0.0 collective-permute-done.5.far_bundle
  12.2 0.7 %shard_map.68 = (f32[8,3200]{1,0:T(8,128)S(1)}, bf16[8,3200]{1,0:T(8,128)(2,1)S(1)}, bf16[8,3200]{1,0:T(8,128)(2,1)S(1)}, bf16[8,3200]{1,0:T(8,128)(2,1)S(1)}) custom-call(bf16[32,3072]{1,0:T(8,128)(2,1)S(1)} %shard_map.64.queries, bf16[208,1024]{1,0:T(8,128)(2,1)S(1)} %shard_map.66.near_bundle, bf16[80,1024]{1,0:T(8,128)(2,1)S(1)} %collective-permute-done.4.near_rest, ...), custom_call_target="tpu_custom_call" | custom-call | tf_op jit(solution)/shard_map/pallas_call | solution.py:251
  12.9 3.1 %collective-permute-start.7 = (bf16[8,3200]{1,0:T(8,128)(2,1)S(1)}, bf16[8,3200]{1,0:T(8,128)(2,1)S(1)}, u32[]{:S(2)}, u32[]{:S(2)}) collective-permute-start(bf16[8,3200]{1,0:T(8,128)(2,1)S(1)} %get-tuple-element.14), channel_id=1, source_target_pairs={{0,13},{1,12},{2,15},{3,14},{4,9},{5,8},{6,11},{7,10},{8,5},{9,4},... | collective-permute-start | bytes 153608 | tf_op jit(solution)/shard_map/ppermute | solution.py:173
  16.0 0.0 collective-permute-start.8
  16.0 0.8 %collective-permute-start.9 = (bf16[8,3200]{1,0:T(8,128)(2,1)S(1)}, bf16[8,3200]{1,0:T(8,128)(2,1)S(1)}, u32[]{:S(2)}, u32[]{:S(2)}) collective-permute-start(bf16[8,3200]{1,0:T(8,128)(2,1)S(1)} %get-tuple-element.16), channel_id=1, source_target_pairs={{0,9},{1,8},{2,11},{3,10},{4,13},{5,12},{6,15},{7,14},{8,1},{9,0},... | collective-permute-start | bytes 153608 | tf_op jit(solution)/shard_map/ppermute | solution.py:173
  16.8 2.1 %collective-permute-done.7.refs_1_ = bf16[8,3200]{1,0:T(8,128)(2,1)S(1)} collective-permute-done((bf16[8,3200]{1,0:T(8,128)(2,1)S(1)}, bf16[8,3200]{1,0:T(8,128)(2,1)S(1)}, u32[]{:S(2)}, u32[]{:S(2)}) %collective-permute-start.7) | collective-permute-done | bytes 51232 | tf_op jit(solution)/shard_map/ppermute | solution.py:173
  18.9 1.8 %collective-permute-done.8.refs_2_ = bf16[8,3200]{1,0:T(8,128)(2,1)S(1)} collective-permute-done((bf16[8,3200]{1,0:T(8,128)(2,1)S(1)}, bf16[8,3200]{1,0:T(8,128)(2,1)S(1)}, u32[]{:S(2)}, u32[]{:S(2)}) %collective-permute-start.8) | collective-permute-done | bytes 51232 | tf_op jit(solution)/shard_map/ppermute | solution.py:173
  20.8 0.0 collective-permute-done.9.refs_3_
  20.8 0.9 %shard_map.69 = bf16[8,3072]{1,0:T(8,128)(2,1)} custom-call(f32[8,3200]{1,0:T(8,128)S(1)} %get-tuple-element.13.refs_0_, bf16[8,3200]{1,0:T(8,128)(2,1)S(1)} %collective-permute-done.7.refs_1_, bf16[8,3200]{1,0:T(8,128)(2,1)S(1)} %collective-permute-done.8.refs_2_, bf16[8,3200]{1,0:T(8,128)(2,1)S(1)} %collective-permute-done.9.refs_3_), custom_call_target="tpu_custom_call" | custom-call | tf_op jit(solution)/shard_map/pallas_call | solution.py:264
  (2 shorter events, 0.0 us)
Async XLA Ops:
  0.0 7.8 %collective-permute-start.2 = (bf16[64,1024]{1,0:T(8,128)(2,1)}, bf16[64,1024]{1,0:T(8,128)(2,1)S(1)}, u32[]{:S(2)}, u32[]{:S(2)}) collective-permute-start(bf16[64,1024]{1,0:T(8,128)(2,1)} %refs_0_.3), channel_id=1, source_target_pairs={{0,2},{1,3},{2,0},{3,1},{4,6},{5,7},{6,4},{7,5},{8,10},{9,11},{10,... | collective-permute-start | bytes 393224 | tf_op jit(solution)/shard_map/ppermute | solution.py:173
  2.1 1.0 %copy-start.2 = (bf16[8,3072]{1,0:T(8,128)(2,1)S(1)}, bf16[8,3072]{1,0:T(8,128)(2,1)}, u32[]{:S(2)}) copy-start(bf16[8,3072]{1,0:T(8,128)(2,1)} %refs_0_.2) | copy-start | bytes 147460
  2.1 7.1 %copy-start = (bf16[64,1024]{1,0:T(8,128)(2,1)S(1)}, bf16[64,1024]{1,0:T(8,128)(2,1)}, u32[]{:S(2)}) copy-start(bf16[64,1024]{1,0:T(8,128)(2,1)} %refs_0_.3) | copy-start | bytes 393220
  3.0 5.9 %copy-start.1 = (s32[128]{0:T(128)S(1)}, s32[128]{0:T(128)}, u32[]{:S(2)}) copy-start(s32[128]{0:T(128)} %param.11) | copy-start | bytes 1540
  3.0 6.3 %collective-permute-start.4 = (bf16[80,1024]{1,0:T(8,128)(2,1)S(1)}, bf16[80,1024]{1,0:T(8,128)(2,1)S(1)}, u32[]{:S(2)}, u32[]{:S(2)}) collective-permute-start(bf16[80,1024]{1,0:T(8,128)(2,1)S(1)} %shard_map.65.refs_2_), channel_id=1, source_target_pairs={{0,2},{1,3},{2,0},{3,1},{4,6},{5,7},{6,4},{7,5},{8,10},{9,11},{10,... | collective-permute-start | bytes 491528 | tf_op jit(solution)/shard_map/ppermute | solution.py:173
  3.1 7.1 %collective-permute-start.1 = (bf16[8,3072]{1,0:T(8,128)(2,1)S(1)}, bf16[8,3072]{1,0:T(8,128)(2,1)S(1)}, u32[]{:S(2)}, u32[]{:S(2)}) collective-permute-start(bf16[8,3072]{1,0:T(8,128)(2,1)S(1)} %copy-done.2), channel_id=1, source_target_pairs={{0,13},{1,12},{2,15},{3,14},{4,9},{5,8},{6,11},{7,10},{8,5},{9,4},... | collective-permute-start | bytes 147464 | tf_op jit(solution)/shard_map/ppermute | solution.py:173
  7.8 4.4 %collective-permute-start = (bf16[8,3072]{1,0:T(8,128)(2,1)S(1)}, bf16[8,3072]{1,0:T(8,128)(2,1)S(1)}, u32[]{:S(2)}, u32[]{:S(2)}) collective-permute-start(bf16[8,3072]{1,0:T(8,128)(2,1)S(1)} %copy-done.2), channel_id=1, source_target_pairs={{0,9},{1,8},{2,11},{3,10},{4,13},{5,12},{6,15},{7,14},{8,1},{9,0},... | collective-permute-start | bytes 147464 | tf_op jit(solution)/shard_map/ppermute | solution.py:173
  7.8 4.4 %collective-permute-start.3 = (bf16[8,3072]{1,0:T(8,128)(2,1)S(1)}, bf16[8,3072]{1,0:T(8,128)(2,1)S(1)}, u32[]{:S(2)}, u32[]{:S(2)}) collective-permute-start(bf16[8,3072]{1,0:T(8,128)(2,1)S(1)} %copy-done.2), channel_id=1, source_target_pairs={{0,5},{1,4},{2,7},{3,6},{4,1},{5,0},{6,3},{7,2},{8,13},{9,12},{10,... | collective-permute-start | bytes 147464 | tf_op jit(solution)/shard_map/ppermute | solution.py:173
  9.2 3.0 %collective-permute-start.5 = (bf16[208,1024]{1,0:T(8,128)(2,1)S(1)}, bf16[208,1024]{1,0:T(8,128)(2,1)S(1)}, u32[]{:S(2)}, u32[]{:S(2)}) collective-permute-start(bf16[208,1024]{1,0:T(8,128)(2,1)S(1)} %shard_map.66.near_bundle), channel_id=1, source_target_pairs={{0,1},{1,0},{2,3},{3,2},{4,5},{5,4},{6,7},{7,6},{8,9},{9,8},{10,11... | collective-permute-start | bytes 1277960 | tf_op jit(solution)/shard_map/ppermute | solution.py:173
  9.3 2.9 %collective-permute-start.6 = (bf16[80,1024]{1,0:T(8,128)(2,1)S(1)}, bf16[80,1024]{1,0:T(8,128)(2,1)S(1)}, u32[]{:S(2)}, u32[]{:S(2)}) collective-permute-start(bf16[80,1024]{1,0:T(8,128)(2,1)S(1)} %collective-permute-done.4.near_rest), channel_id=1, source_target_pairs={{0,1},{1,0},{2,3},{3,2},{4,5},{5,4},{6,7},{7,6},{8,9},{9,8},{10,11... | collective-permute-start | bytes 491528 | tf_op jit(solution)/shard_map/ppermute | solution.py:173
  12.9 6.0 %collective-permute-start.7 = (bf16[8,3200]{1,0:T(8,128)(2,1)S(1)}, bf16[8,3200]{1,0:T(8,128)(2,1)S(1)}, u32[]{:S(2)}, u32[]{:S(2)}) collective-permute-start(bf16[8,3200]{1,0:T(8,128)(2,1)S(1)} %get-tuple-element.14), channel_id=1, source_target_pairs={{0,13},{1,12},{2,15},{3,14},{4,9},{5,8},{6,11},{7,10},{8,5},{9,4},... | collective-permute-start | bytes 153608 | tf_op jit(solution)/shard_map/ppermute | solution.py:173
  16.0 4.8 %collective-permute-start.8 = (bf16[8,3200]{1,0:T(8,128)(2,1)S(1)}, bf16[8,3200]{1,0:T(8,128)(2,1)S(1)}, u32[]{:S(2)}, u32[]{:S(2)}) collective-permute-start(bf16[8,3200]{1,0:T(8,128)(2,1)S(1)} %get-tuple-element.15), channel_id=1, source_target_pairs={{0,5},{1,4},{2,7},{3,6},{4,1},{5,0},{6,3},{7,2},{8,13},{9,12},{10,... | collective-permute-start | bytes 153608 | tf_op jit(solution)/shard_map/ppermute | solution.py:173
  16.0 4.8 %collective-permute-start.9 = (bf16[8,3200]{1,0:T(8,128)(2,1)S(1)}, bf16[8,3200]{1,0:T(8,128)(2,1)S(1)}, u32[]{:S(2)}, u32[]{:S(2)}) collective-permute-start(bf16[8,3200]{1,0:T(8,128)(2,1)S(1)} %get-tuple-element.16), channel_id=1, source_target_pairs={{0,9},{1,8},{2,11},{3,10},{4,13},{5,12},{6,15},{7,14},{8,1},{9,0},... | collective-permute-start | bytes 153608 | tf_op jit(solution)/shard_map/ppermute | solution.py:173

commit v9 on v8

--- a/solution.py
+++ b/solution.py
@@ -17,6 +17,7 @@
 STRIDE = 32
 CHUNKS = 4
 NT = (((1,), (1,)), ((), ()))
+LOG2_E = 1.4426950408889634
 SCHEDULE_LAST = pl.CostEstimate(flops=3 * 10**10, bytes_accessed=10**8, transcendentals=0)
 HEADS = [slice(head * HEAD_DIM, (head + 1) * HEAD_DIM) for head in range(QUERY_HEADS)]
 
@@ -116,13 +117,13 @@
         query = jnp.concatenate([queries[:, HEADS[head * GROUPS + g]] for g in range(GROUPS)], axis=0)
         keys = jnp.concatenate([part[:, HEADS[head]] for part in key_parts], axis=0)
         products = lax.dot_general(query, keys, NT, preferred_element_type=jnp.float32)
-        scores.append(products * HEAD_DIM ** (-0.5) + bias)
+        scores.append(products * (HEAD_DIM ** (-0.5) * LOG2_E) + bias)
     weights = []
     for head in range(KV_HEADS):
         maxima = jnp.max(scores[head], axis=1, keepdims=True)
-        exps = jnp.exp(scores[head] - maxima)
+        exps = jnp.exp2(scores[head] - maxima)
         masses = jnp.sum(exps, axis=1, keepdims=True)
-        weights.append((exps.astype(jnp.bfloat16), maxima + jnp.log(masses), 1.0 / masses))
+        weights.append((exps.astype(jnp.bfloat16), maxima + jnp.log2(masses), 1.0 / masses))
     lane = lax.broadcasted_iota(jnp.int32, (rows, LANES), 1)
     stats = jnp.zeros((rows, LANES), jnp.float32)
     for head, (rounded, level, inverse) in enumerate(weights):
@@ -151,7 +152,7 @@
         terms = part[:, WIDTH:].astype(jnp.float32)
         levels.append(terms + pltpu.roll(terms, LANES - STRIDE, 1) + pltpu.roll(terms, LANES - 2 * STRIDE, 1))
     top = functools.reduce(jnp.maximum, levels)
-    shares = [jnp.exp(level - top) for level in levels]
+    shares = [jnp.exp2(level - top) for level in levels]
     whole = 1.0 / functools.reduce(jnp.add, shares)
     shares = [share * whole for share in shares]
     for head in range(QUERY_HEADS):

time: 21.8 us -> 21.8 us (level)
  no operation moved by 1% of the time
where the time goes in v9:
time: 21.8 us; the launch traced here: 21.6 us
  starting transfers between devices  12.8 us (59%)
  waiting for transfers between devices  5.91 us (27%)
  Pallas kernels  2.84 us (13%)
    ppermute x10, starting transfers between devices, swap(): lax.ppermute(x, 'rows', [(i, i ^ offset) for i in range(lax.axis_size('ro...  12.8 us
    ppermute x10, waiting for transfers between devices, swap(): lax.ppermute(x, 'rows', [(i, i ^ offset) for i in range(lax.axis_size('ro...  5.91 us
    pallas_call x1, Pallas kernels, shards(): pl.pallas_call(rest_kernel, out_shape=pltpu.VMEM((slab + 2 * local_rows,...  0.93 us
    pallas_call x1, Pallas kernels, shards(): pl.pallas_call(merge_kernel, out_shape=jax.ShapeDtypeStruct((local_rows,...  0.93 us
    pallas_call x1, Pallas kernels, shards(): pl.pallas_call(functools.partial(attend_kernel, far, count, slab), out_sh...  0.65 us
  transfers between devices with their start and end apart: 10, of which 3 were waited for; matrix products, arithmetic and copies ran while one was open for 0% of the time, Pallas kernels for 6%

profile of v9, /device:TPU:1, one launch (start us, length us, event | category | flops | bytes accessed | tf_op | source)
XLA Modules:
  0.0 21.6 jit_solution(17099768795408253335)
XLA Ops:
  0.0 2.1 %collective-permute-start.2 = (bf16[64,1024]{1,0:T(8,128)(2,1)}, bf16[64,1024]{1,0:T(8,128)(2,1)S(1)}, u32[]{:S(2)}, u32[]{:S(2)}) collective-permute-start(bf16[64,1024]{1,0:T(8,128)(2,1)} %refs_0_.3), channel_id=1, source_target_pairs={{0,2},{1,3},{2,0},{3,1},{4,6},{5,7},{6,4},{7,5},{8,10},{9,11},{10,... | collective-permute-start | bytes 393224 | tf_op jit(solution)/shard_map/ppermute | solution.py:174
  2.1 0.0 copy-start.2
  2.1 0.0 copy-start
  2.1 0.9 %shard_map.65.refs_2_ = bf16[80,1024]{1,0:T(8,128)(2,1)S(1)} custom-call(bf16[64,1024]{1,0:T(8,128)(2,1)} %prefix_values.1, bf16[64,128]{1,0:T(8,128)(2,1)} %bitcast.12, bf16[64,128]{1,0:T(8,128)(2,1)} %bitcast.13), custom_call_target="tpu_custom_call" | custom-call | tf_op jit(solution)/shard_map/pallas_call | solution.py:198
  3.0 0.0 copy-start.1
  3.0 0.1 collective-permute-start.4
  3.1 0.0 copy-done.2
  3.1 4.6 %collective-permute-start.1 = (bf16[8,3072]{1,0:T(8,128)(2,1)S(1)}, bf16[8,3072]{1,0:T(8,128)(2,1)S(1)}, u32[]{:S(2)}, u32[]{:S(2)}) collective-permute-start(bf16[8,3072]{1,0:T(8,128)(2,1)S(1)} %copy-done.2), channel_id=1, source_target_pairs={{0,13},{1,12},{2,15},{3,14},{4,9},{5,8},{6,11},{7,10},{8,5},{9,4},... | collective-permute-start | bytes 147464 | tf_op jit(solution)/shard_map/ppermute | solution.py:174
  7.8 0.0 collective-permute-start
  7.8 0.0 collective-permute-done.2.refs_1_
  7.8 1.1 %collective-permute-start.3 = (bf16[8,3072]{1,0:T(8,128)(2,1)S(1)}, bf16[8,3072]{1,0:T(8,128)(2,1)S(1)}, u32[]{:S(2)}, u32[]{:S(2)}) collective-permute-start(bf16[8,3072]{1,0:T(8,128)(2,1)S(1)} %copy-done.2), channel_id=1, source_target_pairs={{0,5},{1,4},{2,7},{3,6},{4,1},{5,0},{6,3},{7,2},{8,13},{9,12},{10,... | collective-permute-start | bytes 147464 | tf_op jit(solution)/shard_map/ppermute | solution.py:174
  8.9 0.0 copy-done.1
  8.9 0.3 %shard_map.67.bias_ref = f32[32,320]{1,0:T(8,128)S(1)} custom-call(s32[1,128]{1,0:T(1,128)S(1)} %bitcast.11), custom_call_target="tpu_custom_call" | custom-call | tf_op jit(solution)/shard_map/pallas_call | solution.py:219
  9.2 0.0 copy-done
  9.2 0.1 collective-permute-start.5
  9.3 0.0 collective-permute-done.4.near_rest
  9.3 0.9 %collective-permute-start.6 = (bf16[80,1024]{1,0:T(8,128)(2,1)S(1)}, bf16[80,1024]{1,0:T(8,128)(2,1)S(1)}, u32[]{:S(2)}, u32[]{:S(2)}) collective-permute-start(bf16[80,1024]{1,0:T(8,128)(2,1)S(1)} %collective-permute-done.4.near_rest), channel_id=1, source_target_pairs={{0,1},{1,0},{2,3},{3,2},{4,5},{5,4},{6,7},{7,6},{8,9},{9,8},{10,11... | collective-permute-start | bytes 491528 | tf_op jit(solution)/shard_map/ppermute | solution.py:174
  10.2 0.0 collective-permute-done.1.refs_2_
  10.2 1.9 %collective-permute-done.refs_1_ = bf16[8,3072]{1,0:T(8,128)(2,1)S(1)} collective-permute-done((bf16[8,3072]{1,0:T(8,128)(2,1)S(1)}, bf16[8,3072]{1,0:T(8,128)(2,1)S(1)}, u32[]{:S(2)}, u32[]{:S(2)}) %collective-permute-start) | collective-permute-done | bytes 49184 | tf_op jit(solution)/shard_map/ppermute | solution.py:174
  12.2 0.0 collective-permute-done.3.refs_3_
  12.2 0.0 collective-permute-done.6.far_rest
  12.2 0.0 collective-permute-done.5.far_bundle
  12.2 0.7 %shard_map.68 = (f32[8,3200]{1,0:T(8,128)S(1)}, bf16[8,3200]{1,0:T(8,128)(2,1)S(1)}, bf16[8,3200]{1,0:T(8,128)(2,1)S(1)}, bf16[8,3200]{1,0:T(8,128)(2,1)S(1)}) custom-call(bf16[32,3072]{1,0:T(8,128)(2,1)S(1)} %shard_map.64.queries, bf16[208,1024]{1,0:T(8,128)(2,1)S(1)} %shard_map.66.near_bundle, bf16[80,1024]{1,0:T(8,128)(2,1)S(1)} %collective-permute-done.4.near_rest, ...), custom_call_target="tpu_custom_call" | custom-call | tf_op jit(solution)/shard_map/pallas_call | solution.py:252
  12.9 3.1 %collective-permute-start.7 = (bf16[8,3200]{1,0:T(8,128)(2,1)S(1)}, bf16[8,3200]{1,0:T(8,128)(2,1)S(1)}, u32[]{:S(2)}, u32[]{:S(2)}) collective-permute-start(bf16[8,3200]{1,0:T(8,128)(2,1)S(1)} %get-tuple-element.14), channel_id=1, source_target_pairs={{0,13},{1,12},{2,15},{3,14},{4,9},{5,8},{6,11},{7,10},{8,5},{9,4},... | collective-permute-start | bytes 153608 | tf_op jit(solution)/shard_map/ppermute | solution.py:174
  15.9 0.0 collective-permute-start.8
  15.9 0.8 %collective-permute-start.9 = (bf16[8,3200]{1,0:T(8,128)(2,1)S(1)}, bf16[8,3200]{1,0:T(8,128)(2,1)S(1)}, u32[]{:S(2)}, u32[]{:S(2)}) collective-permute-start(bf16[8,3200]{1,0:T(8,128)(2,1)S(1)} %get-tuple-element.16), channel_id=1, source_target_pairs={{0,9},{1,8},{2,11},{3,10},{4,13},{5,12},{6,15},{7,14},{8,1},{9,0},... | collective-permute-start | bytes 153608 | tf_op jit(solution)/shard_map/ppermute | solution.py:174
  16.7 2.1 %collective-permute-done.7.refs_1_ = bf16[8,3200]{1,0:T(8,128)(2,1)S(1)} collective-permute-done((bf16[8,3200]{1,0:T(8,128)(2,1)S(1)}, bf16[8,3200]{1,0:T(8,128)(2,1)S(1)}, u32[]{:S(2)}, u32[]{:S(2)}) %collective-permute-start.7) | collective-permute-done | bytes 51232 | tf_op jit(solution)/shard_map/ppermute | solution.py:174
  18.9 1.8 %collective-permute-done.8.refs_2_ = bf16[8,3200]{1,0:T(8,128)(2,1)S(1)} collective-permute-done((bf16[8,3200]{1,0:T(8,128)(2,1)S(1)}, bf16[8,3200]{1,0:T(8,128)(2,1)S(1)}, u32[]{:S(2)}, u32[]{:S(2)}) %collective-permute-start.8) | collective-permute-done | bytes 51232 | tf_op jit(solution)/shard_map/ppermute | solution.py:174
  20.7 0.0 collective-permute-done.9.refs_3_
  20.7 0.9 %shard_map.69 = bf16[8,3072]{1,0:T(8,128)(2,1)} custom-call(f32[8,3200]{1,0:T(8,128)S(1)} %get-tuple-element.13.refs_0_, bf16[8,3200]{1,0:T(8,128)(2,1)S(1)} %collective-permute-done.7.refs_1_, bf16[8,3200]{1,0:T(8,128)(2,1)S(1)} %collective-permute-done.8.refs_2_, bf16[8,3200]{1,0:T(8,128)(2,1)S(1)} %collective-permute-done.9.refs_3_), custom_call_target="tpu_custom_call" | custom-call | tf_op jit(solution)/shard_map/pallas_call | solution.py:265
  (2 shorter events, 0.0 us)
Async XLA Ops:
  0.0 7.8 %collective-permute-start.2 = (bf16[64,1024]{1,0:T(8,128)(2,1)}, bf16[64,1024]{1,0:T(8,128)(2,1)S(1)}, u32[]{:S(2)}, u32[]{:S(2)}) collective-permute-start(bf16[64,1024]{1,0:T(8,128)(2,1)} %refs_0_.3), channel_id=1, source_target_pairs={{0,2},{1,3},{2,0},{3,1},{4,6},{5,7},{6,4},{7,5},{8,10},{9,11},{10,... | collective-permute-start | bytes 393224 | tf_op jit(solution)/shard_map/ppermute | solution.py:174
  2.1 1.0 %copy-start.2 = (bf16[8,3072]{1,0:T(8,128)(2,1)S(1)}, bf16[8,3072]{1,0:T(8,128)(2,1)}, u32[]{:S(2)}) copy-start(bf16[8,3072]{1,0:T(8,128)(2,1)} %refs_0_.2) | copy-start | bytes 147460
  2.1 7.1 %copy-start = (bf16[64,1024]{1,0:T(8,128)(2,1)S(1)}, bf16[64,1024]{1,0:T(8,128)(2,1)}, u32[]{:S(2)}) copy-start(bf16[64,1024]{1,0:T(8,128)(2,1)} %refs_0_.3) | copy-start | bytes 393220
  3.0 5.9 %copy-start.1 = (s32[128]{0:T(128)S(1)}, s32[128]{0:T(128)}, u32[]{:S(2)}) copy-start(s32[128]{0:T(128)} %param.11) | copy-start | bytes 1540
  3.0 6.3 %collective-permute-start.4 = (bf16[80,1024]{1,0:T(8,128)(2,1)S(1)}, bf16[80,1024]{1,0:T(8,128)(2,1)S(1)}, u32[]{:S(2)}, u32[]{:S(2)}) collective-permute-start(bf16[80,1024]{1,0:T(8,128)(2,1)S(1)} %shard_map.65.refs_2_), channel_id=1, source_target_pairs={{0,2},{1,3},{2,0},{3,1},{4,6},{5,7},{6,4},{7,5},{8,10},{9,11},{10,... | collective-permute-start | bytes 491528 | tf_op jit(solution)/shard_map/ppermute | solution.py:174
  3.1 7.1 %collective-permute-start.1 = (bf16[8,3072]{1,0:T(8,128)(2,1)S(1)}, bf16[8,3072]{1,0:T(8,128)(2,1)S(1)}, u32[]{:S(2)}, u32[]{:S(2)}) collective-permute-start(bf16[8,3072]{1,0:T(8,128)(2,1)S(1)} %copy-done.2), channel_id=1, source_target_pairs={{0,13},{1,12},{2,15},{3,14},{4,9},{5,8},{6,11},{7,10},{8,5},{9,4},... | collective-permute-start | bytes 147464 | tf_op jit(solution)/shard_map/ppermute | solution.py:174
  7.8 4.4 %collective-permute-start = (bf16[8,3072]{1,0:T(8,128)(2,1)S(1)}, bf16[8,3072]{1,0:T(8,128)(2,1)S(1)}, u32[]{:S(2)}, u32[]{:S(2)}) collective-permute-start(bf16[8,3072]{1,0:T(8,128)(2,1)S(1)} %copy-done.2), channel_id=1, source_target_pairs={{0,9},{1,8},{2,11},{3,10},{4,13},{5,12},{6,15},{7,14},{8,1},{9,0},... | collective-permute-start | bytes 147464 | tf_op jit(solution)/shard_map/ppermute | solution.py:174
  7.8 4.4 %collective-permute-start.3 = (bf16[8,3072]{1,0:T(8,128)(2,1)S(1)}, bf16[8,3072]{1,0:T(8,128)(2,1)S(1)}, u32[]{:S(2)}, u32[]{:S(2)}) collective-permute-start(bf16[8,3072]{1,0:T(8,128)(2,1)S(1)} %copy-done.2), channel_id=1, source_target_pairs={{0,5},{1,4},{2,7},{3,6},{4,1},{5,0},{6,3},{7,2},{8,13},{9,12},{10,... | collective-permute-start | bytes 147464 | tf_op jit(solution)/shard_map/ppermute | solution.py:174
  9.2 3.0 %collective-permute-start.5 = (bf16[208,1024]{1,0:T(8,128)(2,1)S(1)}, bf16[208,1024]{1,0:T(8,128)(2,1)S(1)}, u32[]{:S(2)}, u32[]{:S(2)}) collective-permute-start(bf16[208,1024]{1,0:T(8,128)(2,1)S(1)} %shard_map.66.near_bundle), channel_id=1, source_target_pairs={{0,1},{1,0},{2,3},{3,2},{4,5},{5,4},{6,7},{7,6},{8,9},{9,8},{10,11... | collective-permute-start | bytes 1277960 | tf_op jit(solution)/shard_map/ppermute | solution.py:174
  9.3 2.9 %collective-permute-start.6 = (bf16[80,1024]{1,0:T(8,128)(2,1)S(1)}, bf16[80,1024]{1,0:T(8,128)(2,1)S(1)}, u32[]{:S(2)}, u32[]{:S(2)}) collective-permute-start(bf16[80,1024]{1,0:T(8,128)(2,1)S(1)} %collective-permute-done.4.near_rest), channel_id=1, source_target_pairs={{0,1},{1,0},{2,3},{3,2},{4,5},{5,4},{6,7},{7,6},{8,9},{9,8},{10,11... | collective-permute-start | bytes 491528 | tf_op jit(solution)/shard_map/ppermute | solution.py:174
  12.9 6.0 %collective-permute-start.7 = (bf16[8,3200]{1,0:T(8,128)(2,1)S(1)}, bf16[8,3200]{1,0:T(8,128)(2,1)S(1)}, u32[]{:S(2)}, u32[]{:S(2)}) collective-permute-start(bf16[8,3200]{1,0:T(8,128)(2,1)S(1)} %get-tuple-element.14), channel_id=1, source_target_pairs={{0,13},{1,12},{2,15},{3,14},{4,9},{5,8},{6,11},{7,10},{8,5},{9,4},... | collective-permute-start | bytes 153608 | tf_op jit(solution)/shard_map/ppermute | solution.py:174
  15.9 4.8 %collective-permute-start.8 = (bf16[8,3200]{1,0:T(8,128)(2,1)S(1)}, bf16[8,3200]{1,0:T(8,128)(2,1)S(1)}, u32[]{:S(2)}, u32[]{:S(2)}) collective-permute-start(bf16[8,3200]{1,0:T(8,128)(2,1)S(1)} %get-tuple-element.15), channel_id=1, source_target_pairs={{0,5},{1,4},{2,7},{3,6},{4,1},{5,0},{6,3},{7,2},{8,13},{9,12},{10,... | collective-permute-start | bytes 153608 | tf_op jit(solution)/shard_map/ppermute | solution.py:174
  15.9 4.8 %collective-permute-start.9 = (bf16[8,3200]{1,0:T(8,128)(2,1)S(1)}, bf16[8,3200]{1,0:T(8,128)(2,1)S(1)}, u32[]{:S(2)}, u32[]{:S(2)}) collective-permute-start(bf16[8,3200]{1,0:T(8,128)(2,1)S(1)} %get-tuple-element.16), channel_id=1, source_target_pairs={{0,9},{1,8},{2,11},{3,10},{4,13},{5,12},{6,15},{7,14},{8,1},{9,0},... | collective-permute-start | bytes 153608 | tf_op jit(solution)/shard_map/ppermute | solution.py:174

commit v10 on v9

--- a/solution.py
+++ b/solution.py
@@ -156,13 +156,10 @@
     whole = 1.0 / functools.reduce(jnp.add, shares)
     shares = [share * whole for share in shares]
     for head in range(QUERY_HEADS):
-        total = functools.reduce(
-            jnp.add,
-            [
-                share[:, head : head + 1] * part[:, HEADS[head]].astype(jnp.float32)
-                for share, part in zip(shares, parts)
-            ],
-        )
+        own = parts[0][:, HEADS[head]]
+        total = own
+        for share, part in zip(shares[1:], parts[1:]):
+            total = total + share[:, head : head + 1] * (part[:, HEADS[head]].astype(jnp.float32) - own)
         out[:, HEADS[head]] = total.astype(out.dtype)
 
 

time: 21.8 us -> 21.8 us (level)
  no operation moved by 1% of the time
where the time goes in v10:
time: 21.8 us; the launch traced here: 21.6 us
  starting transfers between devices  12.8 us (59%)
  waiting for transfers between devices  5.91 us (27%)
  Pallas kernels  2.81 us (13%)
    ppermute x10, starting transfers between devices, swap(): lax.ppermute(x, 'rows', [(i, i ^ offset) for i in range(lax.axis_size('ro...  12.8 us
    ppermute x10, waiting for transfers between devices, swap(): lax.ppermute(x, 'rows', [(i, i ^ offset) for i in range(lax.axis_size('ro...  5.91 us
    pallas_call x1, Pallas kernels, shards(): pl.pallas_call(rest_kernel, out_shape=pltpu.VMEM((slab + 2 * local_rows,...  0.93 us
    pallas_call x1, Pallas kernels, shards(): pl.pallas_call(merge_kernel, out_shape=jax.ShapeDtypeStruct((local_rows,...  0.9 us
    pallas_call x1, Pallas kernels, shards(): pl.pallas_call(functools.partial(attend_kernel, far, count, slab), out_sh...  0.65 us
  transfers between devices with their start and end apart: 10, of which 3 were waited for; matrix products, arithmetic and copies ran while one was open for 0% of the time, Pallas kernels for 6%

profile of v10, /device:TPU:1, one launch (start us, length us, event | category | flops | bytes accessed | tf_op | source)
XLA Modules:
  0.0 21.6 jit_solution(66039413757662570)
XLA Ops:
  0.0 2.1 %collective-permute-start.2 = (bf16[64,1024]{1,0:T(8,128)(2,1)}, bf16[64,1024]{1,0:T(8,128)(2,1)S(1)}, u32[]{:S(2)}, u32[]{:S(2)}) collective-permute-start(bf16[64,1024]{1,0:T(8,128)(2,1)} %refs_0_.3), channel_id=1, source_target_pairs={{0,2},{1,3},{2,0},{3,1},{4,6},{5,7},{6,4},{7,5},{8,10},{9,11},{10,... | collective-permute-start | bytes 393224 | tf_op jit(solution)/shard_map/ppermute | solution.py:171
  2.1 0.0 copy-start.2
  2.1 0.0 copy-start
  2.1 0.9 %shard_map.65.refs_2_ = bf16[80,1024]{1,0:T(8,128)(2,1)S(1)} custom-call(bf16[64,1024]{1,0:T(8,128)(2,1)} %prefix_values.1, bf16[64,128]{1,0:T(8,128)(2,1)} %bitcast.12, bf16[64,128]{1,0:T(8,128)(2,1)} %bitcast.13), custom_call_target="tpu_custom_call" | custom-call | tf_op jit(solution)/shard_map/pallas_call | solution.py:195
  3.0 0.0 copy-start.1
  3.0 0.1 collective-permute-start.4
  3.1 0.0 copy-done.2
  3.1 4.6 %collective-permute-start.1 = (bf16[8,3072]{1,0:T(8,128)(2,1)S(1)}, bf16[8,3072]{1,0:T(8,128)(2,1)S(1)}, u32[]{:S(2)}, u32[]{:S(2)}) collective-permute-start(bf16[8,3072]{1,0:T(8,128)(2,1)S(1)} %copy-done.2), channel_id=1, source_target_pairs={{0,13},{1,12},{2,15},{3,14},{4,9},{5,8},{6,11},{7,10},{8,5},{9,4},... | collective-permute-start | bytes 147464 | tf_op jit(solution)/shard_map/ppermute | solution.py:171
  7.8 0.0 collective-permute-start
  7.8 0.0 collective-permute-done.2.refs_1_
  7.8 1.1 %collective-permute-start.3 = (bf16[8,3072]{1,0:T(8,128)(2,1)S(1)}, bf16[8,3072]{1,0:T(8,128)(2,1)S(1)}, u32[]{:S(2)}, u32[]{:S(2)}) collective-permute-start(bf16[8,3072]{1,0:T(8,128)(2,1)S(1)} %copy-done.2), channel_id=1, source_target_pairs={{0,5},{1,4},{2,7},{3,6},{4,1},{5,0},{6,3},{7,2},{8,13},{9,12},{10,... | collective-permute-start | bytes 147464 | tf_op jit(solution)/shard_map/ppermute | solution.py:171
  8.9 0.0 copy-done.1
  8.9 0.3 %shard_map.67.bias_ref = f32[32,320]{1,0:T(8,128)S(1)} custom-call(s32[1,128]{1,0:T(1,128)S(1)} %bitcast.11), custom_call_target="tpu_custom_call" | custom-call | tf_op jit(solution)/shard_map/pallas_call | solution.py:216
  9.2 0.0 copy-done
  9.2 0.1 collective-permute-start.5
  9.3 0.0 collective-permute-done.4.near_rest
  9.3 0.9 %collective-permute-start.6 = (bf16[80,1024]{1,0:T(8,128)(2,1)S(1)}, bf16[80,1024]{1,0:T(8,128)(2,1)S(1)}, u32[]{:S(2)}, u32[]{:S(2)}) collective-permute-start(bf16[80,1024]{1,0:T(8,128)(2,1)S(1)} %collective-permute-done.4.near_rest), channel_id=1, source_target_pairs={{0,1},{1,0},{2,3},{3,2},{4,5},{5,4},{6,7},{7,6},{8,9},{9,8},{10,11... | collective-permute-start | bytes 491528 | tf_op jit(solution)/shard_map/ppermute | solution.py:171
  10.2 0.0 collective-permute-done.1.refs_2_
  10.2 1.9 %collective-permute-done.refs_1_ = bf16[8,3072]{1,0:T(8,128)(2,1)S(1)} collective-permute-done((bf16[8,3072]{1,0:T(8,128)(2,1)S(1)}, bf16[8,3072]{1,0:T(8,128)(2,1)S(1)}, u32[]{:S(2)}, u32[]{:S(2)}) %collective-permute-start) | collective-permute-done | bytes 49184 | tf_op jit(solution)/shard_map/ppermute | solution.py:171
  12.2 0.0 collective-permute-done.3.refs_3_
  12.2 0.0 collective-permute-done.6.far_rest
  12.2 0.0 collective-permute-done.5.far_bundle
  12.2 0.7 %shard_map.68 = (f32[8,3200]{1,0:T(8,128)S(1)}, bf16[8,3200]{1,0:T(8,128)(2,1)S(1)}, bf16[8,3200]{1,0:T(8,128)(2,1)S(1)}, bf16[8,3200]{1,0:T(8,128)(2,1)S(1)}) custom-call(bf16[32,3072]{1,0:T(8,128)(2,1)S(1)} %shard_map.64.queries, bf16[208,1024]{1,0:T(8,128)(2,1)S(1)} %shard_map.66.near_bundle, bf16[80,1024]{1,0:T(8,128)(2,1)S(1)} %collective-permute-done.4.near_rest, ...), custom_call_target="tpu_custom_call" | custom-call | tf_op jit(solution)/shard_map/pallas_call | solution.py:249
  12.9 3.1 %collective-permute-start.7 = (bf16[8,3200]{1,0:T(8,128)(2,1)S(1)}, bf16[8,3200]{1,0:T(8,128)(2,1)S(1)}, u32[]{:S(2)}, u32[]{:S(2)}) collective-permute-start(bf16[8,3200]{1,0:T(8,128)(2,1)S(1)} %get-tuple-element.14), channel_id=1, source_target_pairs={{0,13},{1,12},{2,15},{3,14},{4,9},{5,8},{6,11},{7,10},{8,5},{9,4},... | collective-permute-start | bytes 153608 | tf_op jit(solution)/shard_map/ppermute | solution.py:171
  15.9 0.0 collective-permute-start.8
  15.9 0.8 %collective-permute-start.9 = (bf16[8,3200]{1,0:T(8,128)(2,1)S(1)}, bf16[8,3200]{1,0:T(8,128)(2,1)S(1)}, u32[]{:S(2)}, u32[]{:S(2)}) collective-permute-start(bf16[8,3200]{1,0:T(8,128)(2,1)S(1)} %get-tuple-element.16), channel_id=1, source_target_pairs={{0,9},{1,8},{2,11},{3,10},{4,13},{5,12},{6,15},{7,14},{8,1},{9,0},... | collective-permute-start | bytes 153608 | tf_op jit(solution)/shard_map/ppermute | solution.py:171
  16.7 2.1 %collective-permute-done.7.refs_1_ = bf16[8,3200]{1,0:T(8,128)(2,1)S(1)} collective-permute-done((bf16[8,3200]{1,0:T(8,128)(2,1)S(1)}, bf16[8,3200]{1,0:T(8,128)(2,1)S(1)}, u32[]{:S(2)}, u32[]{:S(2)}) %collective-permute-start.7) | collective-permute-done | bytes 51232 | tf_op jit(solution)/shard_map/ppermute | solution.py:171
  18.9 1.8 %collective-permute-done.8.refs_2_ = bf16[8,3200]{1,0:T(8,128)(2,1)S(1)} collective-permute-done((bf16[8,3200]{1,0:T(8,128)(2,1)S(1)}, bf16[8,3200]{1,0:T(8,128)(2,1)S(1)}, u32[]{:S(2)}, u32[]{:S(2)}) %collective-permute-start.8) | collective-permute-done | bytes 51232 | tf_op jit(solution)/shard_map/ppermute | solution.py:171
  20.7 0.0 collective-permute-done.9.refs_3_
  20.7 0.9 %shard_map.69 = bf16[8,3072]{1,0:T(8,128)(2,1)} custom-call(f32[8,3200]{1,0:T(8,128)S(1)} %get-tuple-element.13.refs_0_, bf16[8,3200]{1,0:T(8,128)(2,1)S(1)} %collective-permute-done.7.refs_1_, bf16[8,3200]{1,0:T(8,128)(2,1)S(1)} %collective-permute-done.8.refs_2_, bf16[8,3200]{1,0:T(8,128)(2,1)S(1)} %collective-permute-done.9.refs_3_), custom_call_target="tpu_custom_call" | custom-call | tf_op jit(solution)/shard_map/pallas_call | solution.py:262
  (2 shorter events, 0.0 us)
Async XLA Ops:
  0.0 7.8 %collective-permute-start.2 = (bf16[64,1024]{1,0:T(8,128)(2,1)}, bf16[64,1024]{1,0:T(8,128)(2,1)S(1)}, u32[]{:S(2)}, u32[]{:S(2)}) collective-permute-start(bf16[64,1024]{1,0:T(8,128)(2,1)} %refs_0_.3), channel_id=1, source_target_pairs={{0,2},{1,3},{2,0},{3,1},{4,6},{5,7},{6,4},{7,5},{8,10},{9,11},{10,... | collective-permute-start | bytes 393224 | tf_op jit(solution)/shard_map/ppermute | solution.py:171
  2.1 1.0 %copy-start.2 = (bf16[8,3072]{1,0:T(8,128)(2,1)S(1)}, bf16[8,3072]{1,0:T(8,128)(2,1)}, u32[]{:S(2)}) copy-start(bf16[8,3072]{1,0:T(8,128)(2,1)} %refs_0_.2) | copy-start | bytes 147460
  2.1 7.1 %copy-start = (bf16[64,1024]{1,0:T(8,128)(2,1)S(1)}, bf16[64,1024]{1,0:T(8,128)(2,1)}, u32[]{:S(2)}) copy-start(bf16[64,1024]{1,0:T(8,128)(2,1)} %refs_0_.3) | copy-start | bytes 393220
  3.0 5.9 %copy-start.1 = (s32[128]{0:T(128)S(1)}, s32[128]{0:T(128)}, u32[]{:S(2)}) copy-start(s32[128]{0:T(128)} %param.11) | copy-start | bytes 1540
  3.0 6.3 %collective-permute-start.4 = (bf16[80,1024]{1,0:T(8,128)(2,1)S(1)}, bf16[80,1024]{1,0:T(8,128)(2,1)S(1)}, u32[]{:S(2)}, u32[]{:S(2)}) collective-permute-start(bf16[80,1024]{1,0:T(8,128)(2,1)S(1)} %shard_map.65.refs_2_), channel_id=1, source_target_pairs={{0,2},{1,3},{2,0},{3,1},{4,6},{5,7},{6,4},{7,5},{8,10},{9,11},{10,... | collective-permute-start | bytes 491528 | tf_op jit(solution)/shard_map/ppermute | solution.py:171
  3.1 7.1 %collective-permute-start.1 = (bf16[8,3072]{1,0:T(8,128)(2,1)S(1)}, bf16[8,3072]{1,0:T(8,128)(2,1)S(1)}, u32[]{:S(2)}, u32[]{:S(2)}) collective-permute-start(bf16[8,3072]{1,0:T(8,128)(2,1)S(1)} %copy-done.2), channel_id=1, source_target_pairs={{0,13},{1,12},{2,15},{3,14},{4,9},{5,8},{6,11},{7,10},{8,5},{9,4},... | collective-permute-start | bytes 147464 | tf_op jit(solution)/shard_map/ppermute | solution.py:171
  7.8 4.4 %collective-permute-start = (bf16[8,3072]{1,0:T(8,128)(2,1)S(1)}, bf16[8,3072]{1,0:T(8,128)(2,1)S(1)}, u32[]{:S(2)}, u32[]{:S(2)}) collective-permute-start(bf16[8,3072]{1,0:T(8,128)(2,1)S(1)} %copy-done.2), channel_id=1, source_target_pairs={{0,9},{1,8},{2,11},{3,10},{4,13},{5,12},{6,15},{7,14},{8,1},{9,0},... | collective-permute-start | bytes 147464 | tf_op jit(solution)/shard_map/ppermute | solution.py:171
  7.8 4.4 %collective-permute-start.3 = (bf16[8,3072]{1,0:T(8,128)(2,1)S(1)}, bf16[8,3072]{1,0:T(8,128)(2,1)S(1)}, u32[]{:S(2)}, u32[]{:S(2)}) collective-permute-start(bf16[8,3072]{1,0:T(8,128)(2,1)S(1)} %copy-done.2), channel_id=1, source_target_pairs={{0,5},{1,4},{2,7},{3,6},{4,1},{5,0},{6,3},{7,2},{8,13},{9,12},{10,... | collective-permute-start | bytes 147464 | tf_op jit(solution)/shard_map/ppermute | solution.py:171
  9.2 3.0 %collective-permute-start.5 = (bf16[208,1024]{1,0:T(8,128)(2,1)S(1)}, bf16[208,1024]{1,0:T(8,128)(2,1)S(1)}, u32[]{:S(2)}, u32[]{:S(2)}) collective-permute-start(bf16[208,1024]{1,0:T(8,128)(2,1)S(1)} %shard_map.66.near_bundle), channel_id=1, source_target_pairs={{0,1},{1,0},{2,3},{3,2},{4,5},{5,4},{6,7},{7,6},{8,9},{9,8},{10,11... | collective-permute-start | bytes 1277960 | tf_op jit(solution)/shard_map/ppermute | solution.py:171
  9.3 2.9 %collective-permute-start.6 = (bf16[80,1024]{1,0:T(8,128)(2,1)S(1)}, bf16[80,1024]{1,0:T(8,128)(2,1)S(1)}, u32[]{:S(2)}, u32[]{:S(2)}) collective-permute-start(bf16[80,1024]{1,0:T(8,128)(2,1)S(1)} %collective-permute-done.4.near_rest), channel_id=1, source_target_pairs={{0,1},{1,0},{2,3},{3,2},{4,5},{5,4},{6,7},{7,6},{8,9},{9,8},{10,11... | collective-permute-start | bytes 491528 | tf_op jit(solution)/shard_map/ppermute | solution.py:171
  12.9 6.0 %collective-permute-start.7 = (bf16[8,3200]{1,0:T(8,128)(2,1)S(1)}, bf16[8,3200]{1,0:T(8,128)(2,1)S(1)}, u32[]{:S(2)}, u32[]{:S(2)}) collective-permute-start(bf16[8,3200]{1,0:T(8,128)(2,1)S(1)} %get-tuple-element.14), channel_id=1, source_target_pairs={{0,13},{1,12},{2,15},{3,14},{4,9},{5,8},{6,11},{7,10},{8,5},{9,4},... | collective-permute-start | bytes 153608 | tf_op jit(solution)/shard_map/ppermute | solution.py:171
  15.9 4.8 %collective-permute-start.8 = (bf16[8,3200]{1,0:T(8,128)(2,1)S(1)}, bf16[8,3200]{1,0:T(8,128)(2,1)S(1)}, u32[]{:S(2)}, u32[]{:S(2)}) collective-permute-start(bf16[8,3200]{1,0:T(8,128)(2,1)S(1)} %get-tuple-element.15), channel_id=1, source_target_pairs={{0,5},{1,4},{2,7},{3,6},{4,1},{5,0},{6,3},{7,2},{8,13},{9,12},{10,... | collective-permute-start | bytes 153608 | tf_op jit(solution)/shard_map/ppermute | solution.py:171
  15.9 4.8 %collective-permute-start.9 = (bf16[8,3200]{1,0:T(8,128)(2,1)S(1)}, bf16[8,3200]{1,0:T(8,128)(2,1)S(1)}, u32[]{:S(2)}, u32[]{:S(2)}) collective-permute-start(bf16[8,3200]{1,0:T(8,128)(2,1)S(1)} %get-tuple-element.16), channel_id=1, source_target_pairs={{0,9},{1,8},{2,11},{3,10},{4,13},{5,12},{6,15},{7,14},{8,1},{9,0},... | collective-permute-start | bytes 153608 | tf_op jit(solution)/shard_map/ppermute | solution.py:171

commit v11 on v9

--- a/solution.py
+++ b/solution.py
@@ -216,6 +216,8 @@
             rest_pieces[offset ^ step] = swap(rest_pieces[offset], step)
     block_offsets = list(key_pieces)
     sibling_offsets = [offset ^ 1 for offset in block_offsets]
+    last_offset = list(rest_pieces)[-1]
+    parents, rest_pieces[last_offset] = after(parents, rest_pieces[last_offset])
     mask = pl.pallas_call(
         functools.partial(mask_kernel, owner_offsets, block_offsets + sibling_offsets, local_rows),
         out_shape=pltpu.VMEM((far * local_rows, near * (slab + 2 * local_rows)), jnp.float32),

time: 21.8 us -> 22 us (level)
  the two profiles are of different devices: /device:TPU:1 before, /device:TPU:0 now
where the time goes in v11:
time: 22 us; the launch traced here: 21.8 us
  starting transfers between devices  12.8 us (58%)
  waiting for transfers between devices  6.09 us (28%)
  Pallas kernels  2.83 us (13%)
    ppermute x10, starting transfers between devices, swap(): lax.ppermute(x, 'rows', [(i, i ^ offset) for i in range(lax.axis_size('ro...  12.8 us
    ppermute x10, waiting for transfers between devices, swap(): lax.ppermute(x, 'rows', [(i, i ^ offset) for i in range(lax.axis_size('ro...  6.09 us
    pallas_call x1, Pallas kernels, shards(): pl.pallas_call(rest_kernel, out_shape=pltpu.VMEM((slab + 2 * local_rows,...  0.93 us
    pallas_call x1, Pallas kernels, shards(): pl.pallas_call(merge_kernel, out_shape=jax.ShapeDtypeStruct((local_rows,...  0.93 us
    pallas_call x1, Pallas kernels, shards(): pl.pallas_call(functools.partial(attend_kernel, far, count, slab), out_sh...  0.65 us
  transfers between devices with their start and end apart: 10, of which 5 were waited for; matrix products, arithmetic and copies ran while one was open for 0% of the time, Pallas kernels for 6%

profile of v11, /device:TPU:0, one launch (start us, length us, event | category | flops | bytes accessed | tf_op | source)
XLA Modules:
  0.0 21.8 jit_solution(1583876813069635561)
XLA Ops:
  0.0 3.0 %collective-permute-start.2 = (bf16[64,1024]{1,0:T(8,128)(2,1)}, bf16[64,1024]{1,0:T(8,128)(2,1)S(1)}, u32[]{:S(2)}, u32[]{:S(2)}) collective-permute-start(bf16[64,1024]{1,0:T(8,128)(2,1)} %refs_0_.3), channel_id=1, source_target_pairs={{0,2},{1,3},{2,0},{3,1},{4,6},{5,7},{6,4},{7,5},{8,10},{9,11},{10,... | collective-permute-start | bytes 393224 | tf_op jit(solution)/shard_map/ppermute | solution.py:174
  3.0 0.0 copy-start.2
  3.0 0.0 copy-start
  3.0 0.9 %shard_map.65.refs_2_ = bf16[80,1024]{1,0:T(8,128)(2,1)S(1)} custom-call(bf16[64,1024]{1,0:T(8,128)(2,1)} %prefix_values.1, bf16[64,128]{1,0:T(8,128)(2,1)} %bitcast.12, bf16[64,128]{1,0:T(8,128)(2,1)} %bitcast.13), custom_call_target="tpu_custom_call" | custom-call | tf_op jit(solution)/shard_map/pallas_call | solution.py:198
  3.9 0.1 collective-permute-start.4
  4.0 0.0 copy-done.2
  4.0 3.0 %collective-permute-start.1 = (bf16[8,3072]{1,0:T(8,128)(2,1)S(1)}, bf16[8,3072]{1,0:T(8,128)(2,1)S(1)}, u32[]{:S(2)}, u32[]{:S(2)}) collective-permute-start(bf16[8,3072]{1,0:T(8,128)(2,1)S(1)} %copy-done.2), channel_id=1, source_target_pairs={{0,13},{1,12},{2,15},{3,14},{4,9},{5,8},{6,11},{7,10},{8,5},{9,4},... | collective-permute-start | bytes 147464 | tf_op jit(solution)/shard_map/ppermute | solution.py:174
  7.0 0.3 %collective-permute-start = (bf16[8,3072]{1,0:T(8,128)(2,1)S(1)}, bf16[8,3072]{1,0:T(8,128)(2,1)S(1)}, u32[]{:S(2)}, u32[]{:S(2)}) collective-permute-start(bf16[8,3072]{1,0:T(8,128)(2,1)S(1)} %copy-done.2), channel_id=1, source_target_pairs={{0,9},{1,8},{2,11},{3,10},{4,13},{5,12},{6,15},{7,14},{8,1},{9,0},... | collective-permute-start | bytes 147464 | tf_op jit(solution)/shard_map/ppermute | solution.py:174
  7.2 0.0 collective-permute-done.2.refs_1_
  7.2 1.1 %collective-permute-start.3 = (bf16[8,3072]{1,0:T(8,128)(2,1)S(1)}, bf16[8,3072]{1,0:T(8,128)(2,1)S(1)}, u32[]{:S(2)}, u32[]{:S(2)}) collective-permute-start(bf16[8,3072]{1,0:T(8,128)(2,1)S(1)} %copy-done.2), channel_id=1, source_target_pairs={{0,5},{1,4},{2,7},{3,6},{4,1},{5,0},{6,3},{7,2},{8,13},{9,12},{10,... | collective-permute-start | bytes 147464 | tf_op jit(solution)/shard_map/ppermute | solution.py:174
  8.4 0.0 copy-done
  8.4 0.0 copy-start.1
  8.4 1.1 %collective-permute-start.5 = (bf16[208,1024]{1,0:T(8,128)(2,1)S(1)}, bf16[208,1024]{1,0:T(8,128)(2,1)S(1)}, u32[]{:S(2)}, u32[]{:S(2)}) collective-permute-start(bf16[208,1024]{1,0:T(8,128)(2,1)S(1)} %shard_map.66.near_bundle), channel_id=1, source_target_pairs={{0,1},{1,0},{2,3},{3,2},{4,5},{5,4},{6,7},{7,6},{8,9},{9,8},{10,11... | collective-permute-start | bytes 1277960 | tf_op jit(solution)/shard_map/ppermute | solution.py:174
  9.5 0.7 %collective-permute-done.4.near_rest = bf16[80,1024]{1,0:T(8,128)(2,1)S(1)} collective-permute-done((bf16[80,1024]{1,0:T(8,128)(2,1)S(1)}, bf16[80,1024]{1,0:T(8,128)(2,1)S(1)}, u32[]{:S(2)}, u32[]{:S(2)}) %collective-permute-start.4) | collective-permute-done | bytes 163872 | tf_op jit(solution)/shard_map/ppermute | solution.py:174
  10.2 0.0 copy-done.1
  10.2 0.3 %shard_map.67.bias_ref = f32[32,320]{1,0:T(8,128)S(1)} custom-call(s32[1,128]{1,0:T(1,128)S(1)} %bitcast.11), custom_call_target="tpu_custom_call" | custom-call | tf_op jit(solution)/shard_map/pallas_call | solution.py:221
  10.5 0.1 collective-permute-start.6
  10.6 0.0 collective-permute-done.1.refs_2_
  10.6 1.6 %collective-permute-done.refs_1_ = bf16[8,3072]{1,0:T(8,128)(2,1)S(1)} collective-permute-done((bf16[8,3072]{1,0:T(8,128)(2,1)S(1)}, bf16[8,3072]{1,0:T(8,128)(2,1)S(1)}, u32[]{:S(2)}, u32[]{:S(2)}) %collective-permute-start) | collective-permute-done | bytes 49184 | tf_op jit(solution)/shard_map/ppermute | solution.py:174
  12.2 0.0 collective-permute-done.3.refs_3_
  12.2 0.0 collective-permute-done.6.far_rest
  12.2 0.0 collective-permute-done.5.far_bundle
  12.2 0.7 %shard_map.68 = (f32[8,3200]{1,0:T(8,128)S(1)}, bf16[8,3200]{1,0:T(8,128)(2,1)S(1)}, bf16[8,3200]{1,0:T(8,128)(2,1)S(1)}, bf16[8,3200]{1,0:T(8,128)(2,1)S(1)}) custom-call(bf16[32,3072]{1,0:T(8,128)(2,1)S(1)} %shard_map.64.queries, bf16[208,1024]{1,0:T(8,128)(2,1)S(1)} %shard_map.66.near_bundle, bf16[80,1024]{1,0:T(8,128)(2,1)S(1)} %collective-permute-done.4.near_rest, ...), custom_call_target="tpu_custom_call" | custom-call | tf_op jit(solution)/shard_map/pallas_call | solution.py:254
  12.9 3.3 %collective-permute-start.7 = (bf16[8,3200]{1,0:T(8,128)(2,1)S(1)}, bf16[8,3200]{1,0:T(8,128)(2,1)S(1)}, u32[]{:S(2)}, u32[]{:S(2)}) collective-permute-start(bf16[8,3200]{1,0:T(8,128)(2,1)S(1)} %get-tuple-element.18), channel_id=1, source_target_pairs={{0,13},{1,12},{2,15},{3,14},{4,9},{5,8},{6,11},{7,10},{8,5},{9,4},... | collective-permute-start | bytes 153608 | tf_op jit(solution)/shard_map/ppermute | solution.py:174
  16.2 0.0 collective-permute-start.8
  16.2 0.9 %collective-permute-start.9 = (bf16[8,3200]{1,0:T(8,128)(2,1)S(1)}, bf16[8,3200]{1,0:T(8,128)(2,1)S(1)}, u32[]{:S(2)}, u32[]{:S(2)}) collective-permute-start(bf16[8,3200]{1,0:T(8,128)(2,1)S(1)} %get-tuple-element.20), channel_id=1, source_target_pairs={{0,9},{1,8},{2,11},{3,10},{4,13},{5,12},{6,15},{7,14},{8,1},{9,0},... | collective-permute-start | bytes 153608 | tf_op jit(solution)/shard_map/ppermute | solution.py:174
  17.1 1.3 %collective-permute-done.7.refs_1_ = bf16[8,3200]{1,0:T(8,128)(2,1)S(1)} collective-permute-done((bf16[8,3200]{1,0:T(8,128)(2,1)S(1)}, bf16[8,3200]{1,0:T(8,128)(2,1)S(1)}, u32[]{:S(2)}, u32[]{:S(2)}) %collective-permute-start.7) | collective-permute-done | bytes 51232 | tf_op jit(solution)/shard_map/ppermute | solution.py:174
  18.4 1.6 %collective-permute-done.8.refs_2_ = bf16[8,3200]{1,0:T(8,128)(2,1)S(1)} collective-permute-done((bf16[8,3200]{1,0:T(8,128)(2,1)S(1)}, bf16[8,3200]{1,0:T(8,128)(2,1)S(1)}, u32[]{:S(2)}, u32[]{:S(2)}) %collective-permute-start.8) | collective-permute-done | bytes 51232 | tf_op jit(solution)/shard_map/ppermute | solution.py:174
  20.0 0.8 %collective-permute-done.9.refs_3_ = bf16[8,3200]{1,0:T(8,128)(2,1)S(1)} collective-permute-done((bf16[8,3200]{1,0:T(8,128)(2,1)S(1)}, bf16[8,3200]{1,0:T(8,128)(2,1)S(1)}, u32[]{:S(2)}, u32[]{:S(2)}) %collective-permute-start.9) | collective-permute-done | bytes 51232 | tf_op jit(solution)/shard_map/ppermute | solution.py:174
  20.9 0.9 %shard_map.69 = bf16[8,3072]{1,0:T(8,128)(2,1)} custom-call(f32[8,3200]{1,0:T(8,128)S(1)} %get-tuple-element.17.refs_0_, bf16[8,3200]{1,0:T(8,128)(2,1)S(1)} %collective-permute-done.7.refs_1_, bf16[8,3200]{1,0:T(8,128)(2,1)S(1)} %collective-permute-done.8.refs_2_, bf16[8,3200]{1,0:T(8,128)(2,1)S(1)} %collective-permute-done.9.refs_3_), custom_call_target="tpu_custom_call" | custom-call | tf_op jit(solution)/shard_map/pallas_call | solution.py:267
  (2 shorter events, 0.0 us)
Async XLA Ops:
  0.0 7.2 %collective-permute-start.2 = (bf16[64,1024]{1,0:T(8,128)(2,1)}, bf16[64,1024]{1,0:T(8,128)(2,1)S(1)}, u32[]{:S(2)}, u32[]{:S(2)}) collective-permute-start(bf16[64,1024]{1,0:T(8,128)(2,1)} %refs_0_.3), channel_id=1, source_target_pairs={{0,2},{1,3},{2,0},{3,1},{4,6},{5,7},{6,4},{7,5},{8,10},{9,11},{10,... | collective-permute-start | bytes 393224 | tf_op jit(solution)/shard_map/ppermute | solution.py:174
  3.0 1.0 %copy-start.2 = (bf16[8,3072]{1,0:T(8,128)(2,1)S(1)}, bf16[8,3072]{1,0:T(8,128)(2,1)}, u32[]{:S(2)}) copy-start(bf16[8,3072]{1,0:T(8,128)(2,1)} %refs_0_.2) | copy-start | bytes 147460
  3.0 5.4 %copy-start = (bf16[64,1024]{1,0:T(8,128)(2,1)S(1)}, bf16[64,1024]{1,0:T(8,128)(2,1)}, u32[]{:S(2)}) copy-start(bf16[64,1024]{1,0:T(8,128)(2,1)} %refs_0_.3) | copy-start | bytes 393220
  3.9 6.3 %collective-permute-start.4 = (bf16[80,1024]{1,0:T(8,128)(2,1)S(1)}, bf16[80,1024]{1,0:T(8,128)(2,1)S(1)}, u32[]{:S(2)}, u32[]{:S(2)}) collective-permute-start(bf16[80,1024]{1,0:T(8,128)(2,1)S(1)} %shard_map.65.refs_2_), channel_id=1, source_target_pairs={{0,2},{1,3},{2,0},{3,1},{4,6},{5,7},{6,4},{7,5},{8,10},{9,11},{10,... | collective-permute-start | bytes 491528 | tf_op jit(solution)/shard_map/ppermute | solution.py:174
  4.0 6.6 %collective-permute-start.1 = (bf16[8,3072]{1,0:T(8,128)(2,1)S(1)}, bf16[8,3072]{1,0:T(8,128)(2,1)S(1)}, u32[]{:S(2)}, u32[]{:S(2)}) collective-permute-start(bf16[8,3072]{1,0:T(8,128)(2,1)S(1)} %copy-done.2), channel_id=1, source_target_pairs={{0,13},{1,12},{2,15},{3,14},{4,9},{5,8},{6,11},{7,10},{8,5},{9,4},... | collective-permute-start | bytes 147464 | tf_op jit(solution)/shard_map/ppermute | solution.py:174
  7.0 5.2 %collective-permute-start = (bf16[8,3072]{1,0:T(8,128)(2,1)S(1)}, bf16[8,3072]{1,0:T(8,128)(2,1)S(1)}, u32[]{:S(2)}, u32[]{:S(2)}) collective-permute-start(bf16[8,3072]{1,0:T(8,128)(2,1)S(1)} %copy-done.2), channel_id=1, source_target_pairs={{0,9},{1,8},{2,11},{3,10},{4,13},{5,12},{6,15},{7,14},{8,1},{9,0},... | collective-permute-start | bytes 147464 | tf_op jit(solution)/shard_map/ppermute | solution.py:174
  7.2 4.9 %collective-permute-start.3 = (bf16[8,3072]{1,0:T(8,128)(2,1)S(1)}, bf16[8,3072]{1,0:T(8,128)(2,1)S(1)}, u32[]{:S(2)}, u32[]{:S(2)}) collective-permute-start(bf16[8,3072]{1,0:T(8,128)(2,1)S(1)} %copy-done.2), channel_id=1, source_target_pairs={{0,5},{1,4},{2,7},{3,6},{4,1},{5,0},{6,3},{7,2},{8,13},{9,12},{10,... | collective-permute-start | bytes 147464 | tf_op jit(solution)/shard_map/ppermute | solution.py:174
  8.4 1.8 %copy-start.1 = (s32[128]{0:T(128)S(1)}, s32[128]{0:T(128)}, u32[]{:S(2)}) copy-start(s32[128]{0:T(128)} %param.11) | copy-start | bytes 1540
  8.4 3.8 %collective-permute-start.5 = (bf16[208,1024]{1,0:T(8,128)(2,1)S(1)}, bf16[208,1024]{1,0:T(8,128)(2,1)S(1)}, u32[]{:S(2)}, u32[]{:S(2)}) collective-permute-start(bf16[208,1024]{1,0:T(8,128)(2,1)S(1)} %shard_map.66.near_bundle), channel_id=1, source_target_pairs={{0,1},{1,0},{2,3},{3,2},{4,5},{5,4},{6,7},{7,6},{8,9},{9,8},{10,11... | collective-permute-start | bytes 1277960 | tf_op jit(solution)/shard_map/ppermute | solution.py:174
  10.5 1.7 %collective-permute-start.6 = (bf16[80,1024]{1,0:T(8,128)(2,1)S(1)}, bf16[80,1024]{1,0:T(8,128)(2,1)S(1)}, u32[]{:S(2)}, u32[]{:S(2)}) collective-permute-start(bf16[80,1024]{1,0:T(8,128)(2,1)S(1)} %collective-permute-done.4.near_rest), channel_id=1, source_target_pairs={{0,1},{1,0},{2,3},{3,2},{4,5},{5,4},{6,7},{7,6},{8,9},{9,8},{10,11... | collective-permute-start | bytes 491528 | tf_op jit(solution)/shard_map/ppermute | solution.py:174
  12.9 5.5 %collective-permute-start.7 = (bf16[8,3200]{1,0:T(8,128)(2,1)S(1)}, bf16[8,3200]{1,0:T(8,128)(2,1)S(1)}, u32[]{:S(2)}, u32[]{:S(2)}) collective-permute-start(bf16[8,3200]{1,0:T(8,128)(2,1)S(1)} %get-tuple-element.18), channel_id=1, source_target_pairs={{0,13},{1,12},{2,15},{3,14},{4,9},{5,8},{6,11},{7,10},{8,5},{9,4},... | collective-permute-start | bytes 153608 | tf_op jit(solution)/shard_map/ppermute | solution.py:174
  16.2 3.8 %collective-permute-start.8 = (bf16[8,3200]{1,0:T(8,128)(2,1)S(1)}, bf16[8,3200]{1,0:T(8,128)(2,1)S(1)}, u32[]{:S(2)}, u32[]{:S(2)}) collective-permute-start(bf16[8,3200]{1,0:T(8,128)(2,1)S(1)} %get-tuple-element.19), channel_id=1, source_target_pairs={{0,5},{1,4},{2,7},{3,6},{4,1},{5,0},{6,3},{7,2},{8,13},{9,12},{10,... | collective-permute-start | bytes 153608 | tf_op jit(solution)/shard_map/ppermute | solution.py:174
  16.2 4.6 %collective-permute-start.9 = (bf16[8,3200]{1,0:T(8,128)(2,1)S(1)}, bf16[8,3200]{1,0:T(8,128)(2,1)S(1)}, u32[]{:S(2)}, u32[]{:S(2)}) collective-permute-start(bf16[8,3200]{1,0:T(8,128)(2,1)S(1)} %get-tuple-element.20), channel_id=1, source_target_pairs={{0,9},{1,8},{2,11},{3,10},{4,13},{5,12},{6,15},{7,14},{8,1},{9,0},... | collective-permute-start | bytes 153608 | tf_op jit(solution)/shard_map/ppermute | solution.py:174
